TPU v7x, 256 devices: a whole 4x4x8 slice. The times are simulated.
256 devices in a mesh: slab: 32 (over y, z_hi, x), pencil: 8 (over z_lo, core).
Axes of the slice: x: 4, y: 4, z: 8 (z_hi: 2, z_lo: 4; z = z_hi * 4 + z_lo), core: 2. Of those that a mesh axis runs over, the one named last changes fastest.
Arguments:
- layer_input: float32 [2, 32, 128, 128, 128], P(None, None, 'slab', 'pencil'), may hold values from -6 to 6
- pre_act: float32 [2, 32, 128, 128, 128], P(None, None, 'slab', 'pencil'), may hold values from -6 to 6
- out_grad: float32 [2, 32, 128, 128, 128], P(None, None, 'slab', 'pencil'), may hold values from -18 to 18
- weight_codes: int32 [32, 32, 32, 2048], P('slab', 'pencil'), may hold values from -127 to 127
- scale_codes: int32 [32, 32, 32, 64], P('slab', 'pencil'), may hold values from 0 to 7
- weight_noise: float32 [32, 32, 32, 2048], P('slab', 'pencil'), may hold values from -1.5 to 1.5
- point_weight: float32 [32, 32], replicated, may hold values from -1 to 1
Outputs:
- grad_input: float32 [2, 32, 128, 128, 128], P(None, None, 'slab', 'pencil')
- grad_spectral: float32 [32, 32, 32, 2048], P('slab', 'pencil')
- grad_point: float32 [32, 32], replicated
- grad_bias: float32 [32], replicated
All inputs are finite; a program needn't handle non-finite values.
Results may differ from a plain program's by a relative error of at most 0.00011.
Values sent between devices are 32-bit elements; how exact they have to be, the bound alone decides.
No kernel may reach another device: no remote copies, remote signals or barrier semaphores. Data moves between devices by JAX's collectives and lax.ppermute only.
A program may use at most 128 MiB of HBM per device.

v0:
```python
import math

import jax
import jax.numpy as jnp
from jax import lax
from jax.sharding import PartitionSpec as P

HIGHEST = lax.Precision.HIGHEST


def gelu_slope(values):
    cdf_part = 0.5 * (1.0 + lax.erf(values * (1.0 / math.sqrt(2.0))))
    return cdf_part + values * jnp.exp(-0.5 * values * values) * (1.0 / math.sqrt(2.0 * math.pi))


def wave_parts(positions, frequencies, period):
    turn_count = positions[:, None] * (frequencies[None, :] % period) % period
    angles = turn_count.astype(jnp.float32) * (2.0 * math.pi / period)
    return (jnp.cos(angles), jnp.sin(angles))


def contract_out(weights, values):
    return jnp.einsum("zxyio,zxybo->zxybi", weights, values, precision=HIGHEST)


def outer_sum(left_side, right_side):
    return jnp.einsum("zxybi,zxybo->zxyio", left_side, right_side, precision=HIGHEST)


def per_device(
    layer_input, pre_act, out_grad, weight_codes, scale_codes, weight_noise, point_weight
):
    batch_size, channels, x_cells, y_cells, z_cells = layer_input.shape
    slab_count = lax.axis_size("slab")
    pencil_count = lax.axis_size("pencil")
    x_total = x_cells * slab_count
    y_total = y_cells * pencil_count
    kz_local = weight_codes.shape[0]
    kx_local = weight_codes.shape[1]
    ky_count = weight_codes.shape[2]
    kz_count = kz_local * slab_count
    kx_count = kx_local * pencil_count
    grad_out = out_grad * gelu_slope(pre_act)
    local_weight = jnp.einsum("bixyz,boxyz->io", layer_input, grad_out, precision=HIGHEST)
    local_bias = jnp.sum(grad_out, axis=(0, 2, 3, 4))
    total_weight, total_bias = lax.psum((local_weight, local_bias), ("slab", "pencil"))
    cell_count = float(batch_size * x_total * y_total * z_cells)
    grad_point = total_weight / cell_count
    grad_bias = total_bias / cell_count
    unit_scale = 1.0 / math.sqrt(x_total * y_total * z_cells)
    kz_kept = jnp.arange(kz_count)
    kx_kept = jnp.arange(kx_count) - kx_count // 2
    ky_kept = jnp.arange(ky_count) - ky_count // 2
    z_width = z_cells // 2 // slab_count
    z_rows = jnp.arange(slab_count * z_width)
    z_owner = z_rows // z_width
    z_slot = z_rows % z_width
    z_freqs = jnp.where(
        z_slot < kz_local,
        z_owner * kz_local + z_slot,
        kz_count + z_owner * (z_width - kz_local) + z_slot - kz_local,
    )
    x_width = x_total // pencil_count
    x_rows = jnp.arange(pencil_count * x_width)
    x_owner = x_rows // x_width
    x_slot = x_rows % x_width
    x_freqs = jnp.where(
        x_slot < kx_local,
        x_owner * kx_local + x_slot - kx_count // 2,
        kx_count // 2 + x_owner * (x_width - kx_local) + x_slot - kx_local,
    )
    z_cos, z_sin = wave_parts(jnp.arange(z_cells), z_freqs, z_cells)
    z_table = jnp.stack([z_cos, -z_sin], axis=2)
    freq_rows = z_freqs.shape[0]

    def along_z(field_data):
        moved_axes = jnp.einsum("bcxyn,nfr->fxrbcy", field_data, z_table, precision=HIGHEST)
        return moved_axes.reshape(freq_rows, x_cells, -1)

    z_spectra = (along_z(layer_input), along_z(grad_out))
    arrived = (
        lax.all_to_all(z_spectra[0], "slab", split_axis=0, concat_axis=1, tiled=True),
        lax.all_to_all(z_spectra[1], "slab", split_axis=0, concat_axis=1, tiled=True),
    )
    arrived = (arrived[0][:kz_local], arrived[1][:kz_local])
    x_cos, x_sin = wave_parts(jnp.arange(x_total), x_freqs, x_total)
    x_cos = x_cos.T
    x_sin = x_sin.T
    x_table = jnp.stack([jnp.stack([x_cos, x_sin], -1), jnp.stack([-x_sin, x_cos], -1)], 1)

    def along_x(incoming):
        return jnp.einsum(
            "knsm,qrns->kqrm",
            incoming.reshape(kz_local, x_total, 2, -1),
            x_table,
            precision=HIGHEST,
        )

    x_spectra = (along_x(arrived[0]), along_x(arrived[1]))
    gathered = (
        lax.all_to_all(x_spectra[0], "pencil", split_axis=1, concat_axis=0, tiled=True),
        lax.all_to_all(x_spectra[1], "pencil", split_axis=1, concat_axis=0, tiled=True),
    )
    gathered = (gathered[0][:, :kx_local], gathered[1][:, :kx_local])
    y_cos, y_sin = wave_parts(jnp.arange(y_total), ky_kept, y_total)
    y_cos = y_cos.reshape(pencil_count, y_cells, ky_count)
    y_sin = y_sin.reshape(pencil_count, y_cells, ky_count)
    y_table = jnp.stack([jnp.stack([y_cos, -y_sin], -1), jnp.stack([y_sin, y_cos], -1)], 2)

    def along_y(incoming):
        shaped = incoming.reshape(
            pencil_count, kz_local, kx_local, 2, batch_size, channels, y_cells
        )
        return jnp.einsum("pkjsbcy,pysqr->kjqbrc", shaped, y_table, precision=HIGHEST) * unit_scale

    u_hat = along_y(gathered[0])
    g_hat = along_y(gathered[1])
    code_values = weight_codes.astype(jnp.float32).reshape(
        kz_local, kx_local, ky_count, 2, channels, channels
    )
    step_size = jnp.exp2(-scale_codes.astype(jnp.float32) / 4.0).reshape(
        kz_local, kx_local, ky_count, 2, channels, 1
    ) / (16.0 * math.sqrt(channels))
    effective = (
        code_values
        * step_size
        * (1.0 + weight_noise.reshape(kz_local, kx_local, ky_count, 2, channels, channels))
    )
    weight_real = effective[:, :, :, 0]
    weight_imag = effective[:, :, :, 1]
    u_real = u_hat[..., 0, :]
    u_imag = u_hat[..., 1, :]
    g_real = g_hat[..., 0, :]
    g_imag = g_hat[..., 1, :]
    q_real = contract_out(weight_real, g_real) + contract_out(weight_imag, g_imag)
    q_imag = contract_out(weight_real, g_imag) - contract_out(weight_imag, g_real)
    grad_real = outer_sum(u_real, g_real) + outer_sum(u_imag, g_imag)
    grad_imag = outer_sum(u_real, g_imag) - outer_sum(u_imag, g_real)
    grad_spectral = jnp.stack([grad_real, grad_imag], axis=3).reshape(
        kz_local, kx_local, ky_count, -1
    )
    q_hat = jnp.stack([q_real, q_imag], axis=4)
    y_back_cos = jnp.transpose(y_cos, (2, 0, 1))
    y_back_sin = jnp.transpose(y_sin, (2, 0, 1))
    y_back_table = jnp.stack(
        [jnp.stack([y_back_cos, y_back_sin], -1), jnp.stack([-y_back_sin, y_back_cos], -1)], 1
    )
    spread_y = jnp.einsum("kjqbsc,qspyr->pkjrbcy", q_hat, y_back_table, precision=HIGHEST)
    spread_y = spread_y.reshape(pencil_count, kz_local, kx_local, 2, -1)
    from_pencil = lax.all_to_all(spread_y, "pencil", split_axis=0, concat_axis=2, tiled=True)
    x_back_cos, x_back_sin = wave_parts(jnp.arange(x_total), kx_kept, x_total)
    x_back_cos = x_back_cos.T.reshape(kx_count, slab_count, x_cells)
    x_back_sin = x_back_sin.T.reshape(kx_count, slab_count, x_cells)
    x_back_table = jnp.stack(
        [jnp.stack([x_back_cos, x_back_sin], -1), jnp.stack([-x_back_sin, x_back_cos], -1)], 1
    )
    spread_x = jnp.einsum(
        "kqsm,qsdxr->dxkrm",
        from_pencil.reshape(kz_local, kx_count, 2, -1),
        x_back_table,
        precision=HIGHEST,
    )
    spread_x = spread_x.reshape(slab_count, x_cells, kz_local, -1)
    from_slab = lax.all_to_all(spread_x, "slab", split_axis=0, concat_axis=2, tiled=True)
    z_back_cos, z_back_sin = wave_parts(jnp.arange(z_cells), kz_kept, z_cells)
    z_back_table = jnp.stack([z_back_cos.T, -z_back_sin.T], 1)
    shaped_back = from_slab.reshape(x_cells, kz_count, 2, batch_size, channels, y_cells)
    spatial = (
        jnp.einsum("xkrbcy,krn->bcxyn", shaped_back, z_back_table, precision=HIGHEST) * unit_scale
    )
    grad_input = jnp.einsum("bcxyz,ic->bixyz", grad_out, point_weight, precision=HIGHEST) + spatial
    return (grad_input, grad_spectral, grad_point, grad_bias)


def solution(mesh):
    in_specs = (
        P(None, None, "slab", "pencil", None),
        P(None, None, "slab", "pencil", None),
        P(None, None, "slab", "pencil", None),
        P("slab", "pencil", None, None),
        P("slab", "pencil", None, None),
        P("slab", "pencil", None, None),
        P(),
    )
    out_specs = (P(None, None, "slab", "pencil", None), P("slab", "pencil", None, None), P(), P())
    return jax.shard_map(
        per_device, mesh=mesh, in_specs=in_specs, out_specs=out_specs, check_vma=False
    )
```

profile of v0, /device:TPU:1, one launch (start us, length us, event | category | flops | bytes accessed | tf_op | source)
XLA Modules:
  0.0 383.2 jit_solution(1469237205785515487)
XLA Ops:
  0.9 5.6 %convolution_bitcast_fusion = f32[64,4,2,2,32,16]{0,4,5,1,3,2:T(8,128)S(1)} fusion(f32[2,32,4,16,128]{4,3,2,1,0:T(8,128)} %param.7, f32[128,64,1]{0,1,2:T(8,128)S(1)} %get-tuple-element.51, f32[128,64,1]{0,1,2:T(8,128)S(1)} %get-tuple-element.50), kind=kOutput, calls=%fused_computation.6 | convolution fusion | flops 805322752 | bytes 4259840 | tf_op jit(solution)/shard_map/bcxyn,nfr->fxrbcy/dot_general | solution.py:77
  6.5 5.2 %copy.150 = f32[64,4,2,2,32,16]{0,5,4,3,2,1:T(8,128)} copy(f32[64,4,2,2,32,16]{0,4,5,1,3,2:T(8,128)S(1)} %convolution_bitcast_fusion) | data formatting | bytes 4194304 | tf_op jit(solution)/shard_map/bcxyn,nfr->fxrbcy/transpose | solution.py:77
  11.7 4.9 %copy.151 = f32[64,4,2048]{2,1,0:T(4,128)} copy(f32[64,4,2048]{0,2,1:T(8,128)} %bitcast.207) | data formatting | bytes 4194304 | tf_op jit(solution)/shard_map/reshape | solution.py:78
  16.6 14.8 %all-to-all-start.4 = ((f32[64,4,2048]{2,1,0:T(4,128)}), f32[64,4,2048]{2,1,0:T(4,128)}, u32[]{:S(2)}, u32[]{:S(2)}) async-start(f32[64,4,2048]{2,1,0:T(4,128)} %copy.151), calls=%async_computation.4 | async-start | bytes 4194304 | tf_op jit(solution)/shard_map/all_to_all | solution.py:82
  31.4 3.4 fusion.134
  34.8 4.0 %convolution_bitcast_fusion.1 = f32[64,4,2,2,32,16]{0,4,5,1,3,2:T(8,128)S(1)} fusion(f32[2,32,4,16,128]{4,3,2,1,0:T(8,128)S(1)} %get-tuple-element.23, f32[128,64,1]{0,1,2:T(8,128)S(1)} %get-tuple-element.51, f32[128,64,1]{0,1,2:T(8,128)S(1)} %get-tuple-element.50), kind=kOutput, calls=%fused_computation.7 | convolution fusion | flops 805322752 | bytes 4259840 | tf_op jit(solution)/shard_map/bcxyn,nfr->fxrbcy/dot_general | solution.py:77
  38.8 5.2 %copy.127 = f32[64,4,2,2,32,16]{0,5,4,3,2,1:T(8,128)} copy(f32[64,4,2,2,32,16]{0,4,5,1,3,2:T(8,128)S(1)} %convolution_bitcast_fusion.1) | data formatting | bytes 4194304 | tf_op jit(solution)/shard_map/bcxyn,nfr->fxrbcy/transpose | solution.py:77
  44.0 5.0 %copy.128 = f32[64,4,2048]{2,1,0:T(4,128)} copy(f32[64,4,2048]{0,2,1:T(8,128)} %bitcast.208) | data formatting | bytes 4194304 | tf_op jit(solution)/shard_map/reshape | solution.py:78
  49.1 19.5 %all-to-all-done.4 = f32[64,4,2048]{2,1,0:T(4,128)} async-done(((f32[64,4,2048]{2,1,0:T(4,128)}), f32[64,4,2048]{2,1,0:T(4,128)}, u32[]{:S(2)}, u32[]{:S(2)}) %all-to-all-start.4) | async-done | bytes 2097184 | tf_op jit(solution)/shard_map/all_to_all | solution.py:82
  68.6 5.0 %all-to-all-start = ((f32[64,4,2048]{2,1,0:T(4,128)}), f32[64,4,2048]{2,1,0:T(4,128)}, u32[]{:S(2)}, u32[]{:S(2)}) async-start(f32[64,4,2048]{2,1,0:T(4,128)} %copy.128), calls=%async_computation | async-start | bytes 4194304 | tf_op jit(solution)/shard_map/all_to_all | solution.py:83
  74.0 2.3 slice.48
  76.3 2.3 reshape.888
  78.6 1.3 convolution_bitcast_fusion.4
  79.9 1.8 copy.153
  81.7 14.6 %all-to-all-done = f32[64,4,2048]{2,1,0:T(4,128)} async-done(((f32[64,4,2048]{2,1,0:T(4,128)}), f32[64,4,2048]{2,1,0:T(4,128)}, u32[]{:S(2)}, u32[]{:S(2)}) %all-to-all-start) | async-done | bytes 2097184 | tf_op jit(solution)/shard_map/all_to_all | solution.py:83
  96.3 39.7 %all-to-all-start.5 = ((f32[1,128,2,1024]{3,2,0,1:T(2,128)}), f32[1,128,2,1024]{3,2,0,1:T(2,128)}, u32[]{:S(2)}, u32[]{:S(2)}) async-start(f32[1,128,2,1024]{3,2,0,1:T(2,128)} %copy.153), calls=%async_computation.5 | async-start | bytes 2097152 | tf_op jit(solution)/shard_map/all_to_all | solution.py:101
  136.0 2.3 slice.42
  138.3 2.3 reshape.876
  140.6 1.3 convolution_bitcast_fusion.5
  141.9 1.8 copy.130
  143.8 18.1 %all-to-all-done.5 = f32[1,128,2,1024]{3,2,0,1:T(2,128)} async-done(((f32[1,128,2,1024]{3,2,0,1:T(2,128)}), f32[1,128,2,1024]{3,2,0,1:T(2,128)}, u32[]{:S(2)}, u32[]{:S(2)}) %all-to-all-start.5) | async-done | bytes 1048608 | tf_op jit(solution)/shard_map/all_to_all | solution.py:101
  161.9 5.0 %all-to-all-start.1 = ((f32[1,128,2,1024]{3,2,0,1:T(2,128)}), f32[1,128,2,1024]{3,2,0,1:T(2,128)}, u32[]{:S(2)}, u32[]{:S(2)}) async-start(f32[1,128,2,1024]{3,2,0,1:T(2,128)} %copy.130), calls=%async_computation.1 | async-start | bytes 2097152 | tf_op jit(solution)/shard_map/all_to_all | solution.py:102
  166.8 1.3 broadcast_add_fusion
  168.2 2.8 add.430
  171.0 1.3 convert_element_type.147
  172.3 2.8 reshape.879
  175.6 0.7 maximum_bitcast_fusion.8
  176.7 5.9 %copy_multiply_fusion = f32[1,4,32,2,32,32]{5,4,2,1,3,0:T(8,128)} fusion(f32[1,4,32,2,32,32]{5,4,3,2,1,0:T(8,128)} %add.430, f32[1,4,32,2,32,32]{5,4,3,2,1,0:T(8,128)} %reshape.879, f32[4,32,2,32]{3,1,0,2:T(8,128)S(1)} %copy.133), kind=kLoop, calls=%fused_computation.3 | loop fusion | flops 524288 | bytes 3178496 | tf_op jit(solution)/shard_map/mul | solution.py:125
  182.6 1.0 slice.49
  183.8 2.0 reshape.889
  185.8 6.9 %all-to-all-done.1 = f32[1,128,2,1024]{3,2,0,1:T(2,128)} async-done(((f32[1,128,2,1024]{3,2,0,1:T(2,128)}), f32[1,128,2,1024]{3,2,0,1:T(2,128)}, u32[]{:S(2)}, u32[]{:S(2)}) %all-to-all-start.1) | async-done | bytes 1048608 | tf_op jit(solution)/shard_map/all_to_all | solution.py:102
  192.7 1.0 slice.43
  193.8 2.1 reshape.877
  195.9 7.4 %fusion.41 = f32[1,4,32,2,2,32]{5,2,3,1,4,0:T(8,128)S(1)} fusion(f32[8,16,1,32,2]{3,1,2,0,4:T(8,128)S(1)} %get-tuple-element.29, f32[8,16,1,32,2]{3,1,2,0,4:T(8,128)S(1)} %get-tuple-element.28, f32[8,4,2,2,32,16]{5,4,3,0,2,1:T(8,128)} %reshape.889), kind=kOutput, calls=%fused_computation.45 | convolution fusion | flops 50364416 | bytes 393216 | tf_op jit(solution)/shard_map/pkjsbcy,pysqr->kjqbrc/dot_general | solution.py:114
  203.3 5.7 %fusion.32 = f32[1,4,32,2,2,32]{5,2,3,1,4,0:T(8,128)S(1)} fusion(f32[8,16,1,32,2]{3,1,2,0,4:T(8,128)S(1)} %get-tuple-element.29, f32[8,16,1,32,2]{3,1,2,0,4:T(8,128)S(1)} %get-tuple-element.28, f32[8,4,2,2,32,16]{5,4,3,0,2,1:T(8,128)S(1)} %copy-done.2), kind=kOutput, calls=%fused_computation.42 | convolution fusion | flops 50364416 | bytes 393216 | tf_op jit(solution)/shard_map/pkjsbcy,pysqr->kjqbrc/dot_general | solution.py:114
  209.7 3.4 fusion.13
  213.0 3.5 fusion.14
  216.6 3.4 fusion.47
  220.0 3.4 fusion.45
  223.5 1.0 convolution_bitcast_fusion.3
  224.5 2.0 copy.191
  226.5 3.3 reshape.914
  229.8 4.4 %all-to-all-start.2 = ((f32[8,1,4,2,1024]{4,3,2,1,0:T(2,128)}), f32[8,1,4,2,1024]{4,3,2,1,0:T(2,128)S(1)}, u32[]{:S(2)}, u32[]{:S(2)}) async-start(f32[8,1,4,2,1024]{4,3,2,1,0:T(2,128)} %reshape.914), calls=%async_computation.2 | async-start | bytes 524288 | tf_op jit(solution)/shard_map/all_to_all | solution.py:150
  234.7 8.3 %all-to-all-done.2 = f32[8,1,4,2,1024]{4,3,2,1,0:T(2,128)S(1)} async-done(((f32[8,1,4,2,1024]{4,3,2,1,0:T(2,128)}), f32[8,1,4,2,1024]{4,3,2,1,0:T(2,128)S(1)}, u32[]{:S(2)}, u32[]{:S(2)}) %all-to-all-start.2) | async-done | bytes 262176 | tf_op jit(solution)/shard_map/all_to_all | solution.py:150
  242.9 1.0 convolution_bitcast_fusion.2
  244.0 0.8 copy.195
  244.8 2.0 reshape.915
  246.9 7.6 %all-to-all-start.3 = ((f32[32,4,1,2048]{3,1,2,0:T(4,128)}), f32[32,4,1,2048]{3,1,2,0:T(4,128)S(1)}, u32[]{:S(2)}, u32[]{:S(2)}) async-start(f32[32,4,1,2048]{3,1,2,0:T(4,128)} %reshape.915), calls=%async_computation.3 | async-start | bytes 2097152 | tf_op jit(solution)/shard_map/all_to_all | solution.py:164
  254.5 6.3 %fusion.48 = f32[32,32]{0,1:T(8,128)} fusion(f32[2,32,4,16,128]{4,3,2,1,0:T(8,128)} %param.7, f32[2,32,4,16,128]{4,3,2,1,0:T(8,128)S(1)} %get-tuple-element.23), kind=kOutput, calls=%fused_computation.50 | convolution fusion | flops 201326592 | bytes 4198400 | tf_op jit(solution)/shard_map/bixyz,boxyz->io/dot_general | solution.py:44
  260.7 79.6 %all-reduce = (f32[32,32]{0,1:T(8,128)}, f32[32]{0:T(128)}) all-reduce(f32[32,32]{0,1:T(8,128)} %fusion.48, f32[32]{0:T(128)} %get-tuple-element.22), channel_id=1, replica_groups=mesh['slab'=32,'pencil'=8] {'slab','pencil'}, use_global_device_ids=true, to_apply=%region_0.0 | all-reduce | flops 1056 | bytes 8448 | tf_op jit(solution)/shard_map/psum | solution.py:46
  340.4 1.3 broadcast_multiply_fusion
  341.7 1.4 copy.168
  343.1 1.2 broadcast_multiply_fusion.1
  344.3 0.8 fusion.121
  345.1 4.4 %fusion.66 = f32[4,32,32,32]{3,2,1,0:T(8,128)S(1)} fusion(f32[4,32,2,32]{3,1,2,0:T(8,128)} %get-tuple-element.25, f32[4,32,2,32]{3,1,2,0:T(8,128)S(1)} %get-tuple-element.52), kind=kOutput, calls=%fused_computation.90 | convolution fusion | flops 3145728 | bytes 589824 | tf_op jit(solution)/shard_map/zxybi,zxybo->zxyio/dot_general | solution.py:27
  349.4 3.5 subtract_bitcast_fusion
  352.9 3.5 fusion.68
  356.4 3.6 add_bitcast_fusion
  360.7 2.6 copy.164
  363.3 4.4 %reshape.892 = f32[1,4,32,2048]{3,2,1,0:T(8,128)} reshape(f32[1,4,32,2,32,32]{5,4,3,2,1,0:T(8,128)} %copy.164) | data formatting | bytes 2097152 | tf_op jit(solution)/shard_map/reshape | solution.py:139
  367.7 2.7 copy.146
  370.4 6.7 %fusion = f32[128,4,2,32,16,1]{0,3,5,4,1,2:T(8,128)S(1)} fusion(f32[4,32,2,2,32,16]{1,5,4,3,2,0:T(8,128)} %bitcast.206, f32[32,1,128]{2,0,1:T(8,128)S(1)} %copy-done.7, f32[32,1,128]{2,0,1:T(8,128)S(1)} %copy-done.6), kind=kOutput, calls=%fused_computation.1 | convolution fusion | flops 402661376 | bytes 3178496 | tf_op jit(solution)/shard_map/xkrbcy,krn->bcxyn/dot_general | solution.py:169
  377.1 3.4 bitcast_add_fusion
  380.5 2.5 copy.167
  (45 shorter events, 3.8 us)
Async XLA Ops:
  0.6 376.5 %copy-start = (f32[32,32]{1,0:T(8,128)S(1)}, f32[32,32]{1,0:T(8,128)}, u32[]{:S(2)}) copy-start(f32[32,32]{1,0:T(8,128)} %param.13) | copy-start | bytes 12292
  16.6 52.0 %all-to-all-start.4 = ((f32[64,4,2048]{2,1,0:T(4,128)}), f32[64,4,2048]{2,1,0:T(4,128)}, u32[]{:S(2)}, u32[]{:S(2)}) async-start(f32[64,4,2048]{2,1,0:T(4,128)} %copy.151), calls=%async_computation.4 | async-start | bytes 4194304 | tf_op jit(solution)/shard_map/all_to_all | solution.py:82
  68.6 27.7 %all-to-all-start = ((f32[64,4,2048]{2,1,0:T(4,128)}), f32[64,4,2048]{2,1,0:T(4,128)}, u32[]{:S(2)}, u32[]{:S(2)}) async-start(f32[64,4,2048]{2,1,0:T(4,128)} %copy.128), calls=%async_computation | async-start | bytes 4194304 | tf_op jit(solution)/shard_map/all_to_all | solution.py:83
  96.3 65.6 %all-to-all-start.5 = ((f32[1,128,2,1024]{3,2,0,1:T(2,128)}), f32[1,128,2,1024]{3,2,0,1:T(2,128)}, u32[]{:S(2)}, u32[]{:S(2)}) async-start(f32[1,128,2,1024]{3,2,0,1:T(2,128)} %copy.153), calls=%async_computation.5 | async-start | bytes 2097152 | tf_op jit(solution)/shard_map/all_to_all | solution.py:101
  161.9 30.8 %all-to-all-start.1 = ((f32[1,128,2,1024]{3,2,0,1:T(2,128)}), f32[1,128,2,1024]{3,2,0,1:T(2,128)}, u32[]{:S(2)}, u32[]{:S(2)}) async-start(f32[1,128,2,1024]{3,2,0,1:T(2,128)} %copy.130), calls=%async_computation.1 | async-start | bytes 2097152 | tf_op jit(solution)/shard_map/all_to_all | solution.py:102
  172.3 2.8 copy-start.8
  175.2 1.4 copy-start.9
  195.9 7.4 %copy-start.2 = (f32[8,4,2,2,32,16]{5,4,3,0,2,1:T(8,128)S(1)}, f32[8,4,2,2,32,16]{5,4,3,0,2,1:T(8,128)}, u32[]{:S(2)}) copy-start(f32[8,4,2,2,32,16]{5,4,3,0,2,1:T(8,128)} %reshape.877) | copy-start | bytes 786436
  195.9 13.8 %copy-start.1 = (f32[1,4,32,2,32,32]{5,4,2,1,3,0:T(8,128)S(1)}, f32[1,4,32,2,32,32]{5,4,2,1,3,0:T(8,128)}, u32[]{:S(2)}) copy-start(f32[1,4,32,2,32,32]{5,4,2,1,3,0:T(8,128)} %copy_multiply_fusion) | copy-start | bytes 3145732
  220.0 3.5 copy-start.4
  220.0 3.5 copy-start.5
  226.5 7.8 %copy-start.10 = (s32[32]{0:T(128)S(1)}, s32[32]{0:T(128)}, u32[]{:S(2)}) copy-start(s32[32]{0:T(128)} %copy-done.9) | copy-start | bytes 388
  229.8 13.1 %all-to-all-start.2 = ((f32[8,1,4,2,1024]{4,3,2,1,0:T(2,128)}), f32[8,1,4,2,1024]{4,3,2,1,0:T(2,128)S(1)}, u32[]{:S(2)}, u32[]{:S(2)}) async-start(f32[8,1,4,2,1024]{4,3,2,1,0:T(2,128)} %reshape.914), calls=%async_computation.2 | async-start | bytes 524288 | tf_op jit(solution)/shard_map/all_to_all | solution.py:150
  246.9 120.9 %all-to-all-start.3 = ((f32[32,4,1,2048]{3,1,2,0:T(4,128)}), f32[32,4,1,2048]{3,1,2,0:T(4,128)S(1)}, u32[]{:S(2)}, u32[]{:S(2)}) async-start(f32[32,4,1,2048]{3,1,2,0:T(4,128)} %reshape.915), calls=%async_computation.3 | async-start | bytes 2097152 | tf_op jit(solution)/shard_map/all_to_all | solution.py:164
  349.4 3.5 copy-start.3
  367.7 2.7 copy-start.6
  367.7 2.7 copy-start.7
where the time goes:
time: 391 us; the launch traced here: 383 us
  blocking collectives  79.6 us (20%)
  starting transfers between devices  76.5 us (20%)
  matrix products  72.1 us (18%)
  local copies, waits for them, and re-layouts  67.9 us (17%)
  waiting for transfers between devices  67.4 us (17%)
  other arithmetic  18.4 us (5%)
    psum x1, blocking collectives, per_device(): lax.psum((local_weight, local_bias), ('slab', 'pencil'))  79.6 us
    all_to_all x1, starting transfers between devices, per_device(): lax.all_to_all(x_spectra[0], 'pencil', split_axis=1, concat_axis=0, tiled...  39.7 us
    all_to_all x1, waiting for transfers between devices, per_device(): lax.all_to_all(z_spectra[0], 'slab', split_axis=0, concat_axis=1, tiled=T...  19.5 us
    all_to_all x1, waiting for transfers between devices, per_device(): lax.all_to_all(x_spectra[0], 'pencil', split_axis=1, concat_axis=0, tiled...  18.1 us
    dot_general x4, matrix products, outer_sum(): jnp.einsum('zxybi,zxybo->zxyio', left_side, right_side, precision=HIGHEST)  14.9 us
    all_to_all x1, starting transfers between devices, per_device(): lax.all_to_all(z_spectra[0], 'slab', split_axis=0, concat_axis=1, tiled=T...  14.8 us
    all_to_all x1, waiting for transfers between devices, per_device(): lax.all_to_all(z_spectra[1], 'slab', split_axis=0, concat_axis=1, tiled=T...  14.6 us
    dot_general x4, matrix products, contract_out(): return jnp.einsum('zxyio,zxybo->zxybi', weights, values, precision=HIGHEST)  13.6 us
  transfers between devices with their start and end apart: 6, of which 5 were waited for; matrix products, arithmetic and copies ran while one was open for 23% of the time, Pallas kernels for 0%

commit v1 on v0

v1 whole, which is shorter than its diff:
```python
import math

import jax
import jax.numpy as jnp
import numpy as np
from jax import lax
from jax.experimental import pallas as pl
from jax.experimental.pallas import tpu as pltpu
from jax.sharding import Mesh
from jax.sharding import PartitionSpec as P

HIGH = lax.Precision.HIGH
F32 = jnp.float32
BF16 = jnp.bfloat16
CELLS = 4194304.0
UNIT = 1.0 / math.sqrt(128.0 * 128.0 * 128.0)
PLANE = ("yp", "xp")
COLUMN = ("zh", "zl", "co")


def mm(left, right, left_dim=1, right_dim=0, precision=HIGH):
    dims = (((left_dim,), (right_dim,)), ((), ()))
    return lax.dot_general(left, right, dims, precision=precision, preferred_element_type=F32)


def halves(values):
    top = values.astype(BF16)
    return top, (values - top.astype(F32)).astype(BF16)


def mm_exact(values, pattern):
    top, rest = halves(values)
    return mm(top, pattern, precision=None) + mm(rest, pattern, precision=None)


def wave(frequency, position):
    angle = 2.0 * np.pi * ((frequency * position) % 128) / 128.0
    return np.cos(angle), np.sin(angle)


def z_table():
    d, x, r, h, x2, z = np.ogrid[:16, :2, :2, :2, :2, :128]
    c, s = wave(8 * (d // 4) + 4 * h + d % 4, z)
    return np.where(x == x2, np.where(r == 0, c, -s), 0.0).reshape(128, 256).astype(np.float32)


def z_back_table():
    d, x, r, h, x2, z = np.ogrid[:16, :2, :2, :2, :2, :128]
    c, s = wave(8 * (d // 4) + 4 * h + d % 4, z)
    return np.where(x == x2, np.where(r == 0, c, -s) * UNIT, 0.0).reshape(128, 256).astype(np.float32)


def turn(cosine, sine, r_out, r_in):
    return np.where(r_out == r_in, cosine, np.where(r_out == 0, -sine, sine))


def x_table():
    zh, h2, q, r2, d, x, r, h = np.ogrid[:2, :2, :32, :2, :16, :4, :2, :2]
    c, s = wave(q - 16, 32 * (d // 4) + 16 * zh + 4 * (d % 4) + x)
    return np.where(h == h2, turn(c, -s, r2, r), 0.0).reshape(2, 128, 256).astype(np.float32)


def x_back_table():
    zh, d, x, r2, h2, h, q, r = np.ogrid[:2, :16, :4, :2, :2, :2, :32, :2]
    c, s = wave(q - 16, 32 * (d // 4) + 16 * zh + 4 * (d % 4) + x)
    return np.where(h == h2, turn(c, s, r2, r), 0.0).reshape(2, 256, 128).astype(np.float32)


def y_table():
    odd, r2, k, r, zh, pen, j = np.ogrid[:2, :2, :32, :2, :2, :8, :8]
    c, s = wave(k - 16, 16 * pen + 2 * j + odd)
    return (turn(c, -s, r2, r) * UNIT + 0.0 * zh).reshape(128, 256).astype(np.float32)


def y_back_table():
    r2, pen, j, odd, r, k = np.ogrid[:2, :8, :8, :2, :2, :32]
    c, s = wave(k - 16, 16 * pen + 2 * j + odd)
    return turn(c, s, r2, r).reshape(128, 128).astype(np.float32)


def spread_patterns():
    half, b, c, b2, i, o = np.ogrid[:2, :2, :32, :2, :32, :32]
    same = (half == 0) & (b == b2)
    by_in = (same & (c == i) & (o >= 0)).reshape(128, 2048)
    by_out = (same & (c == o) & (i >= 0)).reshape(128, 2048)
    return by_in.astype(np.float32), by_out.astype(np.float32)


def front_kernel(table, layer, pre, out_grad, grad, message):
    layer, pre, out_grad, grad2 = (ref.reshape(1024, 128) for ref in (layer, pre, out_grad, grad))

    def slope(i, carry):
        rows = pl.ds(pl.multiple_of(i * 64, 64), 64)
        v = pre[rows, :]
        cdf = 0.5 * (1.0 + lax.erf(v * (1.0 / math.sqrt(2.0))))
        bump = v * jnp.exp(-0.5 * v * v) * (1.0 / math.sqrt(2.0 * math.pi))
        grad2[rows, :] = out_grad[rows, :] * (cdf + bump)
        return carry

    lax.fori_loop(0, 16, slope, 0)
    for field, values in ((0, layer), (1, grad2)):
        for j in range(4):
            cells = jnp.concatenate(
                [
                    jnp.concatenate(
                        [values[pl.ds(x * 8 + 2 * j + odd, 64, stride=16), :] for odd in range(2)], 0
                    )
                    for x in range(2)
                ],
                1,
            )
            spectrum = mm(table[...], cells, 1, 1)
            message[:, field, 0, 8 * j : 8 * j + 8, :] = spectrum.reshape(16, 8, 128)


def local_kernel(point, layer, grad, base, sums, products, totals):
    layer, grad, base = (ref.reshape(1024, 128) for ref in (layer, grad, base))
    step = pl.program_id(0) * 2 + pl.program_id(1)

    @pl.when(step == 0)
    def _():
        products[...] = jnp.zeros_like(products)
        totals[...] = jnp.zeros_like(totals)

    for cell in range(0, 16, 2):
        u = jnp.concatenate([layer[pl.ds(cell + k, 64, stride=16), :] for k in range(2)], 1)
        g = jnp.concatenate([grad[pl.ds(cell + k, 64, stride=16), :] for k in range(2)], 1)
        products[...] += mm(u, g, 1, 1)
        totals[...] += g[:, :128] + g[:, 128:]
        mixed = mm(point[...], g)
        for k in range(2):
            base[pl.ds(cell + k, 64, stride=16), :] = mixed[:, 128 * k : 128 * k + 128]

    @pl.when(step == 3)
    def _():
        sums[...] = jnp.zeros_like(sums)
        by_pair = products[0:32, 0:32] + products[32:64, 32:64]
        for k in range(4):
            sums[0, :, 32 * k : 32 * k + 32] = by_pair[8 * k : 8 * k + 8, :]
        bias = mm(jnp.ones((8, 128), F32), totals[...], 1, 1, lax.Precision.HIGHEST)
        sums[1, :, 0:32] = bias[:, 0:32] + bias[:, 32:64]


def weight_kernel(spread, codes, scales, noise, weight):
    step = jnp.exp2(scales[...].astype(F32) * -0.25) * (1.0 / (16.0 * math.sqrt(32.0)))
    top, rest = halves(step)
    last = (step - top.astype(F32) - rest.astype(F32)).astype(BF16)
    wide = sum(mm(part, spread[...], precision=None) for part in (last, rest, top))
    weight[...] = codes[...].astype(F32) * wide * (1.0 + noise[...])


def x_kernel(zh, table, arrived, sums, message):
    field, half = pl.program_id(0), pl.program_id(1)

    @pl.when(field + half == 0)
    def _():
        message[:, 16:18] = jnp.broadcast_to(sums[...][None], (16, 2, 8, 128))

    for j in range(4):
        cells = arrived[:, 0, :, 8 * j : 8 * j + 8, :].reshape(256, 128)
        message[:, field * 8 + half * 4 + j] = mm(table[0], cells).reshape(16, 8, 128)


def along_y(table, arrived):
    rows = arrived.reshape(1024, 128)
    real, imag = [], []
    for kx in range(4):
        cells = jnp.concatenate([rows[pl.ds(2 * kx + r, 128, stride=8), :] for r in range(2)], 0)
        modes = mm(table[...], cells)
        modes = modes[:64] + pltpu.roll(modes[64:], 64, 1)
        real.append(modes[:32])
        imag.append(modes[32:])
    return jnp.concatenate(real, 0), jnp.concatenate(imag, 0)


def mode_kernel(table, back_table, by_out, gather, weight, arrived, g_hat, message):
    g_real, g_imag = along_y(table, arrived)
    g_hat[0] = g_real
    g_hat[1] = g_imag
    q_real = jnp.zeros((128, 128), F32)
    q_imag = jnp.zeros((128, 128), F32)
    for part in range(4):
        lanes = slice(512 * part, 512 * part + 512)
        pairs = 512 * (part % 2)
        wide_real = mm_exact(g_real, by_out[:, lanes])
        wide_imag = mm_exact(g_imag, by_out[:, lanes])
        w_real = weight[:, pairs : pairs + 512]
        w_imag = weight[:, 1024 + pairs : 1536 + pairs]
        q_real += mm_exact(w_real * wide_real + w_imag * wide_imag, gather[lanes, :])
        q_imag += mm_exact(w_real * wide_imag - w_imag * wide_real, gather[lanes, :])
    rows = message.reshape(1024, 128)
    for kx in range(4):
        some = slice(32 * kx, 32 * kx + 32)
        modes = jnp.concatenate([q_real[some], q_imag[some]], 0)
        cells = mm(back_table[...], jnp.concatenate([modes, pltpu.roll(modes, 64, 1)], 0))
        for r in range(2):
            for zh in range(2):
                rows[pl.ds(512 * zh + 2 * kx + r, 64, stride=8), :] = cells[64 * r : 64 * r + 64]


def outer_kernel(table, by_in, by_out, arrived, g_hat, result):
    u_real, u_imag = along_y(table, arrived)
    g_real, g_imag = g_hat[0], g_hat[1]
    for pairs in range(0, 1024, 256):
        real = jnp.zeros((128, 256), F32)
        imag = jnp.zeros((128, 256), F32)
        for b in range(2):
            lanes = slice(1024 * b + pairs, 1024 * b + pairs + 256)
            ur, ui = mm_exact(u_real, by_in[:, lanes]), mm_exact(u_imag, by_in[:, lanes])
            gr, gi = mm_exact(g_real, by_out[:, lanes]), mm_exact(g_imag, by_out[:, lanes])
            real += ur * gr + ui * gi
            imag += ur * gi - ui * gr
        result[:, pairs : pairs + 256] = real
        result[:, 1024 + pairs : 1280 + pairs] = imag


def x_back_kernel(zh, table, arrived, sums, message):
    message[:, 16:18] = jnp.broadcast_to(jnp.sum(sums[...], axis=0)[None], (16, 2, 8, 128))
    for j in range(8):
        cells = mm(table[0], arrived[:, j].reshape(128, 128)).reshape(16, 2, 8, 128)
        message[:, j] = cells[:, 0]
        message[:, 8 + j] = cells[:, 1]


def end_kernel(table, arrived, sums, base, result, grad_point, grad_bias):
    base, result = base.reshape(1024, 128), result.reshape(1024, 128)

    @pl.when(pl.program_id(0) + pl.program_id(1) == 0)
    def _():
        total = jnp.sum(sums[...], axis=0) * (1.0 / CELLS)
        for k in range(4):
            grad_point[8 * k : 8 * k + 8, :] = total[0, :, 32 * k : 32 * k + 32]
        grad_bias[...] = total[1, 0:1, 0:32]

    for j in range(4):
        cells = mm(arrived[:, j].reshape(128, 128), table[...], 0, 0)
        for x in range(2):
            for odd in range(2):
                rows = pl.ds(x * 8 + 2 * j + odd, 64, stride=16)
                result[rows, :] = (
                    base[rows, :] + cells[64 * odd : 64 * odd + 64, 128 * x : 128 * x + 128]
                )


def params(steps=0):
    return pltpu.CompilerParams(
        dimension_semantics=("arbitrary",) * steps if steps else None,
        vmem_limit_bytes=48 * 1024 * 1024,
    )


def cost(flops, moved):
    return pl.CostEstimate(flops=flops, bytes_accessed=moved, transcendentals=0)


def whole(*shape):
    return pl.BlockSpec(shape, lambda *_: (0,) * len(shape))


def shaped(*shape):
    return jax.ShapeDtypeStruct(shape, F32)


def exchange(message, axes):
    return lax.all_to_all(message, axes, split_axis=0, concat_axis=0, tiled=True)


def per_device(
    layer_input, pre_act, out_grad, weight_codes, scale_codes, weight_noise, point_weight
):
    layer, pre, slope_in = (v.reshape(64, 4, 16, 128) for v in (layer_input, pre_act, out_grad))
    zh = lax.axis_index("zh").reshape(1)
    mega = 1 << 20
    field = pl.BlockSpec((64, 2, 8, 128), lambda p, h: (0, p, h, 0))
    grad, message = pl.pallas_call(
        front_kernel,
        grid=(2, 2),
        in_specs=[whole(128, 256), field, field, field],
        out_specs=[field, pl.BlockSpec((16, 2, 1, 32, 128), lambda p, h: (0, 0, p, h, 0))],
        out_shape=[shaped(64, 4, 16, 128), shaped(16, 2, 2, 64, 128)],
        compiler_params=params(2),
        cost_estimate=cost(1 << 30, 10 * mega),
        name="front",
    )(z_table(), layer, pre, slope_in)
    arrived = exchange(message, PLANE)

    blocks = np.kron(np.eye(2, dtype=np.float32), np.ones((32, 32), np.float32))
    both = jnp.tile(point_weight, (2, 2)) * blocks
    base, sums = pl.pallas_call(
        local_kernel,
        grid=(2, 2),
        in_specs=[whole(64, 64), field, field],
        out_specs=[field, whole(2, 8, 128)],
        out_shape=[shaped(64, 4, 16, 128), shaped(2, 8, 128)],
        scratch_shapes=[pltpu.VMEM((64, 64), F32), pltpu.VMEM((64, 128), F32)],
        compiler_params=params(2),
        cost_estimate=cost(1 << 30, 6 * mega),
        name="local",
    )(both, layer, grad)

    spread = np.kron(np.eye(64, dtype=np.float32), np.ones((1, 32), np.float32))
    column = pl.BlockSpec((128, 512), lambda i: (0, i))
    codes, _ = lax.optimization_barrier((weight_codes, sums))
    weight = pl.pallas_call(
        weight_kernel,
        grid=(4,),
        in_specs=[pl.BlockSpec((64, 512), lambda i: (0, i)), column, whole(128, 64), column],
        out_specs=column,
        out_shape=shaped(128, 2048),
        compiler_params=params(1),
        cost_estimate=cost(1 << 27, 3 * mega),
        name="weight",
    )(
        jnp.asarray(spread, BF16),
        codes.reshape(128, 2048),
        scale_codes.reshape(128, 64),
        weight_noise.reshape(128, 2048),
    )

    message = pl.pallas_call(
        x_kernel,
        grid_spec=pltpu.PrefetchScalarGridSpec(
            num_scalar_prefetch=1,
            grid=(2, 2),
            in_specs=[
                pl.BlockSpec((1, 128, 256), lambda f, h, zh: (zh[0], 0, 0)),
                pl.BlockSpec((16, 1, 2, 32, 128), lambda f, h, zh: (0, f, 0, h, 0)),
                whole(2, 8, 128),
            ],
            out_specs=whole(16, 18, 8, 128),
        ),
        out_shape=shaped(16, 18, 8, 128),
        compiler_params=params(2),
        cost_estimate=cost(1 << 29, 3 * mega),
        name="x_modes",
    )(zh, x_table(), arrived, sums)
    arrived = exchange(message, COLUMN)

    by_in, by_out = (jnp.asarray(v, BF16) for v in spread_patterns())
    gather = jnp.asarray(spread_patterns()[0].T, BF16)
    y_modes = jnp.asarray(y_table())
    half = (16, 8, 8, 128)
    g_hat, message = pl.pallas_call(
        mode_kernel,
        grid=(1,),
        in_specs=[
            whole(128, 256),
            whole(128, 128),
            whole(128, 2048),
            whole(2048, 128),
            whole(128, 2048),
            pl.BlockSpec(half, lambda i: (0, 1, 0, 0)),
        ],
        out_specs=[whole(2, 128, 128), whole(*half)],
        out_shape=[shaped(2, 128, 128), shaped(*half)],
        compiler_params=params(1),
        cost_estimate=cost(1 << 30, 4 * mega),
        name="modes",
    )(y_modes, y_back_table(), by_out, gather, weight, arrived)
    returned = exchange(message, COLUMN)

    grad_spectral = pl.pallas_call(
        outer_kernel,
        grid=(1,),
        in_specs=[
            whole(128, 256),
            whole(128, 2048),
            whole(128, 2048),
            pl.BlockSpec(half, lambda i: (0, 0, 0, 0)),
            whole(2, 128, 128),
        ],
        out_specs=whole(128, 2048),
        out_shape=shaped(128, 2048),
        compiler_params=params(1),
        cost_estimate=cost(1 << 30, 4 * mega),
        name="outer",
    )(y_modes, by_in, by_out, arrived, g_hat)

    last_tiles = pl.BlockSpec((16, 2, 8, 128), lambda *_: (0, 8, 0, 0))
    message = pl.pallas_call(
        x_back_kernel,
        grid_spec=pltpu.PrefetchScalarGridSpec(
            num_scalar_prefetch=1,
            grid=(1,),
            in_specs=[
                pl.BlockSpec((1, 256, 128), lambda i, zh: (zh[0], 0, 0)),
                whole(*half),
                last_tiles,
            ],
            out_specs=whole(16, 18, 8, 128),
        ),
        out_shape=shaped(16, 18, 8, 128),
        compiler_params=params(1),
        cost_estimate=cost(1 << 29, 2 * mega),
        name="x_cells",
    )(zh, x_back_table(), returned, arrived)
    returned = exchange(message, PLANE)

    grad_input, grad_point, grad_bias = pl.pallas_call(
        end_kernel,
        grid=(2, 2),
        in_specs=[
            whole(128, 256),
            pl.BlockSpec((16, 4, 8, 128), lambda p, h: (0, 2 * p + h, 0, 0)),
            last_tiles,
            field,
        ],
        out_specs=[field, whole(32, 32), whole(1, 32)],
        out_shape=[shaped(64, 4, 16, 128), shaped(32, 32), shaped(1, 32)],
        compiler_params=params(2),
        cost_estimate=cost(1 << 29, 5 * mega),
        name="end",
    )(z_back_table(), returned, returned, base)
    return (
        grad_input.reshape(layer_input.shape),
        grad_spectral.reshape(weight_codes.shape),
        grad_point,
        grad_bias.reshape(32),
    )


def solution(mesh):
    fine = Mesh(mesh.devices.reshape(4, 2, 4, 4, 2), ("yp", "zh", "xp", "zl", "co"))
    slab, pencil = ("yp", "zh", "xp"), ("zl", "co")
    field, modes = P(None, None, slab, pencil, None), P(slab, pencil, None, None)
    return jax.shard_map(
        per_device,
        mesh=fine,
        in_specs=(field, field, field, modes, modes, modes, P()),
        out_specs=(field, modes, P(), P()),
        check_vma=False,
    )
```

time: 391 us -> 155 us (0.40); the launches traced: 383 us -> 154 us
  matrix products: 72.1 us -> 0 us
  blocking collectives: 79.6 us -> 20.8 us
  starting transfers between devices: 76.5 us -> 22.1 us
  local copies, waits for them, and re-layouts: 67.9 us -> 16.2 us
  Pallas kernels: 0 us -> 27.3 us
  other arithmetic: 18.4 us -> 0.03 us
    psum x1 -> x0, blocking collectives: 79.6 us -> none  [per_device(): lax.psum((local_weight, local_bias), ('slab', 'pencil'))]
    dot_general x19 -> x0, matrix products: 72.1 us -> none  [the longest x4 14.9 us: outer_sum(): jnp.einsum('zxybi,zxybo->zxyio', left_side, right_side, precision=HIGHEST)]
    all_to_all x6 -> x3, starting transfers between devices: 76.5 us -> 22.1 us  [exchange(): lax.all_to_all(message, axes, split_axis=0, concat_axis=0, tiled=True)]
    pallas_call x0 -> x8, Pallas kernels: none -> 27.3 us  [the longest x1 6.19 us: per_device(): pl.pallas_call(front_kernel, grid=(2, 2), in_specs=[whole(128, 256), fiel...]
    reshape x6 -> x0, local copies, waits for them, and re-layouts: 22.5 us -> none  [the longest x2 9.95 us: along_z(): return moved_axes.reshape(freq_rows, x_cells, -1)]
    all_to_all x0 -> x1, blocking collectives: none -> 20.8 us  [exchange(): lax.all_to_all(message, axes, split_axis=0, concat_axis=0, tiled=True)]
    transpose x6 -> x0, local copies, waits for them, and re-layouts: 16.9 us -> none  [the longest x2 10.4 us: along_z(): jnp.einsum('bcxyn,nfr->fxrbcy', field_data, z_table, precision=HIGHEST)]
    another operation x6 -> x0, local copies, waits for them, and re-layouts: 12 us -> none
  transfers between devices with their start and end apart: 6 -> 3, of which waited for: 5 -> 3; matrix products, arithmetic and copies ran while one was open for 23% -> 0% of each run, Pallas kernels for 0% -> 6%
where the time goes in v1:
time: 155 us; the launch traced here: 154 us
  waiting for transfers between devices  66.6 us (43%)
  Pallas kernels  27.3 us (18%)
  starting transfers between devices  22.1 us (14%)
  blocking collectives  20.8 us (13%)
  local copies, waits for them, and re-layouts  16.2 us (10%)
    all_to_all x3, waiting for transfers between devices, exchange(): lax.all_to_all(message, axes, split_axis=0, concat_axis=0, tiled=True)  66.6 us
    all_to_all x3, starting transfers between devices, exchange(): lax.all_to_all(message, axes, split_axis=0, concat_axis=0, tiled=True)  22.1 us
    all_to_all x1, blocking collectives, exchange(): lax.all_to_all(message, axes, split_axis=0, concat_axis=0, tiled=True)  20.8 us
    unnamed x52, local copies, waits for them, and re-layouts  16.1 us
    pallas_call x1, Pallas kernels, per_device(): pl.pallas_call(front_kernel, grid=(2, 2), in_specs=[whole(128, 256), fiel...  6.19 us
    pallas_call x1, Pallas kernels, per_device(): pl.pallas_call(local_kernel, grid=(2, 2), in_specs=[whole(64, 64), field,...  4.87 us
    pallas_call x1, Pallas kernels, per_device(): pl.pallas_call(x_kernel, grid_spec=pltpu.PrefetchScalarGridSpec(num_scala...  4.45 us
    pallas_call x1, Pallas kernels, per_device(): pl.pallas_call(end_kernel, grid=(2, 2), in_specs=[whole(128, 256), pl.Blo...  3.61 us
  transfers between devices with their start and end apart: 3, of which 3 were waited for; matrix products, arithmetic and copies ran while one was open for 0% of the time, Pallas kernels for 6%

profile of v1, /device:TPU:1, one launch (start us, length us, event | category | flops | bytes accessed | tf_op | source)
XLA Modules:
  0.0 153.9 jit_solution(8856770195436573171)
XLA Ops:
  0.6 0.0 copy-start.13
  0.6 0.9 copy-done.13
  1.5 6.2 %front.1 = (f32[64,4,16,128]{3,2,1,0:T(8,128)S(1)}, f32[16,2,2,64,128]{4,3,2,1,0:T(8,128)S(1)}) custom-call(f32[128,256]{1,0:T(8,128)S(1)} %copy-done.13, f32[64,4,16,128]{3,2,1,0:T(8,128)} %bitcast.10, f32[64,4,16,128]{3,2,1,0:T(8,128)} %bitcast.15, f32[64,4,16,128]{3,2,1,0:T(8,128)} %bitcast.16), custom_call_target="tpu_custom_call" | custom-call | flops 1073741824 | bytes 10485760 | tf_op jit(solution)/shard_map/front/pallas_call | solution.py:275
  7.7 0.0 copy-start.3
  7.8 1.3 copy-done.3
  9.1 0.0 copy-start.4
  9.1 1.3 copy-done.4
  10.4 0.0 copy-start.25
  10.4 0.0 copy-start
  10.4 7.8 %all-to-all-start = ((f32[16,2,2,64,128]{4,3,2,1,0:T(8,128)}), f32[16,2,2,64,128]{4,3,2,1,0:T(8,128)}, u32[]{:S(2)}, u32[]{:S(2)}) async-start(f32[16,2,2,64,128]{4,3,2,1,0:T(8,128)} %copy-done.3), calls=%async_computation | async-start | bytes 4194304 | tf_op jit(solution)/shard_map/all_to_all | solution.py:265
  18.2 0.0 copy-done.24
  18.2 0.0 copy-done.25
  18.2 0.1 reshape.50.point
  18.3 0.0 copy-done
  18.3 4.9 %local.1 = (f32[64,4,16,128]{3,2,1,0:T(8,128)S(1)}, f32[2,8,128]{2,1,0:T(8,128)S(1)}) custom-call(f32[64,64]{1,0:T(8,128)S(1)} %reshape.50.point, f32[64,4,16,128]{3,2,1,0:T(8,128)S(1)} %bitcast.11, f32[64,4,16,128]{3,2,1,0:T(8,128)} %copy-done.4), custom_call_target="tpu_custom_call" | custom-call | flops 1073741824 | bytes 6291456 | tf_op jit(solution)/shard_map/local/pallas_call | solution.py:289
  23.2 0.0 copy-start.1
  23.2 1.3 copy-done.1
  24.5 24.2 %all-to-all-done.arrived = f32[16,2,2,64,128]{4,3,2,1,0:T(8,128)} async-done(((f32[16,2,2,64,128]{4,3,2,1,0:T(8,128)}), f32[16,2,2,64,128]{4,3,2,1,0:T(8,128)}, u32[]{:S(2)}, u32[]{:S(2)}) %all-to-all-start) | async-done | bytes 2097184 | tf_op jit(solution)/shard_map/all_to_all | solution.py:265
  48.7 0.0 copy-start.11
  48.7 0.9 copy-done.11
  49.7 0.0 copy-start.5
  49.7 0.0 copy-start.6
  49.7 0.0 copy-start.10
  49.7 4.5 %x_modes.1 = f32[16,18,8,128]{3,2,1,0:T(8,128)} custom-call(s32[1]{0:T(128)} %bitcast.zh, f32[2,128,256]{2,1,0:T(8,128)S(1)} %copy-done.11, f32[16,2,2,64,128]{4,3,2,1,0:T(8,128)} %all-to-all-done.arrived, f32[2,8,128]{2,1,0:T(8,128)S(1)} %get-tuple-element.15.sums), custom_call_target="tpu_custom_call" | custom-call | flops 536870912 | bytes 3145728 | tf_op jit(solution)/shard_map/x_modes/pallas_call | solution.py:320
  54.1 10.6 %all-to-all-start.1 = ((f32[16,18,8,128]{3,2,1,0:T(8,128)}), f32[16,18,8,128]{3,2,1,0:T(8,128)S(1)}, u32[]{:S(2)}, u32[]{:S(2)}) async-start(f32[16,18,8,128]{3,2,1,0:T(8,128)} %x_modes.1), calls=%async_computation.1 | async-start | bytes 2359296 | tf_op jit(solution)/shard_map/all_to_all | solution.py:265
  64.7 0.0 copy-done.5
  64.7 0.0 copy-done.6
  64.7 0.0 copy-done.10
  64.8 0.0 copy-start.14
  64.8 0.8 copy-done.14
  65.6 1.3 weight.1
  66.9 0.0 copy-start.7
  66.9 1.0 copy-done.7
  67.9 27.4 %all-to-all-done.1.arrived.sums = f32[16,18,8,128]{3,2,1,0:T(8,128)S(1)} async-done(((f32[16,18,8,128]{3,2,1,0:T(8,128)}), f32[16,18,8,128]{3,2,1,0:T(8,128)S(1)}, u32[]{:S(2)}, u32[]{:S(2)}) %all-to-all-start.1) | async-done | bytes 1179680 | tf_op jit(solution)/shard_map/all_to_all | solution.py:265
  95.3 0.0 copy-start.8
  95.3 1.2 copy-done.8
  96.5 0.0 copy-start.15
  96.5 1.0 copy-done.15
  97.6 0.0 copy-start.18
  97.6 1.0 copy-done.18
  98.6 0.0 copy-start.19
  98.6 0.9 copy-done.19
  99.5 0.0 copy-start.21
  99.5 0.8 copy-done.21
  100.3 0.0 copy-start.9
  100.3 2.7 %modes.1 = (f32[2,128,128]{2,1,0:T(8,128)S(1)}, f32[16,8,8,128]{3,2,1,0:T(8,128)S(1)}) custom-call(f32[128,256]{1,0:T(8,128)S(1)} %copy-done.19, f32[128,128]{1,0:T(8,128)S(1)} %copy-done.21, bf16[128,2048]{1,0:T(8,128)(2,1)S(1)} %copy-done.15, bf16[2048,128]{1,0:T(8,128)(2,1)S(1)} %copy-done.18, f32[128,2048]{1,0:T(8,128)S(1)} %copy-done.8, ...), custom_call_target="tpu_custom_call" | custom-call | flops 1073741824 | bytes 4194304 | tf_op jit(solution)/shard_map/modes/pallas_call | solution.py:343
  103.0 0.0 copy-start.22
  103.0 20.8 %all_to_all.20.arrived = f32[16,8,8,128]{3,2,1,0:T(8,128)S(1)} all-to-all(f32[16,8,8,128]{3,2,1,0:T(8,128)S(1)} %get-tuple-element.18), channel_id=1, replica_groups=mesh['yp'=4,'zh'=2,'xp'=4,'zl'=4,'co'=2] {'zh','zl','co'}, dimensions={0} | all-to-all | bytes 1048576 | tf_op jit(solution)/shard_map/all_to_all | solution.py:265
  123.8 0.0 copy-done.22
  123.8 0.0 copy-done.9
  123.8 0.0 copy-start.16
  123.9 1.6 %x_cells.1 = f32[16,18,8,128]{3,2,1,0:T(8,128)} custom-call(s32[1]{0:T(128)} %bitcast.zh, f32[2,256,128]{2,1,0:T(8,128)S(1)} %copy-done.9, f32[16,8,8,128]{3,2,1,0:T(8,128)S(1)} %all_to_all.20.arrived, f32[16,18,8,128]{3,2,1,0:T(8,128)S(1)} %all-to-all-done.1.arrived.sums), custom_call_target="tpu_custom_call" | custom-call | flops 536870912 | bytes 2097152 | tf_op jit(solution)/shard_map/x_cells/pallas_call | solution.py:380
  125.4 3.7 %all-to-all-start.3 = ((f32[16,18,8,128]{3,2,1,0:T(8,128)}), f32[16,18,8,128]{3,2,1,0:T(8,128)S(1)}, u32[]{:S(2)}, u32[]{:S(2)}) async-start(f32[16,18,8,128]{3,2,1,0:T(8,128)} %x_cells.1), calls=%async_computation.3 | async-start | bytes 2359296 | tf_op jit(solution)/shard_map/all_to_all | solution.py:265
  129.2 0.0 copy-start.12
  129.2 0.0 copy-done.16
  129.2 0.0 copy-done.17
  129.2 0.0 copy-start.20
  129.2 0.9 copy-done.20
  130.1 0.9 copy-done.23
  131.0 2.7 %outer.1 = f32[128,2048]{1,0:T(8,128)} custom-call(f32[128,256]{1,0:T(8,128)S(1)} %copy-done.20, bf16[128,2048]{1,0:T(8,128)(2,1)S(1)} %copy-done.17, bf16[128,2048]{1,0:T(8,128)(2,1)S(1)} %copy-done.16, f32[16,18,8,128]{3,2,1,0:T(8,128)S(1)} %all-to-all-done.1.arrived.sums, f32[2,128,128]{2,1,0:T(8,128)S(1)} %copy-done.23), custom_call_target="tpu_custom_call" | custom-call | flops 1073741824 | bytes 4194304 | tf_op jit(solution)/shard_map/outer/pallas_call | solution.py:362
  133.7 15.0 %all-to-all-done.3.arrived.sums = f32[16,18,8,128]{3,2,1,0:T(8,128)S(1)} async-done(((f32[16,18,8,128]{3,2,1,0:T(8,128)}), f32[16,18,8,128]{3,2,1,0:T(8,128)S(1)}, u32[]{:S(2)}, u32[]{:S(2)}) %all-to-all-start.3) | async-done | bytes 1179680 | tf_op jit(solution)/shard_map/all_to_all | solution.py:265
  148.7 0.0 copy-done.12
  148.7 1.6 %copy-done.2 = f32[64,4,16,128]{3,2,1,0:T(8,128)S(1)} copy-done((f32[64,4,16,128]{3,2,1,0:T(8,128)S(1)}, f32[64,4,16,128]{3,2,1,0:T(8,128)}, u32[]{:S(2)}) %copy-start.2) | copy-done | bytes 2097176
  150.3 3.6 %end.1 = (f32[64,4,16,128]{3,2,1,0:T(8,128)}, f32[32,32]{1,0:T(8,128)}, f32[1,32]{1,0:T(1,128)}) custom-call(f32[128,256]{1,0:T(8,128)S(1)} %copy-done.12, f32[16,18,8,128]{3,2,1,0:T(8,128)S(1)} %all-to-all-done.3.arrived.sums, f32[16,18,8,128]{3,2,1,0:T(8,128)S(1)} %all-to-all-done.3.arrived.sums, f32[64,4,16,128]{3,2,1,0:T(8,128)S(1)} %copy-done.2), custom_call_target="tpu_custom_call" | custom-call | flops 536870912 | bytes 5242880 | tf_op jit(solution)/shard_map/end/pallas_call | solution.py:399
  (5 shorter events, 0.0 us)
Async XLA Ops:
  0.6 0.9 copy-start.13
  7.7 1.3 copy-start.3
  9.1 1.3 copy-start.4
  10.4 7.8 %copy-start.24 = (f32[2,32,2,32]{3,2,1,0:T(2,128)S(1)}, f32[2,32,2,32]{3,2,1,0:T(2,128)}, u32[]{:S(2)}) copy-start(f32[2,32,2,32]{3,2,1,0:T(2,128)} %constant.45) | copy-start | bytes 49156
  10.4 7.8 %copy-start.25 = (f32[32,32]{1,0:T(8,128)S(1)}, f32[32,32]{1,0:T(8,128)}, u32[]{:S(2)}) copy-start(f32[32,32]{1,0:T(8,128)} %param.24) | copy-start | bytes 12292
  10.4 7.9 %copy-start = (f32[2,32,4,16,128]{4,3,2,1,0:T(8,128)S(1)}, f32[2,32,4,16,128]{4,3,2,1,0:T(8,128)}, u32[]{:S(2)}) copy-start(f32[2,32,4,16,128]{4,3,2,1,0:T(8,128)} %param.18) | copy-start | bytes 6291460
  10.4 38.3 %all-to-all-start = ((f32[16,2,2,64,128]{4,3,2,1,0:T(8,128)}), f32[16,2,2,64,128]{4,3,2,1,0:T(8,128)}, u32[]{:S(2)}, u32[]{:S(2)}) async-start(f32[16,2,2,64,128]{4,3,2,1,0:T(8,128)} %copy-done.3), calls=%async_computation | async-start | bytes 4194304 | tf_op jit(solution)/shard_map/all_to_all | solution.py:265
  23.2 1.3 copy-start.1
  48.7 1.0 copy-start.11
  49.7 15.1 %copy-start.5 = (s32[1,4,32,2048]{3,2,1,0:T(8,128)S(1)}, s32[1,4,32,2048]{3,2,1,0:T(8,128)}, u32[]{:S(2)}) copy-start(s32[1,4,32,2048]{3,2,1,0:T(8,128)} %param.21) | copy-start | bytes 3145732
  49.7 15.1 %copy-start.6 = (f32[1,4,32,2048]{3,2,1,0:T(8,128)S(1)}, f32[1,4,32,2048]{3,2,1,0:T(8,128)}, u32[]{:S(2)}) copy-start(f32[1,4,32,2048]{3,2,1,0:T(8,128)} %param.23) | copy-start | bytes 3145732
  49.7 15.1 %copy-start.10 = (bf16[64,2048]{1,0:T(8,128)(2,1)S(1)}, bf16[64,2048]{1,0:T(8,128)(2,1)}, u32[]{:S(2)}) copy-start(bf16[64,2048]{1,0:T(8,128)(2,1)} %constant.30.clone.spread) | copy-start | bytes 786436
  54.1 41.2 %all-to-all-start.1 = ((f32[16,18,8,128]{3,2,1,0:T(8,128)}), f32[16,18,8,128]{3,2,1,0:T(8,128)S(1)}, u32[]{:S(2)}, u32[]{:S(2)}) async-start(f32[16,18,8,128]{3,2,1,0:T(8,128)} %x_modes.1), calls=%async_computation.1 | async-start | bytes 2359296 | tf_op jit(solution)/shard_map/all_to_all | solution.py:265
  64.8 0.8 copy-start.14
  66.9 1.0 copy-start.7
  95.3 1.2 copy-start.8
  96.5 1.0 copy-start.15
  97.6 1.0 copy-start.18
  98.6 0.9 copy-start.19
  99.5 0.8 copy-start.21
  100.3 23.5 %copy-start.9 = (f32[2,256,128]{2,1,0:T(8,128)S(1)}, f32[2,256,128]{2,1,0:T(8,128)}, u32[]{:S(2)}) copy-start(f32[2,256,128]{2,1,0:T(8,128)} %constant.37.clone.table) | copy-start | bytes 786436
  103.0 20.8 %copy-start.22 = (f32[2,128,128]{2,1,0:T(8,128)}, f32[2,128,128]{2,1,0:T(8,128)S(1)}, u32[]{:S(2)}) copy-start(f32[2,128,128]{2,1,0:T(8,128)S(1)} %get-tuple-element.21.g_hat) | copy-start | bytes 393220
  123.8 5.3 %copy-start.16 = (bf16[128,2048]{1,0:T(8,128)(2,1)S(1)}, bf16[128,2048]{1,0:T(8,128)(2,1)}, u32[]{:S(2)}) copy-start(bf16[128,2048]{1,0:T(8,128)(2,1)} %constant.33.clone.by_out) | copy-start | bytes 1572868
  123.9 5.3 %copy-start.17 = (bf16[128,2048]{1,0:T(8,128)(2,1)S(1)}, bf16[128,2048]{1,0:T(8,128)(2,1)}, u32[]{:S(2)}) copy-start(bf16[128,2048]{1,0:T(8,128)(2,1)} %constant.32.clone.by_in) | copy-start | bytes 1572868
  125.4 23.3 %all-to-all-start.3 = ((f32[16,18,8,128]{3,2,1,0:T(8,128)}), f32[16,18,8,128]{3,2,1,0:T(8,128)S(1)}, u32[]{:S(2)}, u32[]{:S(2)}) async-start(f32[16,18,8,128]{3,2,1,0:T(8,128)} %x_cells.1), calls=%async_computation.3 | async-start | bytes 2359296 | tf_op jit(solution)/shard_map/all_to_all | solution.py:265
  129.2 19.6 %copy-start.12 = (f32[128,256]{1,0:T(8,128)S(1)}, f32[128,256]{1,0:T(8,128)}, u32[]{:S(2)}) copy-start(f32[128,256]{1,0:T(8,128)} %constant.38.clone.table) | copy-start | bytes 393220
  129.2 0.9 copy-start.20
  130.1 0.9 copy-start.23
  148.7 1.6 %copy-start.2 = (f32[64,4,16,128]{3,2,1,0:T(8,128)S(1)}, f32[64,4,16,128]{3,2,1,0:T(8,128)}, u32[]{:S(2)}) copy-start(f32[64,4,16,128]{3,2,1,0:T(8,128)} %copy-done.1) | copy-start | bytes 6291460

commit v2 on v1

v2 whole, which is shorter than its diff:
```python
import math

import jax
import jax.numpy as jnp
import numpy as np
from jax import lax
from jax.experimental import pallas as pl
from jax.experimental.pallas import tpu as pltpu
from jax.sharding import Mesh
from jax.sharding import PartitionSpec as P

HIGH = lax.Precision.HIGH
F32 = jnp.float32
BF16 = jnp.bfloat16
CELLS = 4194304.0
UNIT = 1.0 / math.sqrt(128.0 * 128.0 * 128.0)
PLANE = ("yp", "xp")
COLUMN = ("zh", "zl", "co")


def mm(left, right, left_dim=1, right_dim=0, precision=HIGH):
    dims = (((left_dim,), (right_dim,)), ((), ()))
    return lax.dot_general(left, right, dims, precision=precision, preferred_element_type=F32)


def halves(values):
    top = values.astype(BF16)
    return top, (values - top.astype(F32)).astype(BF16)


def mm_exact(values, pattern):
    top, rest = halves(values)
    return mm(top, pattern, precision=None) + mm(rest, pattern, precision=None)


def sine(turns):
    angle = ((turns + 64) & 127) - 64
    angle = jnp.where(angle > 32, 64 - angle, jnp.where(angle < -32, -64 - angle, angle))
    x = angle.astype(F32) * (2.0 * math.pi / 128.0)
    square = x * x
    total = jnp.full_like(x, 1.0 / math.factorial(13))
    for power in (11, 9, 7, 5, 3, 1):
        total = total * square + (-1.0) ** (power // 2) / math.factorial(power)
    return total * x


def grid_of(rows, columns):
    shape = (rows, columns)
    return lax.broadcasted_iota(jnp.int32, shape, 0), lax.broadcasted_iota(jnp.int32, shape, 1)


def z_table(scale):
    row, column = grid_of(128, 256)
    kz = 8 * (row >> 5) + ((row >> 3) & 3) + 4 * (row & 1)
    values = sine(kz * (column & 127) + 32 + 32 * ((row >> 1) & 1))
    return jnp.where(((row >> 2) & 1) == (column >> 7), values * scale, 0.0)


def x_table(zh):
    row, column = grid_of(128, 256)
    cell = 32 * (column >> 6) + 16 * zh + ((column >> 2) & 15)
    quarter = 32 - 32 * (((column >> 1) & 1) - (row & 1))
    values = sine((((row >> 1) & 31) - 16) * cell + quarter)
    return jnp.where((row >> 6) == (column & 1), values, 0.0)


def x_back_table(zh):
    row, column = grid_of(256, 128)
    cell = 32 * (row >> 6) + 16 * zh + ((row >> 2) & 15)
    quarter = 32 + 32 * ((column & 1) - ((row >> 1) & 1))
    values = sine((((column >> 1) & 31) - 16) * cell + quarter)
    return jnp.where((row & 1) == (column >> 6), values, 0.0)


def y_table():
    row, column = grid_of(128, 256)
    cell = 2 * (column & 63) + (row >> 6)
    quarter = 32 - 32 * ((column >> 7) - ((row >> 5) & 1))
    return sine(((row & 31) - 16) * cell + quarter) * UNIT


def y_back_table():
    row, column = grid_of(128, 128)
    cell = 2 * (row & 63) + (column >> 6)
    quarter = 32 + 32 * (((column >> 5) & 1) - (row >> 6))
    return sine(((column & 31) - 16) * cell + quarter)


def pattern(keep):
    return jnp.where(keep, 1.0, 0.0).astype(BF16)


def front_kernel(layer, pre, out_grad, grad, message, table):
    @pl.when(pl.program_id(0) + pl.program_id(1) == 0)
    def _():
        table[...] = z_table(1.0)

    layer, pre, out_grad, grad2 = (ref.reshape(1024, 128) for ref in (layer, pre, out_grad, grad))

    def slope(i, carry):
        rows = pl.ds(pl.multiple_of(i * 64, 64), 64)
        v = pre[rows, :]
        cdf = 0.5 * (1.0 + lax.erf(v * (1.0 / math.sqrt(2.0))))
        bump = v * jnp.exp(-0.5 * v * v) * (1.0 / math.sqrt(2.0 * math.pi))
        grad2[rows, :] = out_grad[rows, :] * (cdf + bump)
        return carry

    lax.fori_loop(0, 16, slope, 0)
    for field, values in ((0, layer), (1, grad2)):
        for j in range(0, 4, 2):
            cells = jnp.concatenate(
                [
                    jnp.concatenate(
                        [values[pl.ds(x * 8 + 2 * j + y, 64, stride=16), :] for y in range(4)], 0
                    )
                    for x in range(2)
                ],
                1,
            )
            spectrum = mm(table[...], cells, 1, 1)
            for k in range(2):
                part = spectrum[:, 128 * k : 128 * k + 128].reshape(16, 8, 128)
                message[:, field, 0, 8 * (j + k) : 8 * (j + k) + 8, :] = part


def local_kernel(point, layer, grad, base, sums, products):
    layer, grad, base = (ref.reshape(1024, 128) for ref in (layer, grad, base))
    step = pl.program_id(0) * 2 + pl.program_id(1)

    @pl.when(step == 0)
    def _():
        products[...] = jnp.zeros_like(products)

    for cell in range(0, 16, 2):
        u = jnp.concatenate([layer[pl.ds(cell + k, 64, stride=16), :] for k in range(2)], 1)
        g = jnp.concatenate([grad[pl.ds(cell + k, 64, stride=16), :] for k in range(2)], 1)
        products[...] += mm(u, g, 1, 1)
        mixed = mm(point[...], g)
        for k in range(2):
            base[pl.ds(cell + k, 64, stride=16), :] = mixed[:, 128 * k : 128 * k + 128]

    @pl.when(step == 3)
    def _():
        by_pair = products[0:32, 0:32] + products[32:64, 32:64]
        for k in range(4):
            sums[:, 32 * k : 32 * k + 32] = by_pair[8 * k : 8 * k + 8, :]


def weight_kernel(spread, codes, scales, noise, weight):
    step = jnp.exp2(scales[...].astype(F32) * -0.25) * (1.0 / (16.0 * math.sqrt(32.0)))
    top, rest = halves(step)
    last = (step - top.astype(F32) - rest.astype(F32)).astype(BF16)
    wide = sum(mm(part, spread[...], precision=None) for part in (last, rest, top))
    weight[...] = codes[...].astype(F32) * wide * (1.0 + noise[...])


def x_kernel(place, arrived, sums, message):
    message[:, 16] = jnp.broadcast_to(sums[...][None], (16, 8, 128))
    table = x_table(place[0])
    for field in range(2):
        for j in range(0, 8, 2):
            cells = jnp.concatenate(
                [
                    arrived[:, field, :, 8 * k : 8 * k + 8, :].reshape(256, 128)
                    for k in (j, j + 1)
                ],
                1,
            )
            modes = mm(table, cells)
            for k in range(2):
                part = modes[:, 128 * k : 128 * k + 128].reshape(16, 8, 128)
                message[:, 8 * field + j + k] = part


def along_y(arrived, field):
    rows = arrived.reshape(2176, 128)
    cells = [
        jnp.concatenate(
            [
                rows[pl.ds(136 * peer + 64 * field + 2 * kx + r, 8, stride=8), :]
                for r in range(2)
                for peer in range(16)
            ],
            0,
        )
        for kx in range(4)
    ]
    modes = mm(y_table(), jnp.concatenate(cells, 1))
    modes = [modes[:, 128 * kx : 128 * kx + 128] for kx in range(4)]
    modes = [part[:64] + pltpu.roll(part[64:], 64, 1) for part in modes]
    real, imag = ([part[32 * r : 32 * r + 32] for part in modes] for r in range(2))
    return jnp.concatenate(real, 0), jnp.concatenate(imag, 0)


def mode_kernel(place, weight, arrived, g_hat, message, sums):
    sums[...] = jnp.sum(arrived[:, 16], axis=0)
    g_real, g_imag = along_y(arrived, 1)
    g_hat[0] = g_real
    g_hat[1] = g_imag
    row, column = grid_of(128, 128)
    row_long, column_long = grid_of(1024, 128)
    gather = pattern((row_long >> 5) == column_long)
    q_real = q_imag = None
    for b in range(2):
        wide = pattern(row == (column & 31) + 32 * b)
        wide_real, wide_imag = mm_exact(g_real, wide), mm_exact(g_imag, wide)
        real = imag = 0.0
        for part in range(4):
            lanes = slice(256 * part, 256 * part + 256)
            w_real = weight[:, 256 * part : 256 * part + 256]
            w_imag = weight[:, 1024 + 256 * part : 1280 + 256 * part]
            gr = jnp.concatenate([wide_real, wide_real], 1)
            gi = jnp.concatenate([wide_imag, wide_imag], 1)
            real += mm_exact(w_real * gr + w_imag * gi, gather[lanes])
            imag += mm_exact(w_real * gi - w_imag * gr, gather[lanes])
        if b == 0:
            q_real, q_imag = real, imag
        else:
            q_real, q_imag = q_real + pltpu.roll(real, 32, 1), q_imag + pltpu.roll(imag, 32, 1)
    rows = message.reshape(1024, 128)
    modes = [
        jnp.concatenate([q_real[32 * kx : 32 * kx + 32], q_imag[32 * kx : 32 * kx + 32]], 0)
        for kx in range(4)
    ]
    modes = [jnp.concatenate([part, pltpu.roll(part, 64, 1)], 0) for part in modes]
    cells = mm(y_back_table(), jnp.concatenate(modes, 1))
    for kx in range(4):
        for r in range(2):
            for zh in range(2):
                part = cells[64 * r : 64 * r + 64, 128 * kx : 128 * kx + 128]
                rows[pl.ds(512 * zh + 2 * kx + r, 64, stride=8), :] = part

    @pl.when(place[2] == 1)
    def _():
        bias = g_real[16:17] + pltpu.roll(g_real[16:17], 96, 1)
        rows[pl.ds(1, 16, stride=64), :] = jnp.broadcast_to(bias * (1.0 / (UNIT * CELLS)), (16, 128))


def outer_kernel(arrived, g_hat, result):
    u_real, u_imag = along_y(arrived, 0)
    row, column = grid_of(128, 128)
    u, g = [], []
    for b in range(2):
        wide = pattern(row == (column & 31) + 32 * b)
        u.append([pltpu.roll(v, 96, 1) if b else v for v in (u_real, u_imag)])
        g.append([mm_exact(g_hat[r], wide) for r in range(2)])
    g = [[jnp.concatenate([v, v], 1) for v in pair] for pair in g]
    row, column = grid_of(128, 256)
    for part in range(4):
        wide = pattern(row == (column >> 5) + 8 * part)
        real = imag = 0.0
        for b in range(2):
            ur, ui = (mm_exact(v, wide) for v in u[b])
            gr, gi = g[b]
            real += ur * gr + ui * gi
            imag += ur * gi - ui * gr
        result[:, 256 * part : 256 * part + 256] = real
        result[:, 1024 + 256 * part : 1280 + 256 * part] = imag


def x_back_kernel(place, arrived, sums, message):
    message[:, 16] = jnp.broadcast_to(sums[...][None], (16, 8, 128))
    table = x_back_table(place[0])
    for j in range(0, 8, 2):
        cells = jnp.concatenate([arrived[:, k].reshape(128, 128) for k in (j, j + 1)], 1)
        cells = mm(table, cells)
        for k in range(2):
            part = cells[:, 128 * k : 128 * k + 128].reshape(16, 2, 8, 128)
            message[:, j + k] = part[:, 0]
            message[:, 8 + j + k] = part[:, 1]

    @pl.when(place[1] == 1)
    def _():
        message[:, 0, 2:3] = jnp.broadcast_to(arrived[4, 0, 1:2][None], (16, 1, 128))


def end_kernel(arrived, sums, base, result, grad_point, grad_bias, table):
    base, result = base.reshape(1024, 128), result.reshape(1024, 128)

    @pl.when(pl.program_id(0) + pl.program_id(1) == 0)
    def _():
        table[...] = z_table(UNIT)
        total = jnp.sum(sums[:, 0], axis=0) * (1.0 / CELLS)
        for k in range(4):
            grad_point[8 * k : 8 * k + 8, :] = total[:, 32 * k : 32 * k + 32]
        grad_bias[...] = arrived[0, 0, 2:3, 0:32]

    for j in range(4):
        cells = mm(arrived[:, j].reshape(128, 128), table[...], 0, 0)
        for x in range(2):
            for odd in range(2):
                rows = pl.ds(x * 8 + 2 * j + odd, 64, stride=16)
                result[rows, :] = (
                    base[rows, :] + cells[64 * odd : 64 * odd + 64, 128 * x : 128 * x + 128]
                )


def params(steps=0, mebibytes=20):
    return pltpu.CompilerParams(
        dimension_semantics=("arbitrary",) * steps if steps else None,
        vmem_limit_bytes=mebibytes << 20,
    )


def cost(flops, moved):
    return pl.CostEstimate(flops=flops, bytes_accessed=moved, transcendentals=0)


def whole(*shape):
    return pl.BlockSpec(shape, lambda *_: (0,) * len(shape))


def shaped(*shape):
    return jax.ShapeDtypeStruct(shape, F32)


def exchange(message, axes):
    return lax.all_to_all(message, axes, split_axis=0, concat_axis=0, tiled=True)


def per_device(
    layer_input, pre_act, out_grad, weight_codes, scale_codes, weight_noise, point_weight
):
    layer, pre, slope_in = (v.reshape(64, 4, 16, 128) for v in (layer_input, pre_act, out_grad))
    plane_first = (lax.axis_index("yp") + lax.axis_index("xp") == 0).astype(jnp.int32)
    owner = plane_first * (lax.axis_index(COLUMN) == 4).astype(jnp.int32)
    place = jnp.stack([lax.axis_index("zh"), plane_first, owner]).astype(jnp.int32)
    mega = 1 << 20
    field = pl.BlockSpec((64, 2, 8, 128), lambda p, h: (0, p, h, 0))
    grad, message = pl.pallas_call(
        front_kernel,
        grid=(2, 2),
        in_specs=[field, field, field],
        out_specs=[field, pl.BlockSpec((16, 2, 1, 32, 128), lambda p, h: (0, 0, p, h, 0))],
        out_shape=[shaped(64, 4, 16, 128), shaped(16, 2, 2, 64, 128)],
        scratch_shapes=[pltpu.VMEM((128, 256), F32)],
        compiler_params=params(2, 60),
        cost_estimate=cost(1 << 30, 10 * mega),
        name="front",
    )(layer, pre, slope_in)
    arrived = exchange(message, PLANE)

    blocks = np.kron(np.eye(2, dtype=np.float32), np.ones((32, 32), np.float32))
    both = jnp.tile(point_weight, (2, 2)) * blocks
    base, sums = pl.pallas_call(
        local_kernel,
        grid=(2, 2),
        in_specs=[whole(64, 64), field, field],
        out_specs=[field, whole(8, 128)],
        out_shape=[shaped(64, 4, 16, 128), shaped(8, 128)],
        scratch_shapes=[pltpu.VMEM((64, 64), F32)],
        compiler_params=params(2),
        cost_estimate=cost(1 << 30, 6 * mega),
        name="local",
    )(both, layer, grad)

    spread = np.kron(np.eye(64, dtype=np.float32), np.ones((1, 32), np.float32))
    column = pl.BlockSpec((128, 512), lambda i: (0, i))
    codes, _ = lax.optimization_barrier((weight_codes, sums))
    weight = pl.pallas_call(
        weight_kernel,
        grid=(4,),
        in_specs=[pl.BlockSpec((64, 512), lambda i: (0, i)), column, whole(128, 64), column],
        out_specs=column,
        out_shape=shaped(128, 2048),
        compiler_params=params(1),
        cost_estimate=cost(1 << 27, 3 * mega),
        name="weight",
    )(
        jnp.asarray(spread, BF16),
        codes.reshape(128, 2048),
        scale_codes.reshape(128, 64),
        weight_noise.reshape(128, 2048),
    )

    def placed(in_specs, out_specs):
        return pltpu.PrefetchScalarGridSpec(
            num_scalar_prefetch=1, grid=(1,), in_specs=in_specs, out_specs=out_specs
        )

    message = pl.pallas_call(
        x_kernel,
        grid_spec=placed([whole(16, 2, 2, 64, 128), whole(8, 128)], whole(16, 17, 8, 128)),
        out_shape=shaped(16, 17, 8, 128),
        compiler_params=params(1),
        cost_estimate=cost(1 << 29, 3 * mega),
        name="x_modes",
    )(place, arrived, sums)
    arrived = exchange(message, COLUMN)

    g_hat, message, sums = pl.pallas_call(
        mode_kernel,
        grid_spec=placed(
            [whole(128, 2048), whole(16, 17, 8, 128)],
            [whole(2, 128, 128), whole(16, 8, 8, 128), whole(8, 128)],
        ),
        out_shape=[shaped(2, 128, 128), shaped(16, 8, 8, 128), shaped(8, 128)],
        compiler_params=params(1),
        cost_estimate=cost(1 << 30, 3 * mega),
        name="modes",
    )(place, weight, arrived)
    returned = exchange(message, COLUMN)

    grad_spectral = pl.pallas_call(
        outer_kernel,
        grid=(1,),
        in_specs=[whole(16, 17, 8, 128), whole(2, 128, 128)],
        out_specs=whole(128, 2048),
        out_shape=shaped(128, 2048),
        compiler_params=params(1),
        cost_estimate=cost(1 << 30, 4 * mega),
        name="outer",
    )(arrived, g_hat)

    message = pl.pallas_call(
        x_back_kernel,
        grid_spec=placed([whole(16, 8, 8, 128), whole(8, 128)], whole(16, 17, 8, 128)),
        out_shape=shaped(16, 17, 8, 128),
        compiler_params=params(1),
        cost_estimate=cost(1 << 29, 2 * mega),
        name="x_cells",
    )(place, returned, sums)
    returned = exchange(message, PLANE)

    grad_input, grad_point, grad_bias = pl.pallas_call(
        end_kernel,
        grid=(2, 2),
        in_specs=[
            pl.BlockSpec((16, 4, 8, 128), lambda p, h: (0, 2 * p + h, 0, 0)),
            pl.BlockSpec((16, 1, 8, 128), lambda p, h: (0, 16, 0, 0)),
            field,
        ],
        out_specs=[field, whole(32, 32), whole(1, 32)],
        out_shape=[shaped(64, 4, 16, 128), shaped(32, 32), shaped(1, 32)],
        scratch_shapes=[pltpu.VMEM((128, 256), F32)],
        compiler_params=params(2, 60),
        cost_estimate=cost(1 << 29, 5 * mega),
        name="end",
    )(returned, returned, base)
    return (
        grad_input.reshape(layer_input.shape),
        grad_spectral.reshape(weight_codes.shape),
        grad_point,
        grad_bias.reshape(32),
    )


def solution(mesh):
    fine = Mesh(mesh.devices.reshape(4, 2, 4, 4, 2), ("yp", "zh", "xp", "zl", "co"))
    slab, pencil = ("yp", "zh", "xp"), ("zl", "co")
    field, modes = P(None, None, slab, pencil, None), P(slab, pencil, None, None)
    return jax.shard_map(
        per_device,
        mesh=fine,
        in_specs=(field, field, field, modes, modes, modes, P()),
        out_specs=(field, modes, P(), P()),
        check_vma=False,
    )
```

time: 155 us -> 147 us (0.948)
  local copies, waits for them, and re-layouts: 16.2 us -> 6.24 us
  Pallas kernels: 27.3 us -> 29.3 us
    unnamed x52 -> x24, local copies, waits for them, and re-layouts: 16.1 us -> 6.14 us
    pallas_call x6, Pallas kernels: 21.2 us -> 24.5 us  [the longest x1 8.01 us: per_device(): pl.pallas_call(front_kernel, grid=(2, 2), in_specs=[field, field, field],...]
  transfers between devices with their start and end apart: 3 -> 3, of which waited for: 3 -> 3; matrix products, arithmetic and copies ran while one was open for 0% -> 0% of each run, Pallas kernels for 6% -> 5%
where the time goes in v2:
time: 147 us; the launch traced here: 146 us
  waiting for transfers between devices  67.2 us (46%)
  Pallas kernels  29.3 us (20%)
  starting transfers between devices  22.1 us (15%)
  blocking collectives  20.7 us (14%)
  local copies, waits for them, and re-layouts  6.24 us (4%)
    all_to_all x3, waiting for transfers between devices, exchange(): lax.all_to_all(message, axes, split_axis=0, concat_axis=0, tiled=True)  67.2 us
    all_to_all x3, starting transfers between devices, exchange(): lax.all_to_all(message, axes, split_axis=0, concat_axis=0, tiled=True)  22.1 us
    all_to_all x1, blocking collectives, exchange(): lax.all_to_all(message, axes, split_axis=0, concat_axis=0, tiled=True)  20.7 us
    pallas_call x1, Pallas kernels, per_device(): pl.pallas_call(front_kernel, grid=(2, 2), in_specs=[field, field, field],...  8.01 us
    unnamed x24, local copies, waits for them, and re-layouts  6.14 us
    pallas_call x1, Pallas kernels, per_device(): pl.pallas_call(end_kernel, grid=(2, 2), in_specs=[pl.BlockSpec((16, 4, 8,...  5.26 us
    pallas_call x1, Pallas kernels, per_device(): pl.pallas_call(x_kernel, grid_spec=placed([whole(16, 2, 2, 64, 128), whol...  4.1 us
    pallas_call x1, Pallas kernels, per_device(): pl.pallas_call(local_kernel, grid=(2, 2), in_specs=[whole(64, 64), field,...  3.48 us
  transfers between devices with their start and end apart: 3, of which 3 were waited for; matrix products, arithmetic and copies ran while one was open for 0% of the time, Pallas kernels for 5%

profile of v2, /device:TPU:1, one launch (start us, length us, event | category | flops | bytes accessed | tf_op | source)
XLA Modules:
  0.0 146.3 jit_solution(13645155269713118624)
XLA Ops:
  0.6 8.0 %front.1 = (f32[64,4,16,128]{3,2,1,0:T(8,128)}, f32[16,2,2,64,128]{4,3,2,1,0:T(8,128)}) custom-call(f32[64,4,16,128]{3,2,1,0:T(8,128)} %bitcast.12, f32[64,4,16,128]{3,2,1,0:T(8,128)} %bitcast.17, f32[64,4,16,128]{3,2,1,0:T(8,128)} %bitcast.18), custom_call_target="tpu_custom_call" | custom-call | flops 1073741824 | bytes 10485760 | tf_op jit(solution)/shard_map/front/pallas_call | solution.py:330
  8.6 0.0 copy-start.10
  8.6 0.0 copy-start.11
  8.6 0.0 copy-start
  8.7 7.8 %all-to-all-start = ((f32[16,2,2,64,128]{4,3,2,1,0:T(8,128)}), f32[16,2,2,64,128]{4,3,2,1,0:T(8,128)}, u32[]{:S(2)}, u32[]{:S(2)}) async-start(f32[16,2,2,64,128]{4,3,2,1,0:T(8,128)} %get-tuple-element.18), calls=%async_computation | async-start | bytes 4194304 | tf_op jit(solution)/shard_map/all_to_all | solution.py:318
  16.5 0.0 copy-done.10
  16.5 0.0 copy-done.11
  16.5 0.1 reshape.46.point
  16.6 0.0 copy-done
  16.6 0.0 copy-start.1
  16.6 1.6 %copy-done.1 = f32[64,4,16,128]{3,2,1,0:T(8,128)S(1)} copy-done((f32[64,4,16,128]{3,2,1,0:T(8,128)S(1)}, f32[64,4,16,128]{3,2,1,0:T(8,128)}, u32[]{:S(2)}) %copy-start.1) | copy-done | bytes 2097176
  18.2 3.5 %local.1 = (f32[64,4,16,128]{3,2,1,0:T(8,128)S(1)}, f32[8,128]{1,0:T(8,128)S(1)}) custom-call(f32[64,64]{1,0:T(8,128)S(1)} %reshape.46.point, f32[64,4,16,128]{3,2,1,0:T(8,128)S(1)} %bitcast.13, f32[64,4,16,128]{3,2,1,0:T(8,128)S(1)} %copy-done.1), custom_call_target="tpu_custom_call" | custom-call | flops 1073741824 | bytes 6291456 | tf_op jit(solution)/shard_map/local/pallas_call | solution.py:345
  21.7 0.0 copy-start.2
  21.7 1.3 copy-done.2
  23.0 0.1 pad_add_fusion.place
  23.1 23.9 %all-to-all-done.arrived = f32[16,2,2,64,128]{4,3,2,1,0:T(8,128)} async-done(((f32[16,2,2,64,128]{4,3,2,1,0:T(8,128)}), f32[16,2,2,64,128]{4,3,2,1,0:T(8,128)}, u32[]{:S(2)}, u32[]{:S(2)}) %all-to-all-start) | async-done | bytes 2097184 | tf_op jit(solution)/shard_map/all_to_all | solution.py:318
  47.0 0.0 copy-start.3
  47.0 0.0 copy-start.4
  47.0 0.0 copy-start.7
  47.0 0.0 copy-start.8
  47.0 4.1 %x_modes.1 = f32[16,17,8,128]{3,2,1,0:T(8,128)} custom-call(s32[3]{0:T(128)S(1)} %pad_add_fusion.place, f32[16,2,2,64,128]{4,3,2,1,0:T(8,128)} %all-to-all-done.arrived, f32[8,128]{1,0:T(8,128)S(1)} %get-tuple-element.16.sums), custom_call_target="tpu_custom_call" | custom-call | flops 536870912 | bytes 3145728 | tf_op jit(solution)/shard_map/x_modes/pallas_call | solution.py:381
  51.1 10.6 %all-to-all-start.1 = ((f32[16,17,8,128]{3,2,1,0:T(8,128)}), f32[16,17,8,128]{3,2,1,0:T(8,128)S(1)}, u32[]{:S(2)}, u32[]{:S(2)}) async-start(f32[16,17,8,128]{3,2,1,0:T(8,128)} %x_modes.1), calls=%async_computation.1 | async-start | bytes 2228224 | tf_op jit(solution)/shard_map/all_to_all | solution.py:318
  61.7 0.0 copy-done.3
  61.7 0.0 copy-done.4
  61.7 0.0 copy-done.7
  61.7 0.0 copy-done.8
  61.7 1.3 weight.1
  63.1 0.0 copy-start.5
  63.1 1.0 copy-done.5
  64.0 26.9 %all-to-all-done.1.arrived = f32[16,17,8,128]{3,2,1,0:T(8,128)S(1)} async-done(((f32[16,17,8,128]{3,2,1,0:T(8,128)}), f32[16,17,8,128]{3,2,1,0:T(8,128)S(1)}, u32[]{:S(2)}, u32[]{:S(2)}) %all-to-all-start.1) | async-done | bytes 1114144 | tf_op jit(solution)/shard_map/all_to_all | solution.py:318
  91.0 0.0 copy-start.6
  91.0 1.2 copy-done.6
  92.2 2.6 %modes.1 = (f32[2,128,128]{2,1,0:T(8,128)S(1)}, f32[16,8,8,128]{3,2,1,0:T(8,128)S(1)}, f32[8,128]{1,0:T(8,128)S(1)}) custom-call(s32[3]{0:T(128)S(1)} %pad_add_fusion.place, f32[128,2048]{1,0:T(8,128)S(1)} %copy-done.6, f32[16,17,8,128]{3,2,1,0:T(8,128)S(1)} %all-to-all-done.1.arrived), custom_call_target="tpu_custom_call" | custom-call | flops 1073741824 | bytes 3145728 | tf_op jit(solution)/shard_map/modes/pallas_call | solution.py:391
  94.8 20.7 %all_to_all.20.arrived = f32[16,8,8,128]{3,2,1,0:T(8,128)S(1)} all-to-all(f32[16,8,8,128]{3,2,1,0:T(8,128)S(1)} %get-tuple-element.19), channel_id=1, replica_groups=mesh['yp'=4,'zh'=2,'xp'=4,'zl'=4,'co'=2] {'zh','zl','co'}, dimensions={0} | all-to-all | bytes 1048576 | tf_op jit(solution)/shard_map/all_to_all | solution.py:318
  115.5 2.3 %x_cells.1 = f32[16,17,8,128]{3,2,1,0:T(8,128)} custom-call(s32[3]{0:T(128)S(1)} %pad_add_fusion.place, f32[16,8,8,128]{3,2,1,0:T(8,128)S(1)} %all_to_all.20.arrived, f32[8,128]{1,0:T(8,128)S(1)} %get-tuple-element.20.sums), custom_call_target="tpu_custom_call" | custom-call | flops 536870912 | bytes 2097152 | tf_op jit(solution)/shard_map/x_cells/pallas_call | solution.py:415
  117.8 3.7 %all-to-all-start.3 = ((f32[16,17,8,128]{3,2,1,0:T(8,128)}), f32[16,17,8,128]{3,2,1,0:T(8,128)S(1)}, u32[]{:S(2)}, u32[]{:S(2)}) async-start(f32[16,17,8,128]{3,2,1,0:T(8,128)} %x_cells.1), calls=%async_computation.3 | async-start | bytes 2228224 | tf_op jit(solution)/shard_map/all_to_all | solution.py:318
  121.5 2.3 %outer.1 = f32[128,2048]{1,0:T(8,128)} custom-call(f32[16,17,8,128]{3,2,1,0:T(8,128)S(1)} %all-to-all-done.1.arrived, f32[2,128,128]{2,1,0:T(8,128)S(1)} %get-tuple-element.23.g_hat), custom_call_target="tpu_custom_call" | custom-call | flops 1073741824 | bytes 4194304 | tf_op jit(solution)/shard_map/outer/pallas_call | solution.py:404
  123.7 16.4 %all-to-all-done.3.arrived.sums = f32[16,17,8,128]{3,2,1,0:T(8,128)S(1)} async-done(((f32[16,17,8,128]{3,2,1,0:T(8,128)}), f32[16,17,8,128]{3,2,1,0:T(8,128)S(1)}, u32[]{:S(2)}, u32[]{:S(2)}) %all-to-all-start.3) | async-done | bytes 1114144 | tf_op jit(solution)/shard_map/all_to_all | solution.py:318
  140.1 0.0 copy-start.9
  140.1 1.0 copy-done.9
  141.1 5.3 %end.1 = (f32[64,4,16,128]{3,2,1,0:T(8,128)}, f32[32,32]{1,0:T(8,128)}, f32[1,32]{1,0:T(1,128)}) custom-call(f32[16,17,8,128]{3,2,1,0:T(8,128)} %copy-done.9, f32[16,17,8,128]{3,2,1,0:T(8,128)} %copy-done.9, f32[64,4,16,128]{3,2,1,0:T(8,128)} %copy-done.2), custom_call_target="tpu_custom_call" | custom-call | flops 536870912 | bytes 5242880 | tf_op jit(solution)/shard_map/end/pallas_call | solution.py:425
  (1 shorter events, 0.0 us)
Async XLA Ops:
  8.6 7.8 %copy-start.10 = (f32[2,32,2,32]{3,2,1,0:T(2,128)S(1)}, f32[2,32,2,32]{3,2,1,0:T(2,128)}, u32[]{:S(2)}) copy-start(f32[2,32,2,32]{3,2,1,0:T(2,128)} %constant.40) | copy-start | bytes 49156
  8.6 7.8 %copy-start.11 = (f32[32,32]{1,0:T(8,128)S(1)}, f32[32,32]{1,0:T(8,128)}, u32[]{:S(2)}) copy-start(f32[32,32]{1,0:T(8,128)} %param.15) | copy-start | bytes 12292
  8.6 8.0 %copy-start = (f32[2,32,4,16,128]{4,3,2,1,0:T(8,128)S(1)}, f32[2,32,4,16,128]{4,3,2,1,0:T(8,128)}, u32[]{:S(2)}) copy-start(f32[2,32,4,16,128]{4,3,2,1,0:T(8,128)} %param.9) | copy-start | bytes 6291460
  8.7 38.3 %all-to-all-start = ((f32[16,2,2,64,128]{4,3,2,1,0:T(8,128)}), f32[16,2,2,64,128]{4,3,2,1,0:T(8,128)}, u32[]{:S(2)}, u32[]{:S(2)}) async-start(f32[16,2,2,64,128]{4,3,2,1,0:T(8,128)} %get-tuple-element.18), calls=%async_computation | async-start | bytes 4194304 | tf_op jit(solution)/shard_map/all_to_all | solution.py:318
  16.6 1.6 %copy-start.1 = (f32[64,4,16,128]{3,2,1,0:T(8,128)S(1)}, f32[64,4,16,128]{3,2,1,0:T(8,128)}, u32[]{:S(2)}) copy-start(f32[64,4,16,128]{3,2,1,0:T(8,128)} %get-tuple-element.15.grad) | copy-start | bytes 6291460
  21.7 1.3 copy-start.2
  47.0 14.7 %copy-start.3 = (s32[1,4,32,2048]{3,2,1,0:T(8,128)S(1)}, s32[1,4,32,2048]{3,2,1,0:T(8,128)}, u32[]{:S(2)}) copy-start(s32[1,4,32,2048]{3,2,1,0:T(8,128)} %param.12) | copy-start | bytes 3145732
  47.0 14.7 %copy-start.4 = (f32[1,4,32,2048]{3,2,1,0:T(8,128)S(1)}, f32[1,4,32,2048]{3,2,1,0:T(8,128)}, u32[]{:S(2)}) copy-start(f32[1,4,32,2048]{3,2,1,0:T(8,128)} %param.14) | copy-start | bytes 3145732
  47.0 14.7 %copy-start.7 = (bf16[64,2048]{1,0:T(8,128)(2,1)S(1)}, bf16[64,2048]{1,0:T(8,128)(2,1)}, u32[]{:S(2)}) copy-start(bf16[64,2048]{1,0:T(8,128)(2,1)} %constant.33.clone.spread) | copy-start | bytes 786436
  47.0 14.7 %copy-start.8 = (s32[1,4,32,64]{3,2,1,0:T(8,128)S(1)}, s32[1,4,32,64]{3,2,1,0:T(8,128)}, u32[]{:S(2)}) copy-start(s32[1,4,32,64]{3,2,1,0:T(8,128)} %param.13) | copy-start | bytes 98308
  51.1 39.8 %all-to-all-start.1 = ((f32[16,17,8,128]{3,2,1,0:T(8,128)}), f32[16,17,8,128]{3,2,1,0:T(8,128)S(1)}, u32[]{:S(2)}, u32[]{:S(2)}) async-start(f32[16,17,8,128]{3,2,1,0:T(8,128)} %x_modes.1), calls=%async_computation.1 | async-start | bytes 2228224 | tf_op jit(solution)/shard_map/all_to_all | solution.py:318
  63.1 1.0 copy-start.5
  91.0 1.2 copy-start.6
  117.8 22.3 %all-to-all-start.3 = ((f32[16,17,8,128]{3,2,1,0:T(8,128)}), f32[16,17,8,128]{3,2,1,0:T(8,128)S(1)}, u32[]{:S(2)}, u32[]{:S(2)}) async-start(f32[16,17,8,128]{3,2,1,0:T(8,128)} %x_cells.1), calls=%async_computation.3 | async-start | bytes 2228224 | tf_op jit(solution)/shard_map/all_to_all | solution.py:318
  140.1 1.0 copy-start.9

commit v3 on v2

--- a/solution.py
+++ b/solution.py
@@ -72,9 +72,9 @@
     return jnp.where((row & 1) == (column >> 6), values, 0.0)
 
 
-def y_table():
+def y_table(pencil_of):
     row, column = grid_of(128, 256)
-    cell = 2 * (column & 63) + (row >> 6)
+    cell = 16 * pencil_of((column >> 3) & 15) + 2 * (column & 7) + (row >> 6)
     quarter = 32 - 32 * ((column >> 7) - ((row >> 5) & 1))
     return sine(((row & 31) - 16) * cell + quarter) * UNIT
 
@@ -90,22 +90,25 @@
     return jnp.where(keep, 1.0, 0.0).astype(BF16)
 
 
-def front_kernel(layer, pre, out_grad, grad, message, table):
-    @pl.when(pl.program_id(0) + pl.program_id(1) == 0)
-    def _():
-        table[...] = z_table(1.0)
-
-    layer, pre, out_grad, grad2 = (ref.reshape(1024, 128) for ref in (layer, pre, out_grad, grad))
-
-    def slope(i, carry):
+def make_grad(pre, out_grad, grad):
+    def some(i, carry):
         rows = pl.ds(pl.multiple_of(i * 64, 64), 64)
         v = pre[rows, :]
         cdf = 0.5 * (1.0 + lax.erf(v * (1.0 / math.sqrt(2.0))))
         bump = v * jnp.exp(-0.5 * v * v) * (1.0 / math.sqrt(2.0 * math.pi))
-        grad2[rows, :] = out_grad[rows, :] * (cdf + bump)
+        grad[rows, :] = out_grad[rows, :] * (cdf + bump)
         return carry
 
-    lax.fori_loop(0, 16, slope, 0)
+    lax.fori_loop(0, grad.shape[0] // 64, some, 0)
+
+
+def front_kernel(layer, pre, out_grad, message, table, grad2):
+    @pl.when(pl.program_id(0) + pl.program_id(1) == 0)
+    def _():
+        table[...] = z_table(1.0)
+
+    layer, pre, out_grad = (ref.reshape(1024, 128) for ref in (layer, pre, out_grad))
+    make_grad(pre, out_grad, grad2)
     for field, values in ((0, layer), (1, grad2)):
         for j in range(0, 4, 2):
             cells = jnp.concatenate(
@@ -123,8 +126,9 @@
                 message[:, field, 0, 8 * (j + k) : 8 * (j + k) + 8, :] = part
 
 
-def local_kernel(point, layer, grad, base, sums, products):
-    layer, grad, base = (ref.reshape(1024, 128) for ref in (layer, grad, base))
+def local_kernel(point, layer, pre, out_grad, base, sums, products, grad):
+    layer, pre, out_grad, base = (ref.reshape(1024, 128) for ref in (layer, pre, out_grad, base))
+    make_grad(pre, out_grad, grad)
     step = pl.program_id(0) * 2 + pl.program_id(1)
 
     @pl.when(step == 0)
@@ -154,38 +158,46 @@
     weight[...] = codes[...].astype(F32) * wide * (1.0 + noise[...])
 
 
+def along_x(table, arrived, j):
+    cells = [arrived[:, 0, :, 8 * k : 8 * k + 8, :].reshape(256, 128) for k in (j, j + 1)]
+    return mm(table, jnp.concatenate(cells, 1))
+
+
 def x_kernel(place, arrived, sums, message):
-    message[:, 16] = jnp.broadcast_to(sums[...][None], (16, 8, 128))
+    message[:, 8] = jnp.broadcast_to(sums[...][None], (16, 8, 128))
     table = x_table(place[0])
-    for field in range(2):
-        for j in range(0, 8, 2):
-            cells = jnp.concatenate(
-                [
-                    arrived[:, field, :, 8 * k : 8 * k + 8, :].reshape(256, 128)
-                    for k in (j, j + 1)
-                ],
-                1,
-            )
-            modes = mm(table, cells)
-            for k in range(2):
-                part = modes[:, 128 * k : 128 * k + 128].reshape(16, 8, 128)
-                message[:, 8 * field + j + k] = part
-
-
-def along_y(arrived, field):
-    rows = arrived.reshape(2176, 128)
+    for j in range(0, 8, 2):
+        modes = along_x(table, arrived, j)
+        for k in range(2):
+            message[:, j + k] = modes[:, 128 * k : 128 * k + 128].reshape(16, 8, 128)
+
+
+def x_side_kernel(place, arrived, keep, give, tiles):
+    table = x_table(place[0])
+    for j in range(0, 8, 2):
+        modes = along_x(table, arrived, j)
+        for k in range(2):
+            tiles[:, j + k] = modes[:, 128 * k : 128 * k + 128].reshape(16, 8, 128)
+    for step in range(8):
+        peer = 2 * ((place[3] + step) & 7)
+        keep[step] = tiles[peer + place[4]]
+        give[step] = tiles[peer + 1 - place[4]]
+
+
+def pair_kernel(keep, got, *pairs):
+    for step, pair in enumerate(pairs):
+        pair[0] = keep[step]
+        pair[1] = got[step]
+
+
+def along_y(table, pieces):
     cells = [
         jnp.concatenate(
-            [
-                rows[pl.ds(136 * peer + 64 * field + 2 * kx + r, 8, stride=8), :]
-                for r in range(2)
-                for peer in range(16)
-            ],
-            0,
+            [rows[pl.ds(at + 2 * kx + r, 8, stride=8), :] for r in range(2) for rows, at in pieces], 0
         )
         for kx in range(4)
     ]
-    modes = mm(y_table(), jnp.concatenate(cells, 1))
+    modes = mm(table, jnp.concatenate(cells, 1))
     modes = [modes[:, 128 * kx : 128 * kx + 128] for kx in range(4)]
     modes = [part[:64] + pltpu.roll(part[64:], 64, 1) for part in modes]
     real, imag = ([part[32 * r : 32 * r + 32] for part in modes] for r in range(2))
@@ -193,8 +205,10 @@
 
 
 def mode_kernel(place, weight, arrived, g_hat, message, sums):
-    sums[...] = jnp.sum(arrived[:, 16], axis=0)
-    g_real, g_imag = along_y(arrived, 1)
+    sums[...] = jnp.sum(arrived[:, 8], axis=0)
+    sources = arrived.reshape(1152, 128)
+    table = y_table(lambda source: source & 7)
+    g_real, g_imag = along_y(table, [(sources, 72 * peer) for peer in range(16)])
     g_hat[0] = g_real
     g_hat[1] = g_imag
     row, column = grid_of(128, 128)
@@ -236,8 +250,14 @@
         rows[pl.ds(1, 16, stride=64), :] = jnp.broadcast_to(bias * (1.0 / (UNIT * CELLS)), (16, 128))
 
 
-def outer_kernel(arrived, g_hat, result):
-    u_real, u_imag = along_y(arrived, 0)
+def outer_kernel(place, *refs):
+    *pairs, g_hat, result = refs
+
+    def pencil(source):
+        return 2 * ((place[3] - (source >> 1)) & 3) + ((source & 1) ^ place[4])
+
+    pieces = [(pair.reshape(128, 128), 64 * k) for pair in pairs for k in range(2)]
+    u_real, u_imag = along_y(y_table(pencil), pieces)
     row, column = grid_of(128, 128)
     u, g = [], []
     for b in range(2):
@@ -274,25 +294,37 @@
         message[:, 0, 2:3] = jnp.broadcast_to(arrived[4, 0, 1:2][None], (16, 1, 128))
 
 
-def end_kernel(arrived, sums, base, result, grad_point, grad_bias, table):
-    base, result = base.reshape(1024, 128), result.reshape(1024, 128)
-
-    @pl.when(pl.program_id(0) + pl.program_id(1) == 0)
+def end_kernel(arrived, sums, base, result, grad_point, grad_bias, table, held, taken):
+    result = result.reshape(1024, 128)
+    step = 2 * pl.program_id(0) + pl.program_id(1)
+
+    def load(n):
+        there = base.at[:, pl.ds(2 * (n // 2), 2), pl.ds(8 * (n % 2), 8), :]
+        return pltpu.make_async_copy(there, held.at[n], taken.at[n])
+
+    @pl.when(step == 0)
     def _():
+        for n in range(4):
+            load(n).start()
         table[...] = z_table(UNIT)
         total = jnp.sum(sums[:, 0], axis=0) * (1.0 / CELLS)
         for k in range(4):
             grad_point[8 * k : 8 * k + 8, :] = total[:, 32 * k : 32 * k + 32]
         grad_bias[...] = arrived[0, 0, 2:3, 0:32]
 
-    for j in range(4):
-        cells = mm(arrived[:, j].reshape(128, 128), table[...], 0, 0)
-        for x in range(2):
-            for odd in range(2):
-                rows = pl.ds(x * 8 + 2 * j + odd, 64, stride=16)
-                result[rows, :] = (
-                    base[rows, :] + cells[64 * odd : 64 * odd + 64, 128 * x : 128 * x + 128]
-                )
+    for n in range(4):
+
+        @pl.when(step == n)
+        def _():
+            load(n).wait()
+            rest = held.at[n].reshape(1024, 128)
+            for j in range(4):
+                cells = mm(arrived[:, j].reshape(128, 128), table[...], 0, 0)
+                for x in range(2):
+                    for odd in range(2):
+                        rows = pl.ds(x * 8 + 2 * j + odd, 64, stride=16)
+                        part = cells[64 * odd : 64 * odd + 64, 128 * x : 128 * x + 128]
+                        result[rows, :] = rest[rows, :] + part
 
 
 def params(steps=0, mebibytes=20):
@@ -324,16 +356,17 @@
     layer, pre, slope_in = (v.reshape(64, 4, 16, 128) for v in (layer_input, pre_act, out_grad))
     plane_first = (lax.axis_index("yp") + lax.axis_index("xp") == 0).astype(jnp.int32)
     owner = plane_first * (lax.axis_index(COLUMN) == 4).astype(jnp.int32)
-    place = jnp.stack([lax.axis_index("zh"), plane_first, owner]).astype(jnp.int32)
+    chip, core = lax.axis_index(("zh", "zl")), lax.axis_index("co")
+    place = jnp.stack([lax.axis_index("zh"), plane_first, owner, chip, core]).astype(jnp.int32)
     mega = 1 << 20
     field = pl.BlockSpec((64, 2, 8, 128), lambda p, h: (0, p, h, 0))
-    grad, message = pl.pallas_call(
+    message = pl.pallas_call(
         front_kernel,
         grid=(2, 2),
         in_specs=[field, field, field],
-        out_specs=[field, pl.BlockSpec((16, 2, 1, 32, 128), lambda p, h: (0, 0, p, h, 0))],
-        out_shape=[shaped(64, 4, 16, 128), shaped(16, 2, 2, 64, 128)],
-        scratch_shapes=[pltpu.VMEM((128, 256), F32)],
+        out_specs=pl.BlockSpec((16, 2, 1, 32, 128), lambda p, h: (0, 0, p, h, 0)),
+        out_shape=shaped(16, 2, 2, 64, 128),
+        scratch_shapes=[pltpu.VMEM((128, 256), F32), pltpu.VMEM((1024, 128), F32)],
         compiler_params=params(2, 60),
         cost_estimate=cost(1 << 30, 10 * mega),
         name="front",
@@ -345,14 +378,14 @@
     base, sums = pl.pallas_call(
         local_kernel,
         grid=(2, 2),
-        in_specs=[whole(64, 64), field, field],
+        in_specs=[whole(64, 64), field, field, field],
         out_specs=[field, whole(8, 128)],
         out_shape=[shaped(64, 4, 16, 128), shaped(8, 128)],
-        scratch_shapes=[pltpu.VMEM((64, 64), F32)],
-        compiler_params=params(2),
-        cost_estimate=cost(1 << 30, 6 * mega),
+        scratch_shapes=[pltpu.VMEM((64, 64), F32), pltpu.VMEM((1024, 128), F32)],
+        compiler_params=params(2, 60),
+        cost_estimate=cost(1 << 30, 8 * mega),
         name="local",
-    )(both, layer, grad)
+    )(both, layer, pre, slope_in)
 
     spread = np.kron(np.eye(64, dtype=np.float32), np.ones((1, 32), np.float32))
     column = pl.BlockSpec((128, 512), lambda i: (0, i))
@@ -373,25 +406,60 @@
         weight_noise.reshape(128, 2048),
     )
 
-    def placed(in_specs, out_specs):
+    def placed(in_specs, out_specs, scratch=()):
         return pltpu.PrefetchScalarGridSpec(
-            num_scalar_prefetch=1, grid=(1,), in_specs=in_specs, out_specs=out_specs
+            num_scalar_prefetch=1,
+            grid=(1,),
+            in_specs=in_specs,
+            out_specs=out_specs,
+            scratch_shapes=scratch,
         )
+
+    def one_field(index):
+        return pl.BlockSpec((16, 1, 2, 64, 128), lambda *_: (0, index, 0, 0, 0))
 
     message = pl.pallas_call(
         x_kernel,
-        grid_spec=placed([whole(16, 2, 2, 64, 128), whole(8, 128)], whole(16, 17, 8, 128)),
-        out_shape=shaped(16, 17, 8, 128),
+        grid_spec=placed([one_field(1), whole(8, 128)], whole(16, 9, 8, 128)),
+        out_shape=shaped(16, 9, 8, 128),
         compiler_params=params(1),
-        cost_estimate=cost(1 << 29, 3 * mega),
+        cost_estimate=cost(1 << 29, 2 * mega),
         name="x_modes",
     )(place, arrived, sums)
+    keep, give = pl.pallas_call(
+        x_side_kernel,
+        grid_spec=placed(
+            [one_field(0)], [whole(8, 8, 8, 128)] * 2, [pltpu.VMEM((16, 8, 8, 128), F32)]
+        ),
+        out_shape=[shaped(8, 8, 8, 128)] * 2,
+        compiler_params=params(1),
+        cost_estimate=cost(1 << 29, 2 * mega),
+        name="x_side",
+    )(place, arrived)
     arrived = exchange(message, COLUMN)
-
+    got = lax.ppermute(give, "co", [(0, 1), (1, 0)])
+    pairs = pl.pallas_call(
+        pair_kernel,
+        grid=(1,),
+        in_specs=[whole(8, 8, 8, 128)] * 2,
+        out_specs=[whole(2, 8, 8, 128)] * 8,
+        out_shape=[shaped(2, 8, 8, 128)] * 8,
+        compiler_params=params(1),
+        cost_estimate=cost(1 << 20, mega),
+        name="pair",
+    )(keep, got)
+
+    def hop(step):
+        route = [(chip, (chip + step) % 8) for chip in range(8)]
+        return lax.ppermute(pairs[step], ("zh", "zl"), route)
+
+    sent = {0: pairs[0]}
+    sent.update((step, hop(step)) for step in ())
+    weight, sent, pairs = lax.optimization_barrier((weight, sent, pairs))
     g_hat, message, sums = pl.pallas_call(
         mode_kernel,
         grid_spec=placed(
-            [whole(128, 2048), whole(16, 17, 8, 128)],
+            [whole(128, 2048), whole(16, 9, 8, 128)],
             [whole(2, 128, 128), whole(16, 8, 8, 128), whole(8, 128)],
         ),
         out_shape=[shaped(2, 128, 128), shaped(16, 8, 8, 128), shaped(8, 128)],
@@ -400,17 +468,8 @@
         name="modes",
     )(place, weight, arrived)
     returned = exchange(message, COLUMN)
-
-    grad_spectral = pl.pallas_call(
-        outer_kernel,
-        grid=(1,),
-        in_specs=[whole(16, 17, 8, 128), whole(2, 128, 128)],
-        out_specs=whole(128, 2048),
-        out_shape=shaped(128, 2048),
-        compiler_params=params(1),
-        cost_estimate=cost(1 << 30, 4 * mega),
-        name="outer",
-    )(arrived, g_hat)
+    sent.update((step, hop(step)) for step in (1, 7, 2, 6))
+    returned, sent = lax.optimization_barrier((returned, sent))
 
     message = pl.pallas_call(
         x_back_kernel,
@@ -422,18 +481,33 @@
     )(place, returned, sums)
     returned = exchange(message, PLANE)
 
+    pairs, _ = lax.optimization_barrier((pairs, message))
+    sent.update((step, hop(step)) for step in range(1, 8) if step not in sent)
+    grad_spectral = pl.pallas_call(
+        outer_kernel,
+        grid_spec=placed([whole(2, 8, 8, 128)] * 8 + [whole(2, 128, 128)], whole(128, 2048)),
+        out_shape=shaped(128, 2048),
+        compiler_params=params(1, 60),
+        cost_estimate=cost(1 << 30, 4 * mega),
+        name="outer",
+    )(place, *(sent[step] for step in range(8)), g_hat)
+
     grad_input, grad_point, grad_bias = pl.pallas_call(
         end_kernel,
         grid=(2, 2),
         in_specs=[
             pl.BlockSpec((16, 4, 8, 128), lambda p, h: (0, 2 * p + h, 0, 0)),
             pl.BlockSpec((16, 1, 8, 128), lambda p, h: (0, 16, 0, 0)),
-            field,
+            pl.BlockSpec(memory_space=pltpu.HBM),
         ],
         out_specs=[field, whole(32, 32), whole(1, 32)],
         out_shape=[shaped(64, 4, 16, 128), shaped(32, 32), shaped(1, 32)],
-        scratch_shapes=[pltpu.VMEM((128, 256), F32)],
-        compiler_params=params(2, 60),
+        scratch_shapes=[
+            pltpu.VMEM((128, 256), F32),
+            pltpu.VMEM((4, 64, 2, 8, 128), F32),
+            pltpu.SemaphoreType.DMA((4,)),
+        ],
+        compiler_params=params(2),
         cost_estimate=cost(1 << 29, 5 * mega),
         name="end",
     )(returned, returned, base)

time: 147 us -> 135 us (0.918)
  blocking collectives: 20.7 us -> 0 us
  starting transfers between devices: 22.1 us -> 38.6 us
  waiting for transfers between devices: 67.2 us -> 56.9 us
  Pallas kernels: 29.3 us -> 33.9 us
  local copies, waits for them, and re-layouts: 6.24 us -> 3.45 us
    all_to_all x3 -> x4, waiting for transfers between devices: 67.2 us -> 37.7 us  [exchange(): lax.all_to_all(message, axes, split_axis=0, concat_axis=0, tiled=True)]
    all_to_all x1 -> x0, blocking collectives: 20.7 us -> none  [exchange(): lax.all_to_all(message, axes, split_axis=0, concat_axis=0, tiled=True)]
    ppermute x0 -> x8, waiting for transfers between devices: none -> 19.3 us  [the longest x7 19.2 us: hop(): return lax.ppermute(pairs[step], ('zh', 'zl'), route)]
    ppermute x0 -> x8, starting transfers between devices: none -> 13 us  [the longest x7 12.7 us: hop(): return lax.ppermute(pairs[step], ('zh', 'zl'), route)]
    pallas_call x1, Pallas kernels: 3.48 us -> 7.28 us  [per_device(): pl.pallas_call(local_kernel, grid=(2, 2), in_specs=[whole(64, 64), field,...]
    all_to_all x3 -> x4, starting transfers between devices: 22.1 us -> 25.6 us  [exchange(): lax.all_to_all(message, axes, split_axis=0, concat_axis=0, tiled=True)]
    unnamed x24 -> x36, local copies, waits for them, and re-layouts: 6.14 us -> 2.66 us
    pallas_call x1, Pallas kernels: 2.6 us -> 4.45 us  [per_device(): pl.pallas_call(mode_kernel, grid_spec=placed([whole(128, 2048), whole(16,...]
  transfers between devices with their start and end apart: 3 -> 12, of which waited for: 3 -> 7; matrix products, arithmetic and copies ran while one was open for 0% -> 1% of each run, Pallas kernels for 5% -> 10%
where the time goes in v3:
time: 135 us; the launch traced here: 134 us
  waiting for transfers between devices  56.9 us (42%)
  starting transfers between devices  38.6 us (29%)
  Pallas kernels  33.9 us (25%)
  local copies, waits for them, and re-layouts  3.45 us (3%)
    all_to_all x4, waiting for transfers between devices, exchange(): lax.all_to_all(message, axes, split_axis=0, concat_axis=0, tiled=True)  37.7 us
    all_to_all x4, starting transfers between devices, exchange(): lax.all_to_all(message, axes, split_axis=0, concat_axis=0, tiled=True)  25.6 us
    ppermute x7, waiting for transfers between devices, hop(): return lax.ppermute(pairs[step], ('zh', 'zl'), route)  19.2 us
    ppermute x7, starting transfers between devices, hop(): return lax.ppermute(pairs[step], ('zh', 'zl'), route)  12.7 us
    pallas_call x1, Pallas kernels, per_device(): pl.pallas_call(front_kernel, grid=(2, 2), in_specs=[field, field, field],...  7.57 us
    pallas_call x1, Pallas kernels, per_device(): pl.pallas_call(local_kernel, grid=(2, 2), in_specs=[whole(64, 64), field,...  7.28 us
    pallas_call x1, Pallas kernels, per_device(): pl.pallas_call(mode_kernel, grid_spec=placed([whole(128, 2048), whole(16,...  4.45 us
    pallas_call x1, Pallas kernels, per_device(): pl.pallas_call(outer_kernel, grid_spec=placed([whole(2, 8, 8, 128)] * 8 +...  4.1 us
  transfers between devices with their start and end apart: 12, of which 7 were waited for; matrix products, arithmetic and copies ran while one was open for 1% of the time, Pallas kernels for 10%

profile of v3, /device:TPU:1, one launch (start us, length us, event | category | flops | bytes accessed | tf_op | source)
XLA Modules:
  0.0 133.9 jit_solution(360367568586189876)
XLA Ops:
  0.6 7.6 %front.1 = f32[16,2,2,64,128]{4,3,2,1,0:T(8,128)} custom-call(f32[64,4,16,128]{3,2,1,0:T(8,128)} %bitcast.17, f32[64,4,16,128]{3,2,1,0:T(8,128)} %bitcast.19, f32[64,4,16,128]{3,2,1,0:T(8,128)} %bitcast.21), custom_call_target="tpu_custom_call" | custom-call | flops 1073741824 | bytes 10485760 | tf_op jit(solution)/shard_map/front/pallas_call | solution.py:363
  8.2 0.0 copy-start.9
  8.2 0.0 copy-start.10
  8.2 7.7 %all-to-all-start = ((f32[16,2,2,64,128]{4,3,2,1,0:T(8,128)}), f32[16,2,2,64,128]{4,3,2,1,0:T(8,128)S(1)}, u32[]{:S(2)}, u32[]{:S(2)}) async-start(f32[16,2,2,64,128]{4,3,2,1,0:T(8,128)} %front.1), calls=%async_computation | async-start | bytes 4194304 | tf_op jit(solution)/shard_map/all_to_all | solution.py:350
  15.9 0.0 copy-done.9
  16.0 0.0 copy-done.10
  16.0 0.7 reshape.46.point
  16.7 0.1 stack.23.place
  16.8 0.0 copy-start.5
  16.8 7.3 %local.1 = (f32[64,4,16,128]{3,2,1,0:T(8,128)}, f32[8,128]{1,0:T(8,128)}) custom-call(f32[64,64]{1,0:T(8,128)} %reshape.46.point, f32[64,4,16,128]{3,2,1,0:T(8,128)} %bitcast.18, f32[64,4,16,128]{3,2,1,0:T(8,128)} %bitcast.20, f32[64,4,16,128]{3,2,1,0:T(8,128)} %bitcast.22), custom_call_target="tpu_custom_call" | custom-call | flops 1073741824 | bytes 8388608 | tf_op jit(solution)/shard_map/local/pallas_call | solution.py:378
  24.1 22.3 %all-to-all-done.arrived = f32[16,2,2,64,128]{4,3,2,1,0:T(8,128)S(1)} async-done(((f32[16,2,2,64,128]{4,3,2,1,0:T(8,128)}), f32[16,2,2,64,128]{4,3,2,1,0:T(8,128)S(1)}, u32[]{:S(2)}, u32[]{:S(2)}) %all-to-all-start) | async-done | bytes 2097184 | tf_op jit(solution)/shard_map/all_to_all | solution.py:350
  46.4 0.0 copy-start.6
  46.4 0.7 copy-done.6
  47.1 1.9 %x_modes.1 = f32[16,9,8,128]{3,2,1,0:T(8,128)} custom-call(s32[5]{0:T(128)S(1)} %stack.23.place, f32[16,2,2,64,128]{4,3,2,1,0:T(8,128)S(1)} %all-to-all-done.arrived, f32[8,128]{1,0:T(8,128)S(1)} %copy-done.6), custom_call_target="tpu_custom_call" | custom-call | flops 536870912 | bytes 2097152 | tf_op jit(solution)/shard_map/x_modes/pallas_call | solution.py:421
  49.0 0.0 copy-start.1
  49.0 0.0 copy-start.3
  49.0 0.0 copy-start.4
  49.0 10.7 %all-to-all-start.1 = ((f32[16,9,8,128]{3,2,1,0:T(8,128)}), f32[16,9,8,128]{3,2,1,0:T(8,128)}, u32[]{:S(2)}, u32[]{:S(2)}) async-start(f32[16,9,8,128]{3,2,1,0:T(8,128)} %x_modes.1), calls=%async_computation.1 | async-start | bytes 1179648 | tf_op jit(solution)/shard_map/all_to_all | solution.py:350
  59.8 1.1 x_side.1
  60.9 0.2 collective-permute-start
  61.2 0.0 copy-done.1
  61.2 0.0 copy-done.3
  61.2 0.0 copy-done.4
  61.2 0.0 copy-done.2
  61.2 1.3 weight.1
  62.5 0.1 collective-permute-done.got
  62.6 0.0 copy-start.7
  62.6 0.6 copy-done.7
  63.2 15.3 %all-to-all-done.1.arrived = f32[16,9,8,128]{3,2,1,0:T(8,128)} async-done(((f32[16,9,8,128]{3,2,1,0:T(8,128)}), f32[16,9,8,128]{3,2,1,0:T(8,128)}, u32[]{:S(2)}, u32[]{:S(2)}) %all-to-all-start.1) | async-done | bytes 589856 | tf_op jit(solution)/shard_map/all_to_all | solution.py:350
  78.5 4.5 %modes.1 = (f32[2,128,128]{2,1,0:T(8,128)S(1)}, f32[16,8,8,128]{3,2,1,0:T(8,128)}, f32[8,128]{1,0:T(8,128)S(1)}) custom-call(s32[5]{0:T(128)S(1)} %stack.23.place, f32[128,2048]{1,0:T(8,128)S(1)} %weight.1, f32[16,9,8,128]{3,2,1,0:T(8,128)} %all-to-all-done.1.arrived), custom_call_target="tpu_custom_call" | custom-call | flops 1073741824 | bytes 3145728 | tf_op jit(solution)/shard_map/modes/pallas_call | solution.py:459
  83.0 0.0 copy-start.8
  83.0 0.7 copy-done.8
  83.7 3.5 %all-to-all-start.2 = ((f32[16,8,8,128]{3,2,1,0:T(8,128)}), f32[16,8,8,128]{3,2,1,0:T(8,128)S(1)}, u32[]{:S(2)}, u32[]{:S(2)}) async-start(f32[16,8,8,128]{3,2,1,0:T(8,128)} %get-tuple-element.54), calls=%async_computation.2 | async-start | bytes 1048576 | tf_op jit(solution)/shard_map/all_to_all | solution.py:350
  87.1 0.9 collective-permute-start.1
  88.0 2.1 %collective-permute-start.2 = (f32[2,8,8,128]{3,2,1,0:T(8,128)S(1)}, f32[2,8,8,128]{3,2,1,0:T(8,128)S(1)}, u32[]{:S(2)}, u32[]{:S(2)}) collective-permute-start(f32[2,8,8,128]{3,2,1,0:T(8,128)S(1)} %get-tuple-element.57), channel_id=1, source_target_pairs={{0,4},{2,6},{4,32},{6,34},{32,36},{34,38},{36,0},{38,2},{1,5},{3,7... | collective-permute-start | bytes 196616 | tf_op jit(solution)/shard_map/ppermute | solution.py:454
  90.1 1.5 %collective-permute-start.3 = (f32[2,8,8,128]{3,2,1,0:T(8,128)S(1)}, f32[2,8,8,128]{3,2,1,0:T(8,128)S(1)}, u32[]{:S(2)}, u32[]{:S(2)}) collective-permute-start(f32[2,8,8,128]{3,2,1,0:T(8,128)S(1)} %get-tuple-element.58), channel_id=1, source_target_pairs={{0,36},{2,38},{4,0},{6,2},{32,4},{34,6},{36,32},{38,34},{1,37},{3,... | collective-permute-start | bytes 196616 | tf_op jit(solution)/shard_map/ppermute | solution.py:454
  91.6 0.7 collective-permute-start.4
  92.2 10.2 %collective-permute-done.1.refs_1_ = f32[2,8,8,128]{3,2,1,0:T(8,128)S(1)} collective-permute-done((f32[2,8,8,128]{3,2,1,0:T(8,128)S(1)}, f32[2,8,8,128]{3,2,1,0:T(8,128)S(1)}, u32[]{:S(2)}, u32[]{:S(2)}) %collective-permute-start.1) | collective-permute-done | bytes 65568 | tf_op jit(solution)/shard_map/ppermute | solution.py:454
  102.4 3.2 %collective-permute-done.2.refs_2_ = f32[2,8,8,128]{3,2,1,0:T(8,128)S(1)} collective-permute-done((f32[2,8,8,128]{3,2,1,0:T(8,128)S(1)}, f32[2,8,8,128]{3,2,1,0:T(8,128)S(1)}, u32[]{:S(2)}, u32[]{:S(2)}) %collective-permute-start.2) | collective-permute-done | bytes 65568 | tf_op jit(solution)/shard_map/ppermute | solution.py:454
  105.6 0.0 collective-permute-done.3.refs_6_
  105.6 0.0 collective-permute-done.4.refs_7_
  105.6 0.0 copy-start.14
  105.6 0.0 all-to-all-done.2.arrived
  105.7 0.0 copy-done.5
  105.7 2.3 %x_cells.1 = f32[16,17,8,128]{3,2,1,0:T(8,128)} custom-call(s32[5]{0:T(128)S(1)} %stack.23.place, f32[16,8,8,128]{3,2,1,0:T(8,128)S(1)} %all-to-all-done.2.arrived, f32[8,128]{1,0:T(8,128)S(1)} %get-tuple-element.61.sums), custom_call_target="tpu_custom_call" | custom-call | flops 536870912 | bytes 2097152 | tf_op jit(solution)/shard_map/x_cells/pallas_call | solution.py:474
  107.9 0.0 copy-done.13
  107.9 0.0 copy-done.14
  107.9 0.0 copy-done.11
  107.9 0.0 copy-done.12
  107.9 3.7 %all-to-all-start.3 = ((f32[16,17,8,128]{3,2,1,0:T(8,128)}), f32[16,17,8,128]{3,2,1,0:T(8,128)S(1)}, u32[]{:S(2)}, u32[]{:S(2)}) async-start(f32[16,17,8,128]{3,2,1,0:T(8,128)} %x_cells.1), calls=%async_computation.3 | async-start | bytes 2228224 | tf_op jit(solution)/shard_map/all_to_all | solution.py:350
  111.6 0.0 copy-start
  111.7 3.4 %collective-permute-start.5 = (f32[2,8,8,128]{3,2,1,0:T(8,128)S(1)}, f32[2,8,8,128]{3,2,1,0:T(8,128)S(1)}, u32[]{:S(2)}, u32[]{:S(2)}) collective-permute-start(f32[2,8,8,128]{3,2,1,0:T(8,128)S(1)} %get-tuple-element.70), channel_id=1, source_target_pairs={{0,6},{2,32},{4,34},{6,36},{32,38},{34,0},{36,2},{38,4},{1,7},{3,3... | collective-permute-start | bytes 196616 | tf_op jit(solution)/shard_map/ppermute | solution.py:454
  115.1 0.7 collective-permute-start.6
  115.8 3.5 %collective-permute-start.7 = (f32[2,8,8,128]{3,2,1,0:T(8,128)S(1)}, f32[2,8,8,128]{3,2,1,0:T(8,128)S(1)}, u32[]{:S(2)}, u32[]{:S(2)}) collective-permute-start(f32[2,8,8,128]{3,2,1,0:T(8,128)S(1)} %get-tuple-element.72), channel_id=1, source_target_pairs={{0,34},{2,36},{4,38},{6,0},{32,2},{34,4},{36,6},{38,32},{1,35},{3,... | collective-permute-start | bytes 196616 | tf_op jit(solution)/shard_map/ppermute | solution.py:454
  119.3 0.2 collective-permute-done.5.refs_3_
  119.5 5.6 %collective-permute-done.6.refs_4_ = f32[2,8,8,128]{3,2,1,0:T(8,128)S(1)} collective-permute-done((f32[2,8,8,128]{3,2,1,0:T(8,128)S(1)}, f32[2,8,8,128]{3,2,1,0:T(8,128)S(1)}, u32[]{:S(2)}, u32[]{:S(2)}) %collective-permute-start.6) | collective-permute-done | bytes 65568 | tf_op jit(solution)/shard_map/ppermute | solution.py:454
  125.1 0.0 collective-permute-done.7.refs_5_
  125.1 0.0 copy-done.15
  125.1 0.6 copy-done.16
  125.7 0.0 copy-done.17
  125.8 4.1 %outer.1 = f32[128,2048]{1,0:T(8,128)} custom-call(s32[5]{0:T(128)} %copy-done.5, f32[2,8,8,128]{3,2,1,0:T(8,128)} %copy-done.7, f32[2,8,8,128]{3,2,1,0:T(8,128)} %copy-done.11, f32[2,8,8,128]{3,2,1,0:T(8,128)} %copy-done.12, f32[2,8,8,128]{3,2,1,0:T(8,128)} %copy-done.15, f32[2,8,8,128]{3,2,1,0:T(8,128)} %copy-done.16, f32[2,8,8,128]{3,2,1,0:T(8,128)} %copy-done.17, ...), custom_call_target="tpu_custom_call" | custom-call | flops 1073741824 | bytes 4194304 | tf_op jit(solution)/shard_map/outer/pallas_call | solution.py:486
  129.9 0.0 all-to-all-done.3.arrived.sums
  129.9 0.0 copy-done
  129.9 3.9 %end.1 = (f32[64,4,16,128]{3,2,1,0:T(8,128)}, f32[32,32]{1,0:T(8,128)}, f32[1,32]{1,0:T(1,128)}) custom-call(f32[16,17,8,128]{3,2,1,0:T(8,128)S(1)} %all-to-all-done.3.arrived.sums, f32[16,17,8,128]{3,2,1,0:T(8,128)S(1)} %all-to-all-done.3.arrived.sums, f32[64,4,16,128]{3,2,1,0:T(8,128)S(1)} %copy-done), custom_call_target="tpu_custom_call" | custom-call | flops 536870912 | bytes 5242880 | tf_op jit(solution)/shard_map/end/pallas_call | solution.py:495
  (9 shorter events, 0.1 us)
Async XLA Ops:
  8.2 7.7 %copy-start.9 = (f32[2,32,2,32]{3,2,1,0:T(2,128)S(1)}, f32[2,32,2,32]{3,2,1,0:T(2,128)}, u32[]{:S(2)}) copy-start(f32[2,32,2,32]{3,2,1,0:T(2,128)} %constant.40) | copy-start | bytes 49156
  8.2 7.8 %copy-start.10 = (f32[32,32]{1,0:T(8,128)S(1)}, f32[32,32]{1,0:T(8,128)}, u32[]{:S(2)}) copy-start(f32[32,32]{1,0:T(8,128)} %param.15) | copy-start | bytes 12292
  8.2 38.2 %all-to-all-start = ((f32[16,2,2,64,128]{4,3,2,1,0:T(8,128)}), f32[16,2,2,64,128]{4,3,2,1,0:T(8,128)S(1)}, u32[]{:S(2)}, u32[]{:S(2)}) async-start(f32[16,2,2,64,128]{4,3,2,1,0:T(8,128)} %front.1), calls=%async_computation | async-start | bytes 4194304 | tf_op jit(solution)/shard_map/all_to_all | solution.py:350
  16.8 88.8 %copy-start.5 = (s32[5]{0:T(128)}, s32[5]{0:T(128)S(1)}, u32[]{:S(2)}) copy-start(s32[5]{0:T(128)S(1)} %stack.23.place) | copy-start | bytes 64
  46.4 0.7 copy-start.6
  49.0 12.1 %copy-start.1 = (s32[1,4,32,2048]{3,2,1,0:T(8,128)S(1)}, s32[1,4,32,2048]{3,2,1,0:T(8,128)}, u32[]{:S(2)}) copy-start(s32[1,4,32,2048]{3,2,1,0:T(8,128)} %param.12) | copy-start | bytes 3145732
  49.0 12.1 %copy-start.3 = (bf16[64,2048]{1,0:T(8,128)(2,1)S(1)}, bf16[64,2048]{1,0:T(8,128)(2,1)}, u32[]{:S(2)}) copy-start(bf16[64,2048]{1,0:T(8,128)(2,1)} %constant.33.clone.spread) | copy-start | bytes 786436
  49.0 12.1 %copy-start.4 = (s32[1,4,32,64]{3,2,1,0:T(8,128)S(1)}, s32[1,4,32,64]{3,2,1,0:T(8,128)}, u32[]{:S(2)}) copy-start(s32[1,4,32,64]{3,2,1,0:T(8,128)} %param.13) | copy-start | bytes 98308
  49.0 29.5 %all-to-all-start.1 = ((f32[16,9,8,128]{3,2,1,0:T(8,128)}), f32[16,9,8,128]{3,2,1,0:T(8,128)}, u32[]{:S(2)}, u32[]{:S(2)}) async-start(f32[16,9,8,128]{3,2,1,0:T(8,128)} %x_modes.1), calls=%async_computation.1 | async-start | bytes 1179648 | tf_op jit(solution)/shard_map/all_to_all | solution.py:350
  59.8 1.4 %copy-start.2 = (f32[1,4,32,2048]{3,2,1,0:T(8,128)S(1)}, f32[1,4,32,2048]{3,2,1,0:T(8,128)}, u32[]{:S(2)}) copy-start(f32[1,4,32,2048]{3,2,1,0:T(8,128)} %param.14) | copy-start | bytes 3145732
  60.9 1.6 %collective-permute-start = (f32[8,8,8,128]{3,2,1,0:T(8,128)S(1)}, f32[8,8,8,128]{3,2,1,0:T(8,128)S(1)}, u32[]{:S(2)}, u32[]{:S(2)}) collective-permute-start(f32[8,8,8,128]{3,2,1,0:T(8,128)S(1)} %get-tuple-element.44), channel_id=1, source_target_pairs={{0,1},{1,0},{2,3},{3,2},{4,5},{5,4},{6,7},{7,6},{8,9},{9,8},{10,11... | collective-permute-start | bytes 786440 | tf_op jit(solution)/shard_map/ppermute | solution.py:440
  62.6 0.6 copy-start.7
  83.0 0.7 copy-start.8
  83.7 22.0 %all-to-all-start.2 = ((f32[16,8,8,128]{3,2,1,0:T(8,128)}), f32[16,8,8,128]{3,2,1,0:T(8,128)S(1)}, u32[]{:S(2)}, u32[]{:S(2)}) async-start(f32[16,8,8,128]{3,2,1,0:T(8,128)} %get-tuple-element.54), calls=%async_computation.2 | async-start | bytes 1048576 | tf_op jit(solution)/shard_map/all_to_all | solution.py:350
  87.1 15.3 %collective-permute-start.1 = (f32[2,8,8,128]{3,2,1,0:T(8,128)S(1)}, f32[2,8,8,128]{3,2,1,0:T(8,128)S(1)}, u32[]{:S(2)}, u32[]{:S(2)}) collective-permute-start(f32[2,8,8,128]{3,2,1,0:T(8,128)S(1)} %get-tuple-element.56), channel_id=1, source_target_pairs={{0,2},{2,4},{4,6},{6,32},{32,34},{34,36},{36,38},{38,0},{1,3},{3,5... | collective-permute-start | bytes 196616 | tf_op jit(solution)/shard_map/ppermute | solution.py:454
  88.0 17.6 %collective-permute-start.2 = (f32[2,8,8,128]{3,2,1,0:T(8,128)S(1)}, f32[2,8,8,128]{3,2,1,0:T(8,128)S(1)}, u32[]{:S(2)}, u32[]{:S(2)}) collective-permute-start(f32[2,8,8,128]{3,2,1,0:T(8,128)S(1)} %get-tuple-element.57), channel_id=1, source_target_pairs={{0,4},{2,6},{4,32},{6,34},{32,36},{34,38},{36,0},{38,2},{1,5},{3,7... | collective-permute-start | bytes 196616 | tf_op jit(solution)/shard_map/ppermute | solution.py:454
  90.1 15.5 %collective-permute-start.3 = (f32[2,8,8,128]{3,2,1,0:T(8,128)S(1)}, f32[2,8,8,128]{3,2,1,0:T(8,128)S(1)}, u32[]{:S(2)}, u32[]{:S(2)}) collective-permute-start(f32[2,8,8,128]{3,2,1,0:T(8,128)S(1)} %get-tuple-element.58), channel_id=1, source_target_pairs={{0,36},{2,38},{4,0},{6,2},{32,4},{34,6},{36,32},{38,34},{1,37},{3,... | collective-permute-start | bytes 196616 | tf_op jit(solution)/shard_map/ppermute | solution.py:454
  91.6 14.0 %collective-permute-start.4 = (f32[2,8,8,128]{3,2,1,0:T(8,128)S(1)}, f32[2,8,8,128]{3,2,1,0:T(8,128)S(1)}, u32[]{:S(2)}, u32[]{:S(2)}) collective-permute-start(f32[2,8,8,128]{3,2,1,0:T(8,128)S(1)} %get-tuple-element.59), channel_id=1, source_target_pairs={{0,38},{2,0},{4,2},{6,4},{32,6},{34,32},{36,34},{38,36},{1,39},{3,... | collective-permute-start | bytes 196616 | tf_op jit(solution)/shard_map/ppermute | solution.py:454
  102.4 5.5 %copy-start.11 = (f32[2,8,8,128]{3,2,1,0:T(8,128)}, f32[2,8,8,128]{3,2,1,0:T(8,128)S(1)}, u32[]{:S(2)}) copy-start(f32[2,8,8,128]{3,2,1,0:T(8,128)S(1)} %collective-permute-done.1.refs_1_) | copy-start | bytes 196612
  105.6 2.3 %copy-start.12 = (f32[2,8,8,128]{3,2,1,0:T(8,128)}, f32[2,8,8,128]{3,2,1,0:T(8,128)S(1)}, u32[]{:S(2)}) copy-start(f32[2,8,8,128]{3,2,1,0:T(8,128)S(1)} %collective-permute-done.2.refs_2_) | copy-start | bytes 196612
  105.6 2.3 %copy-start.13 = (f32[2,8,8,128]{3,2,1,0:T(8,128)}, f32[2,8,8,128]{3,2,1,0:T(8,128)S(1)}, u32[]{:S(2)}) copy-start(f32[2,8,8,128]{3,2,1,0:T(8,128)S(1)} %collective-permute-done.3.refs_6_) | copy-start | bytes 196612
  105.6 2.3 %copy-start.14 = (f32[2,8,8,128]{3,2,1,0:T(8,128)}, f32[2,8,8,128]{3,2,1,0:T(8,128)S(1)}, u32[]{:S(2)}) copy-start(f32[2,8,8,128]{3,2,1,0:T(8,128)S(1)} %collective-permute-done.4.refs_7_) | copy-start | bytes 196612
  107.9 21.9 %all-to-all-start.3 = ((f32[16,17,8,128]{3,2,1,0:T(8,128)}), f32[16,17,8,128]{3,2,1,0:T(8,128)S(1)}, u32[]{:S(2)}, u32[]{:S(2)}) async-start(f32[16,17,8,128]{3,2,1,0:T(8,128)} %x_cells.1), calls=%async_computation.3 | async-start | bytes 2228224 | tf_op jit(solution)/shard_map/all_to_all | solution.py:350
  111.6 18.2 %copy-start = (f32[64,4,16,128]{3,2,1,0:T(8,128)S(1)}, f32[64,4,16,128]{3,2,1,0:T(8,128)}, u32[]{:S(2)}) copy-start(f32[64,4,16,128]{3,2,1,0:T(8,128)} %get-tuple-element.62.base) | copy-start | bytes 6291460
  111.7 7.8 %collective-permute-start.5 = (f32[2,8,8,128]{3,2,1,0:T(8,128)S(1)}, f32[2,8,8,128]{3,2,1,0:T(8,128)S(1)}, u32[]{:S(2)}, u32[]{:S(2)}) collective-permute-start(f32[2,8,8,128]{3,2,1,0:T(8,128)S(1)} %get-tuple-element.70), channel_id=1, source_target_pairs={{0,6},{2,32},{4,34},{6,36},{32,38},{34,0},{36,2},{38,4},{1,7},{3,3... | collective-permute-start | bytes 196616 | tf_op jit(solution)/shard_map/ppermute | solution.py:454
  115.1 10.0 %collective-permute-start.6 = (f32[2,8,8,128]{3,2,1,0:T(8,128)S(1)}, f32[2,8,8,128]{3,2,1,0:T(8,128)S(1)}, u32[]{:S(2)}, u32[]{:S(2)}) collective-permute-start(f32[2,8,8,128]{3,2,1,0:T(8,128)S(1)} %get-tuple-element.71), channel_id=1, source_target_pairs={{0,32},{2,34},{4,36},{6,38},{32,0},{34,2},{36,4},{38,6},{1,33},{3,... | collective-permute-start | bytes 196616 | tf_op jit(solution)/shard_map/ppermute | solution.py:454
  115.8 9.3 %collective-permute-start.7 = (f32[2,8,8,128]{3,2,1,0:T(8,128)S(1)}, f32[2,8,8,128]{3,2,1,0:T(8,128)S(1)}, u32[]{:S(2)}, u32[]{:S(2)}) collective-permute-start(f32[2,8,8,128]{3,2,1,0:T(8,128)S(1)} %get-tuple-element.72), channel_id=1, source_target_pairs={{0,34},{2,36},{4,38},{6,0},{32,2},{34,4},{36,6},{38,32},{1,35},{3,... | collective-permute-start | bytes 196616 | tf_op jit(solution)/shard_map/ppermute | solution.py:454
  119.5 5.6 %copy-start.15 = (f32[2,8,8,128]{3,2,1,0:T(8,128)}, f32[2,8,8,128]{3,2,1,0:T(8,128)S(1)}, u32[]{:S(2)}) copy-start(f32[2,8,8,128]{3,2,1,0:T(8,128)S(1)} %collective-permute-done.5.refs_3_) | copy-start | bytes 196612
  125.1 0.6 copy-start.16
  125.1 0.7 copy-start.17

commit v4 on v3

--- a/solution.py
+++ b/solution.py
@@ -9,7 +9,6 @@
 from jax.sharding import Mesh
 from jax.sharding import PartitionSpec as P
 
-HIGH = lax.Precision.HIGH
 F32 = jnp.float32
 BF16 = jnp.bfloat16
 CELLS = 4194304.0
@@ -18,9 +17,9 @@
 COLUMN = ("zh", "zl", "co")
 
 
-def mm(left, right, left_dim=1, right_dim=0, precision=HIGH):
+def dot(left, right, left_dim=1, right_dim=0):
     dims = (((left_dim,), (right_dim,)), ((), ()))
-    return lax.dot_general(left, right, dims, precision=precision, preferred_element_type=F32)
+    return lax.dot_general(left, right, dims, preferred_element_type=F32)
 
 
 def halves(values):
@@ -28,9 +27,16 @@
     return top, (values - top.astype(F32)).astype(BF16)
 
 
+def mm(left, right, left_dim=1, right_dim=0):
+    (left_top, left_rest), (right_top, right_rest) = halves(left), halves(right)
+    size = left.shape[1 - left_dim]
+    both = dot(jnp.concatenate([left_top, left_rest], 1 - left_dim), right_top, left_dim, right_dim)
+    return both[:size] + both[size:] + dot(left_top, right_rest, left_dim, right_dim)
+
+
 def mm_exact(values, pattern):
     top, rest = halves(values)
-    return mm(top, pattern, precision=None) + mm(rest, pattern, precision=None)
+    return dot(top, pattern) + dot(rest, pattern)
 
 
 def sine(turns):
@@ -105,22 +111,22 @@
 def front_kernel(layer, pre, out_grad, message, table, grad2):
     @pl.when(pl.program_id(0) + pl.program_id(1) == 0)
     def _():
-        table[...] = z_table(1.0)
+        table[...] = jnp.concatenate(halves(z_table(1.0)), 0)
 
     layer, pre, out_grad = (ref.reshape(1024, 128) for ref in (layer, pre, out_grad))
     make_grad(pre, out_grad, grad2)
     for field, values in ((0, layer), (1, grad2)):
         for j in range(0, 4, 2):
-            cells = jnp.concatenate(
-                [
-                    jnp.concatenate(
-                        [values[pl.ds(x * 8 + 2 * j + y, 64, stride=16), :] for y in range(4)], 0
-                    )
-                    for x in range(2)
-                ],
-                1,
-            )
-            spectrum = mm(table[...], cells, 1, 1)
+            cells = [
+                jnp.concatenate(
+                    [values[pl.ds(x * 8 + 2 * j + y, 64, stride=16), :] for y in range(4)], 0
+                )
+                for x in range(2)
+            ]
+            top, rest = halves(jnp.concatenate(cells, 1))
+            spectrum = dot(top, table[...], 1, 1)
+            spectrum = spectrum[:, :128] + spectrum[:, 128:] + dot(rest, table[:128], 1, 1)
+            spectrum = spectrum.T
             for k in range(2):
                 part = spectrum[:, 128 * k : 128 * k + 128].reshape(16, 8, 128)
                 message[:, field, 0, 8 * (j + k) : 8 * (j + k) + 8, :] = part
@@ -154,7 +160,7 @@
     step = jnp.exp2(scales[...].astype(F32) * -0.25) * (1.0 / (16.0 * math.sqrt(32.0)))
     top, rest = halves(step)
     last = (step - top.astype(F32) - rest.astype(F32)).astype(BF16)
-    wide = sum(mm(part, spread[...], precision=None) for part in (last, rest, top))
+    wide = sum(dot(part, spread[...]) for part in (last, rest, top))
     weight[...] = codes[...].astype(F32) * wide * (1.0 + noise[...])
 
 
@@ -204,13 +210,15 @@
     return jnp.concatenate(real, 0), jnp.concatenate(imag, 0)
 
 
-def mode_kernel(place, weight, arrived, g_hat, message, sums):
+def mode_kernel(place, weight, arrived, g_there, message, sums, g_hat, sent):
     sums[...] = jnp.sum(arrived[:, 8], axis=0)
     sources = arrived.reshape(1152, 128)
     table = y_table(lambda source: source & 7)
     g_real, g_imag = along_y(table, [(sources, 72 * peer) for peer in range(16)])
     g_hat[0] = g_real
     g_hat[1] = g_imag
+    store = pltpu.make_async_copy(g_hat, g_there, sent)
+    store.start()
     row, column = grid_of(128, 128)
     row_long, column_long = grid_of(1024, 128)
     gather = pattern((row_long >> 5) == column_long)
@@ -249,6 +257,8 @@
         bias = g_real[16:17] + pltpu.roll(g_real[16:17], 96, 1)
         rows[pl.ds(1, 16, stride=64), :] = jnp.broadcast_to(bias * (1.0 / (UNIT * CELLS)), (16, 128))
 
+    store.wait()
+
 
 def outer_kernel(place, *refs):
     *pairs, g_hat, result = refs
@@ -366,7 +376,7 @@
         in_specs=[field, field, field],
         out_specs=pl.BlockSpec((16, 2, 1, 32, 128), lambda p, h: (0, 0, p, h, 0)),
         out_shape=shaped(16, 2, 2, 64, 128),
-        scratch_shapes=[pltpu.VMEM((128, 256), F32), pltpu.VMEM((1024, 128), F32)],
+        scratch_shapes=[pltpu.VMEM((256, 256), BF16), pltpu.VMEM((1024, 128), F32)],
         compiler_params=params(2, 60),
         cost_estimate=cost(1 << 30, 10 * mega),
         name="front",
@@ -382,7 +392,7 @@
         out_specs=[field, whole(8, 128)],
         out_shape=[shaped(64, 4, 16, 128), shaped(8, 128)],
         scratch_shapes=[pltpu.VMEM((64, 64), F32), pltpu.VMEM((1024, 128), F32)],
-        compiler_params=params(2, 60),
+        compiler_params=params(2),
         cost_estimate=cost(1 << 30, 8 * mega),
         name="local",
     )(both, layer, pre, slope_in)
@@ -414,6 +424,8 @@
             out_specs=out_specs,
             scratch_shapes=scratch,
         )
+
+    in_hbm = pl.BlockSpec(memory_space=pltpu.HBM)
 
     def one_field(index):
         return pl.BlockSpec((16, 1, 2, 64, 128), lambda *_: (0, index, 0, 0, 0))
@@ -454,13 +466,13 @@
         return lax.ppermute(pairs[step], ("zh", "zl"), route)
 
     sent = {0: pairs[0]}
-    sent.update((step, hop(step)) for step in ())
     weight, sent, pairs = lax.optimization_barrier((weight, sent, pairs))
     g_hat, message, sums = pl.pallas_call(
         mode_kernel,
         grid_spec=placed(
             [whole(128, 2048), whole(16, 9, 8, 128)],
-            [whole(2, 128, 128), whole(16, 8, 8, 128), whole(8, 128)],
+            [in_hbm, whole(16, 8, 8, 128), whole(8, 128)],
+            [pltpu.VMEM((2, 128, 128), F32), pltpu.SemaphoreType.DMA],
         ),
         out_shape=[shaped(2, 128, 128), shaped(16, 8, 8, 128), shaped(8, 128)],
         compiler_params=params(1),
@@ -468,7 +480,7 @@
         name="modes",
     )(place, weight, arrived)
     returned = exchange(message, COLUMN)
-    sent.update((step, hop(step)) for step in (1, 7, 2, 6))
+    sent.update((step, hop(step)) for step in (1,7,2,6))
     returned, sent = lax.optimization_barrier((returned, sent))
 
     message = pl.pallas_call(
@@ -498,7 +510,7 @@
         in_specs=[
             pl.BlockSpec((16, 4, 8, 128), lambda p, h: (0, 2 * p + h, 0, 0)),
             pl.BlockSpec((16, 1, 8, 128), lambda p, h: (0, 16, 0, 0)),
-            pl.BlockSpec(memory_space=pltpu.HBM),
+            in_hbm,
         ],
         out_specs=[field, whole(32, 32), whole(1, 32)],
         out_shape=[shaped(64, 4, 16, 128), shaped(32, 32), shaped(1, 32)],

time: 135 us -> 133 us (0.985)
  local copies, waits for them, and re-layouts: 3.45 us -> 8.25 us
  waiting for transfers between devices: 56.9 us -> 53.7 us
  Pallas kernels: 33.9 us -> 31 us
    unnamed x36 -> x42, local copies, waits for them, and re-layouts: 2.66 us -> 8.07 us
    all_to_all x4, waiting for transfers between devices: 37.7 us -> 34.4 us  [exchange(): lax.all_to_all(message, axes, split_axis=0, concat_axis=0, tiled=True)]
    pallas_call x1, Pallas kernels: 7.28 us -> 4.99 us  [per_device(): pl.pallas_call(local_kernel, grid=(2, 2), in_specs=[whole(64, 64), field,...]
  transfers between devices with their start and end apart: 12 -> 12, of which waited for: 7 -> 7; matrix products, arithmetic and copies ran while one was open for 1% -> 0% of each run, Pallas kernels for 10% -> 9%
where the time goes in v4:
time: 133 us
  waiting for transfers between devices  53.7 us (40%)
  starting transfers between devices  38.6 us (29%)
  Pallas kernels  31 us (23%)
  local copies, waits for them, and re-layouts  8.25 us (6%)
    all_to_all x4, waiting for transfers between devices, exchange(): lax.all_to_all(message, axes, split_axis=0, concat_axis=0, tiled=True)  34.4 us
    all_to_all x4, starting transfers between devices, exchange(): lax.all_to_all(message, axes, split_axis=0, concat_axis=0, tiled=True)  25.7 us
    ppermute x7, waiting for transfers between devices, hop(): return lax.ppermute(pairs[step], ('zh', 'zl'), route)  19.2 us
    ppermute x7, starting transfers between devices, hop(): return lax.ppermute(pairs[step], ('zh', 'zl'), route)  12.7 us
    unnamed x42, local copies, waits for them, and re-layouts  8.07 us
    pallas_call x1, Pallas kernels, per_device(): pl.pallas_call(front_kernel, grid=(2, 2), in_specs=[field, field, field],...  6.87 us
    pallas_call x1, Pallas kernels, per_device(): pl.pallas_call(local_kernel, grid=(2, 2), in_specs=[whole(64, 64), field,...  4.99 us
    pallas_call x1, Pallas kernels, per_device(): pl.pallas_call(mode_kernel, grid_spec=placed([whole(128, 2048), whole(16,...  4.63 us
  transfers between devices with their start and end apart: 12, of which 7 were waited for; matrix products, arithmetic and copies ran while one was open for 0% of the time, Pallas kernels for 9%

profile of v4, /device:TPU:1, one launch (start us, length us, event | category | flops | bytes accessed | tf_op | source)
XLA Modules:
  0.0 132.6 jit_solution(16581483212226394992)
XLA Ops:
  0.6 6.9 %front.1 = f32[16,2,2,64,128]{4,3,2,1,0:T(8,128)} custom-call(f32[64,4,16,128]{3,2,1,0:T(8,128)} %bitcast.14, f32[64,4,16,128]{3,2,1,0:T(8,128)} %bitcast.16, f32[64,4,16,128]{3,2,1,0:T(8,128)} %bitcast.18), custom_call_target="tpu_custom_call" | custom-call | flops 1073741824 | bytes 10485760 | tf_op jit(solution)/shard_map/front/pallas_call | solution.py:373
  7.5 0.0 copy-start.12
  7.5 0.0 copy-start.13
  7.5 7.7 %all-to-all-start = ((f32[16,2,2,64,128]{4,3,2,1,0:T(8,128)}), f32[16,2,2,64,128]{4,3,2,1,0:T(8,128)S(1)}, u32[]{:S(2)}, u32[]{:S(2)}) async-start(f32[16,2,2,64,128]{4,3,2,1,0:T(8,128)} %front.1), calls=%async_computation | async-start | bytes 4194304 | tf_op jit(solution)/shard_map/all_to_all | solution.py:360
  15.2 0.0 copy-done.12
  15.2 0.0 copy-done.13
  15.3 0.1 reshape.46.point
  15.4 0.1 stack.23.place
  15.5 0.0 copy-start
  15.5 1.6 %copy-done = f32[2,32,4,16,128]{4,3,2,1,0:T(8,128)S(1)} copy-done((f32[2,32,4,16,128]{4,3,2,1,0:T(8,128)S(1)}, f32[2,32,4,16,128]{4,3,2,1,0:T(8,128)}, u32[]{:S(2)}) %copy-start) | copy-done | bytes 2097176
  17.1 1.6 %copy-done.1 = f32[2,32,4,16,128]{4,3,2,1,0:T(8,128)S(1)} copy-done((f32[2,32,4,16,128]{4,3,2,1,0:T(8,128)S(1)}, f32[2,32,4,16,128]{4,3,2,1,0:T(8,128)}, u32[]{:S(2)}) %copy-start.1) | copy-done | bytes 2097176
  18.7 1.6 %copy-done.2 = f32[2,32,4,16,128]{4,3,2,1,0:T(8,128)S(1)} copy-done((f32[2,32,4,16,128]{4,3,2,1,0:T(8,128)S(1)}, f32[2,32,4,16,128]{4,3,2,1,0:T(8,128)}, u32[]{:S(2)}) %copy-start.2) | copy-done | bytes 2097176
  20.3 5.0 %local.1 = (f32[64,4,16,128]{3,2,1,0:T(8,128)S(1)}, f32[8,128]{1,0:T(8,128)S(1)}) custom-call(f32[64,64]{1,0:T(8,128)S(1)} %reshape.46.point, f32[64,4,16,128]{3,2,1,0:T(8,128)S(1)} %bitcast.15, f32[64,4,16,128]{3,2,1,0:T(8,128)S(1)} %bitcast.17, f32[64,4,16,128]{3,2,1,0:T(8,128)S(1)} %bitcast.19), custom_call_target="tpu_custom_call" | custom-call | flops 1073741824 | bytes 8388608 | tf_op jit(solution)/shard_map/local/pallas_call | solution.py:388
  25.3 0.0 copy-start.3
  25.3 1.3 %copy-done.3 = f32[64,4,16,128]{3,2,1,0:T(8,128)} copy-done((f32[64,4,16,128]{3,2,1,0:T(8,128)}, f32[64,4,16,128]{3,2,1,0:T(8,128)S(1)}, u32[]{:S(2)}) %copy-start.3) | copy-done | bytes 2097176
  26.6 19.1 %all-to-all-done.arrived = f32[16,2,2,64,128]{4,3,2,1,0:T(8,128)S(1)} async-done(((f32[16,2,2,64,128]{4,3,2,1,0:T(8,128)}), f32[16,2,2,64,128]{4,3,2,1,0:T(8,128)S(1)}, u32[]{:S(2)}, u32[]{:S(2)}) %all-to-all-start) | async-done | bytes 2097184 | tf_op jit(solution)/shard_map/all_to_all | solution.py:360
  45.7 1.9 %x_modes.1 = f32[16,9,8,128]{3,2,1,0:T(8,128)} custom-call(s32[5]{0:T(128)S(1)} %stack.23.place, f32[16,2,2,64,128]{4,3,2,1,0:T(8,128)S(1)} %all-to-all-done.arrived, f32[8,128]{1,0:T(8,128)S(1)} %get-tuple-element.41.sums), custom_call_target="tpu_custom_call" | custom-call | flops 536870912 | bytes 2097152 | tf_op jit(solution)/shard_map/x_modes/pallas_call | solution.py:433
  47.6 10.8 %all-to-all-start.1 = ((f32[16,9,8,128]{3,2,1,0:T(8,128)}), f32[16,9,8,128]{3,2,1,0:T(8,128)}, u32[]{:S(2)}, u32[]{:S(2)}) async-start(f32[16,9,8,128]{3,2,1,0:T(8,128)} %x_modes.1), calls=%async_computation.1 | async-start | bytes 1179648 | tf_op jit(solution)/shard_map/all_to_all | solution.py:360
  58.4 1.1 x_side.1
  59.5 0.2 collective-permute-start
  59.7 0.0 copy-done.5
  59.7 0.0 copy-done.7
  59.7 0.0 copy-done.8
  59.7 0.0 copy-done.6
  59.7 1.3 weight.1
  61.0 0.1 collective-permute-done.got
  61.1 0.0 copy-start.10
  61.1 0.6 copy-done.10
  61.7 15.4 %all-to-all-done.1.arrived = f32[16,9,8,128]{3,2,1,0:T(8,128)} async-done(((f32[16,9,8,128]{3,2,1,0:T(8,128)}), f32[16,9,8,128]{3,2,1,0:T(8,128)}, u32[]{:S(2)}, u32[]{:S(2)}) %all-to-all-start.1) | async-done | bytes 589856 | tf_op jit(solution)/shard_map/all_to_all | solution.py:360
  77.1 4.6 %modes.1 = (f32[2,128,128]{2,1,0:T(8,128)S(1)}, f32[16,8,8,128]{3,2,1,0:T(8,128)}, f32[8,128]{1,0:T(8,128)S(1)}) custom-call(s32[5]{0:T(128)S(1)} %stack.23.place, f32[128,2048]{1,0:T(8,128)S(1)} %weight.1, f32[16,9,8,128]{3,2,1,0:T(8,128)} %all-to-all-done.1.arrived), custom_call_target="tpu_custom_call" | custom-call | flops 1073741824 | bytes 3145728 | tf_op jit(solution)/shard_map/modes/pallas_call | solution.py:470
  81.7 0.0 copy-start.11
  81.8 0.7 copy-done.11
  82.4 3.5 %all-to-all-start.2 = ((f32[16,8,8,128]{3,2,1,0:T(8,128)}), f32[16,8,8,128]{3,2,1,0:T(8,128)S(1)}, u32[]{:S(2)}, u32[]{:S(2)}) async-start(f32[16,8,8,128]{3,2,1,0:T(8,128)} %get-tuple-element.54), calls=%async_computation.2 | async-start | bytes 1048576 | tf_op jit(solution)/shard_map/all_to_all | solution.py:360
  85.9 0.9 collective-permute-start.1
  86.8 2.1 %collective-permute-start.2 = (f32[2,8,8,128]{3,2,1,0:T(8,128)S(1)}, f32[2,8,8,128]{3,2,1,0:T(8,128)S(1)}, u32[]{:S(2)}, u32[]{:S(2)}) collective-permute-start(f32[2,8,8,128]{3,2,1,0:T(8,128)S(1)} %get-tuple-element.57), channel_id=1, source_target_pairs={{0,4},{2,6},{4,32},{6,34},{32,36},{34,38},{36,0},{38,2},{1,5},{3,7... | collective-permute-start | bytes 196616 | tf_op jit(solution)/shard_map/ppermute | solution.py:466
  88.8 1.5 %collective-permute-start.3 = (f32[2,8,8,128]{3,2,1,0:T(8,128)S(1)}, f32[2,8,8,128]{3,2,1,0:T(8,128)S(1)}, u32[]{:S(2)}, u32[]{:S(2)}) collective-permute-start(f32[2,8,8,128]{3,2,1,0:T(8,128)S(1)} %get-tuple-element.58), channel_id=1, source_target_pairs={{0,36},{2,38},{4,0},{6,2},{32,4},{34,6},{36,32},{38,34},{1,37},{3,... | collective-permute-start | bytes 196616 | tf_op jit(solution)/shard_map/ppermute | solution.py:466
  90.3 0.7 collective-permute-start.4
  91.0 10.2 %collective-permute-done.1.refs_1_ = f32[2,8,8,128]{3,2,1,0:T(8,128)S(1)} collective-permute-done((f32[2,8,8,128]{3,2,1,0:T(8,128)S(1)}, f32[2,8,8,128]{3,2,1,0:T(8,128)S(1)}, u32[]{:S(2)}, u32[]{:S(2)}) %collective-permute-start.1) | collective-permute-done | bytes 65568 | tf_op jit(solution)/shard_map/ppermute | solution.py:466
  101.2 3.2 %collective-permute-done.2.refs_2_ = f32[2,8,8,128]{3,2,1,0:T(8,128)S(1)} collective-permute-done((f32[2,8,8,128]{3,2,1,0:T(8,128)S(1)}, f32[2,8,8,128]{3,2,1,0:T(8,128)S(1)}, u32[]{:S(2)}, u32[]{:S(2)}) %collective-permute-start.2) | collective-permute-done | bytes 65568 | tf_op jit(solution)/shard_map/ppermute | solution.py:466
  104.4 0.0 collective-permute-done.3.refs_6_
  104.4 0.0 collective-permute-done.4.refs_7_
  104.4 0.0 copy-start.17
  104.4 0.0 all-to-all-done.2.arrived
  104.4 0.0 copy-done.9
  104.4 2.2 %x_cells.1 = f32[16,17,8,128]{3,2,1,0:T(8,128)} custom-call(s32[5]{0:T(128)S(1)} %stack.23.place, f32[16,8,8,128]{3,2,1,0:T(8,128)S(1)} %all-to-all-done.2.arrived, f32[8,128]{1,0:T(8,128)S(1)} %get-tuple-element.61.sums), custom_call_target="tpu_custom_call" | custom-call | flops 536870912 | bytes 2097152 | tf_op jit(solution)/shard_map/x_cells/pallas_call | solution.py:486
  106.6 0.0 copy-done.16
  106.7 0.0 copy-done.17
  106.7 0.0 copy-done.14
  106.7 0.0 copy-done.15
  106.7 3.7 %all-to-all-start.3 = ((f32[16,17,8,128]{3,2,1,0:T(8,128)}), f32[16,17,8,128]{3,2,1,0:T(8,128)S(1)}, u32[]{:S(2)}, u32[]{:S(2)}) async-start(f32[16,17,8,128]{3,2,1,0:T(8,128)} %x_cells.1), calls=%async_computation.3 | async-start | bytes 2228224 | tf_op jit(solution)/shard_map/all_to_all | solution.py:360
  110.4 0.0 copy-start.4
  110.4 3.4 %collective-permute-start.5 = (f32[2,8,8,128]{3,2,1,0:T(8,128)S(1)}, f32[2,8,8,128]{3,2,1,0:T(8,128)S(1)}, u32[]{:S(2)}, u32[]{:S(2)}) collective-permute-start(f32[2,8,8,128]{3,2,1,0:T(8,128)S(1)} %get-tuple-element.70), channel_id=1, source_target_pairs={{0,6},{2,32},{4,34},{6,36},{32,38},{34,0},{36,2},{38,4},{1,7},{3,3... | collective-permute-start | bytes 196616 | tf_op jit(solution)/shard_map/ppermute | solution.py:466
  113.8 0.7 collective-permute-start.6
  114.5 3.5 %collective-permute-start.7 = (f32[2,8,8,128]{3,2,1,0:T(8,128)S(1)}, f32[2,8,8,128]{3,2,1,0:T(8,128)S(1)}, u32[]{:S(2)}, u32[]{:S(2)}) collective-permute-start(f32[2,8,8,128]{3,2,1,0:T(8,128)S(1)} %get-tuple-element.72), channel_id=1, source_target_pairs={{0,34},{2,36},{4,38},{6,0},{32,2},{34,4},{36,6},{38,32},{1,35},{3,... | collective-permute-start | bytes 196616 | tf_op jit(solution)/shard_map/ppermute | solution.py:466
  118.0 0.2 collective-permute-done.5.refs_3_
  118.2 5.6 %collective-permute-done.6.refs_4_ = f32[2,8,8,128]{3,2,1,0:T(8,128)S(1)} collective-permute-done((f32[2,8,8,128]{3,2,1,0:T(8,128)S(1)}, f32[2,8,8,128]{3,2,1,0:T(8,128)S(1)}, u32[]{:S(2)}, u32[]{:S(2)}) %collective-permute-start.6) | collective-permute-done | bytes 65568 | tf_op jit(solution)/shard_map/ppermute | solution.py:466
  123.8 0.0 collective-permute-done.7.refs_5_
  123.8 0.0 copy-done.18
  123.8 0.6 copy-done.19
  124.5 0.0 copy-done.20
  124.5 4.1 %outer.1 = f32[128,2048]{1,0:T(8,128)} custom-call(s32[5]{0:T(128)} %copy-done.9, f32[2,8,8,128]{3,2,1,0:T(8,128)} %copy-done.10, f32[2,8,8,128]{3,2,1,0:T(8,128)} %copy-done.14, f32[2,8,8,128]{3,2,1,0:T(8,128)} %copy-done.15, f32[2,8,8,128]{3,2,1,0:T(8,128)} %copy-done.18, f32[2,8,8,128]{3,2,1,0:T(8,128)} %copy-done.19, f32[2,8,8,128]{3,2,1,0:T(8,128)} %copy-done.20, ...), custom_call_target="tpu_custom_call" | custom-call | flops 1073741824 | bytes 4194304 | tf_op jit(solution)/shard_map/outer/pallas_call | solution.py:498
  128.6 0.0 all-to-all-done.3.arrived.sums
  128.6 0.0 copy-done.4
  128.6 3.8 %end.1 = (f32[64,4,16,128]{3,2,1,0:T(8,128)}, f32[32,32]{1,0:T(8,128)}, f32[1,32]{1,0:T(1,128)}) custom-call(f32[16,17,8,128]{3,2,1,0:T(8,128)S(1)} %all-to-all-done.3.arrived.sums, f32[16,17,8,128]{3,2,1,0:T(8,128)S(1)} %all-to-all-done.3.arrived.sums, f32[64,4,16,128]{3,2,1,0:T(8,128)S(1)} %copy-done.4), custom_call_target="tpu_custom_call" | custom-call | flops 536870912 | bytes 5242880 | tf_op jit(solution)/shard_map/end/pallas_call | solution.py:507
  (15 shorter events, 0.1 us)
Async XLA Ops:
  7.5 7.7 %copy-start.12 = (f32[2,32,2,32]{3,2,1,0:T(2,128)S(1)}, f32[2,32,2,32]{3,2,1,0:T(2,128)}, u32[]{:S(2)}) copy-start(f32[2,32,2,32]{3,2,1,0:T(2,128)} %constant.40) | copy-start | bytes 49156
  7.5 7.8 %copy-start.13 = (f32[32,32]{1,0:T(8,128)S(1)}, f32[32,32]{1,0:T(8,128)}, u32[]{:S(2)}) copy-start(f32[32,32]{1,0:T(8,128)} %param.15) | copy-start | bytes 12292
  7.5 38.2 %all-to-all-start = ((f32[16,2,2,64,128]{4,3,2,1,0:T(8,128)}), f32[16,2,2,64,128]{4,3,2,1,0:T(8,128)S(1)}, u32[]{:S(2)}, u32[]{:S(2)}) async-start(f32[16,2,2,64,128]{4,3,2,1,0:T(8,128)} %front.1), calls=%async_computation | async-start | bytes 4194304 | tf_op jit(solution)/shard_map/all_to_all | solution.py:360
  15.5 1.6 %copy-start = (f32[2,32,4,16,128]{4,3,2,1,0:T(8,128)S(1)}, f32[2,32,4,16,128]{4,3,2,1,0:T(8,128)}, u32[]{:S(2)}) copy-start(f32[2,32,4,16,128]{4,3,2,1,0:T(8,128)} %param.9) | copy-start | bytes 6291460
  17.1 1.6 %copy-start.1 = (f32[2,32,4,16,128]{4,3,2,1,0:T(8,128)S(1)}, f32[2,32,4,16,128]{4,3,2,1,0:T(8,128)}, u32[]{:S(2)}) copy-start(f32[2,32,4,16,128]{4,3,2,1,0:T(8,128)} %param.10) | copy-start | bytes 6291460
  18.7 1.6 %copy-start.2 = (f32[2,32,4,16,128]{4,3,2,1,0:T(8,128)S(1)}, f32[2,32,4,16,128]{4,3,2,1,0:T(8,128)}, u32[]{:S(2)}) copy-start(f32[2,32,4,16,128]{4,3,2,1,0:T(8,128)} %param.11) | copy-start | bytes 6291460
  20.3 84.1 %copy-start.9 = (s32[5]{0:T(128)}, s32[5]{0:T(128)S(1)}, u32[]{:S(2)}) copy-start(s32[5]{0:T(128)S(1)} %stack.23.place) | copy-start | bytes 64
  25.3 1.4 %copy-start.3 = (f32[64,4,16,128]{3,2,1,0:T(8,128)}, f32[64,4,16,128]{3,2,1,0:T(8,128)S(1)}, u32[]{:S(2)}) copy-start(f32[64,4,16,128]{3,2,1,0:T(8,128)S(1)} %get-tuple-element.62.base) | copy-start | bytes 6291460
  47.6 12.1 %copy-start.5 = (s32[1,4,32,2048]{3,2,1,0:T(8,128)S(1)}, s32[1,4,32,2048]{3,2,1,0:T(8,128)}, u32[]{:S(2)}) copy-start(s32[1,4,32,2048]{3,2,1,0:T(8,128)} %param.12) | copy-start | bytes 3145732
  47.6 12.1 %copy-start.7 = (bf16[64,2048]{1,0:T(8,128)(2,1)S(1)}, bf16[64,2048]{1,0:T(8,128)(2,1)}, u32[]{:S(2)}) copy-start(bf16[64,2048]{1,0:T(8,128)(2,1)} %constant.33.clone.spread) | copy-start | bytes 786436
  47.6 12.1 %copy-start.8 = (s32[1,4,32,64]{3,2,1,0:T(8,128)S(1)}, s32[1,4,32,64]{3,2,1,0:T(8,128)}, u32[]{:S(2)}) copy-start(s32[1,4,32,64]{3,2,1,0:T(8,128)} %param.13) | copy-start | bytes 98308
  47.6 29.5 %all-to-all-start.1 = ((f32[16,9,8,128]{3,2,1,0:T(8,128)}), f32[16,9,8,128]{3,2,1,0:T(8,128)}, u32[]{:S(2)}, u32[]{:S(2)}) async-start(f32[16,9,8,128]{3,2,1,0:T(8,128)} %x_modes.1), calls=%async_computation.1 | async-start | bytes 1179648 | tf_op jit(solution)/shard_map/all_to_all | solution.py:360
  58.3 1.4 %copy-start.6 = (f32[1,4,32,2048]{3,2,1,0:T(8,128)S(1)}, f32[1,4,32,2048]{3,2,1,0:T(8,128)}, u32[]{:S(2)}) copy-start(f32[1,4,32,2048]{3,2,1,0:T(8,128)} %param.14) | copy-start | bytes 3145732
  59.5 1.6 %collective-permute-start = (f32[8,8,8,128]{3,2,1,0:T(8,128)S(1)}, f32[8,8,8,128]{3,2,1,0:T(8,128)S(1)}, u32[]{:S(2)}, u32[]{:S(2)}) collective-permute-start(f32[8,8,8,128]{3,2,1,0:T(8,128)S(1)} %get-tuple-element.44), channel_id=1, source_target_pairs={{0,1},{1,0},{2,3},{3,2},{4,5},{5,4},{6,7},{7,6},{8,9},{9,8},{10,11... | collective-permute-start | bytes 786440 | tf_op jit(solution)/shard_map/ppermute | solution.py:452
  61.1 0.6 copy-start.10
  81.7 0.7 copy-start.11
  82.4 22.0 %all-to-all-start.2 = ((f32[16,8,8,128]{3,2,1,0:T(8,128)}), f32[16,8,8,128]{3,2,1,0:T(8,128)S(1)}, u32[]{:S(2)}, u32[]{:S(2)}) async-start(f32[16,8,8,128]{3,2,1,0:T(8,128)} %get-tuple-element.54), calls=%async_computation.2 | async-start | bytes 1048576 | tf_op jit(solution)/shard_map/all_to_all | solution.py:360
  85.9 15.3 %collective-permute-start.1 = (f32[2,8,8,128]{3,2,1,0:T(8,128)S(1)}, f32[2,8,8,128]{3,2,1,0:T(8,128)S(1)}, u32[]{:S(2)}, u32[]{:S(2)}) collective-permute-start(f32[2,8,8,128]{3,2,1,0:T(8,128)S(1)} %get-tuple-element.56), channel_id=1, source_target_pairs={{0,2},{2,4},{4,6},{6,32},{32,34},{34,36},{36,38},{38,0},{1,3},{3,5... | collective-permute-start | bytes 196616 | tf_op jit(solution)/shard_map/ppermute | solution.py:466
  86.8 17.6 %collective-permute-start.2 = (f32[2,8,8,128]{3,2,1,0:T(8,128)S(1)}, f32[2,8,8,128]{3,2,1,0:T(8,128)S(1)}, u32[]{:S(2)}, u32[]{:S(2)}) collective-permute-start(f32[2,8,8,128]{3,2,1,0:T(8,128)S(1)} %get-tuple-element.57), channel_id=1, source_target_pairs={{0,4},{2,6},{4,32},{6,34},{32,36},{34,38},{36,0},{38,2},{1,5},{3,7... | collective-permute-start | bytes 196616 | tf_op jit(solution)/shard_map/ppermute | solution.py:466
  88.8 15.5 %collective-permute-start.3 = (f32[2,8,8,128]{3,2,1,0:T(8,128)S(1)}, f32[2,8,8,128]{3,2,1,0:T(8,128)S(1)}, u32[]{:S(2)}, u32[]{:S(2)}) collective-permute-start(f32[2,8,8,128]{3,2,1,0:T(8,128)S(1)} %get-tuple-element.58), channel_id=1, source_target_pairs={{0,36},{2,38},{4,0},{6,2},{32,4},{34,6},{36,32},{38,34},{1,37},{3,... | collective-permute-start | bytes 196616 | tf_op jit(solution)/shard_map/ppermute | solution.py:466
  90.3 14.0 %collective-permute-start.4 = (f32[2,8,8,128]{3,2,1,0:T(8,128)S(1)}, f32[2,8,8,128]{3,2,1,0:T(8,128)S(1)}, u32[]{:S(2)}, u32[]{:S(2)}) collective-permute-start(f32[2,8,8,128]{3,2,1,0:T(8,128)S(1)} %get-tuple-element.59), channel_id=1, source_target_pairs={{0,38},{2,0},{4,2},{6,4},{32,6},{34,32},{36,34},{38,36},{1,39},{3,... | collective-permute-start | bytes 196616 | tf_op jit(solution)/shard_map/ppermute | solution.py:466
  101.2 5.5 %copy-start.14 = (f32[2,8,8,128]{3,2,1,0:T(8,128)}, f32[2,8,8,128]{3,2,1,0:T(8,128)S(1)}, u32[]{:S(2)}) copy-start(f32[2,8,8,128]{3,2,1,0:T(8,128)S(1)} %collective-permute-done.1.refs_1_) | copy-start | bytes 196612
  104.4 2.3 %copy-start.15 = (f32[2,8,8,128]{3,2,1,0:T(8,128)}, f32[2,8,8,128]{3,2,1,0:T(8,128)S(1)}, u32[]{:S(2)}) copy-start(f32[2,8,8,128]{3,2,1,0:T(8,128)S(1)} %collective-permute-done.2.refs_2_) | copy-start | bytes 196612
  104.4 2.3 %copy-start.16 = (f32[2,8,8,128]{3,2,1,0:T(8,128)}, f32[2,8,8,128]{3,2,1,0:T(8,128)S(1)}, u32[]{:S(2)}) copy-start(f32[2,8,8,128]{3,2,1,0:T(8,128)S(1)} %collective-permute-done.3.refs_6_) | copy-start | bytes 196612
  104.4 2.3 %copy-start.17 = (f32[2,8,8,128]{3,2,1,0:T(8,128)}, f32[2,8,8,128]{3,2,1,0:T(8,128)S(1)}, u32[]{:S(2)}) copy-start(f32[2,8,8,128]{3,2,1,0:T(8,128)S(1)} %collective-permute-done.4.refs_7_) | copy-start | bytes 196612
  106.7 21.9 %all-to-all-start.3 = ((f32[16,17,8,128]{3,2,1,0:T(8,128)}), f32[16,17,8,128]{3,2,1,0:T(8,128)S(1)}, u32[]{:S(2)}, u32[]{:S(2)}) async-start(f32[16,17,8,128]{3,2,1,0:T(8,128)} %x_cells.1), calls=%async_computation.3 | async-start | bytes 2228224 | tf_op jit(solution)/shard_map/all_to_all | solution.py:360
  110.4 18.2 %copy-start.4 = (f32[64,4,16,128]{3,2,1,0:T(8,128)S(1)}, f32[64,4,16,128]{3,2,1,0:T(8,128)}, u32[]{:S(2)}) copy-start(f32[64,4,16,128]{3,2,1,0:T(8,128)} %copy-done.3) | copy-start | bytes 6291460
  110.4 7.8 %collective-permute-start.5 = (f32[2,8,8,128]{3,2,1,0:T(8,128)S(1)}, f32[2,8,8,128]{3,2,1,0:T(8,128)S(1)}, u32[]{:S(2)}, u32[]{:S(2)}) collective-permute-start(f32[2,8,8,128]{3,2,1,0:T(8,128)S(1)} %get-tuple-element.70), channel_id=1, source_target_pairs={{0,6},{2,32},{4,34},{6,36},{32,38},{34,0},{36,2},{38,4},{1,7},{3,3... | collective-permute-start | bytes 196616 | tf_op jit(solution)/shard_map/ppermute | solution.py:466
  113.8 10.0 %collective-permute-start.6 = (f32[2,8,8,128]{3,2,1,0:T(8,128)S(1)}, f32[2,8,8,128]{3,2,1,0:T(8,128)S(1)}, u32[]{:S(2)}, u32[]{:S(2)}) collective-permute-start(f32[2,8,8,128]{3,2,1,0:T(8,128)S(1)} %get-tuple-element.71), channel_id=1, source_target_pairs={{0,32},{2,34},{4,36},{6,38},{32,0},{34,2},{36,4},{38,6},{1,33},{3,... | collective-permute-start | bytes 196616 | tf_op jit(solution)/shard_map/ppermute | solution.py:466
  114.5 9.3 %collective-permute-start.7 = (f32[2,8,8,128]{3,2,1,0:T(8,128)S(1)}, f32[2,8,8,128]{3,2,1,0:T(8,128)S(1)}, u32[]{:S(2)}, u32[]{:S(2)}) collective-permute-start(f32[2,8,8,128]{3,2,1,0:T(8,128)S(1)} %get-tuple-element.72), channel_id=1, source_target_pairs={{0,34},{2,36},{4,38},{6,0},{32,2},{34,4},{36,6},{38,32},{1,35},{3,... | collective-permute-start | bytes 196616 | tf_op jit(solution)/shard_map/ppermute | solution.py:466
  118.2 5.6 %copy-start.18 = (f32[2,8,8,128]{3,2,1,0:T(8,128)}, f32[2,8,8,128]{3,2,1,0:T(8,128)S(1)}, u32[]{:S(2)}) copy-start(f32[2,8,8,128]{3,2,1,0:T(8,128)S(1)} %collective-permute-done.5.refs_3_) | copy-start | bytes 196612
  123.8 0.6 copy-start.19
  123.8 0.6 copy-start.20

commit v5 on v4

--- a/solution.py
+++ b/solution.py
@@ -169,8 +169,7 @@
     return mm(table, jnp.concatenate(cells, 1))
 
 
-def x_kernel(place, arrived, sums, message):
-    message[:, 8] = jnp.broadcast_to(sums[...][None], (16, 8, 128))
+def x_kernel(place, arrived, message):
     table = x_table(place[0])
     for j in range(0, 8, 2):
         modes = along_x(table, arrived, j)
@@ -210,11 +209,10 @@
     return jnp.concatenate(real, 0), jnp.concatenate(imag, 0)
 
 
-def mode_kernel(place, weight, arrived, g_there, message, sums, g_hat, sent):
-    sums[...] = jnp.sum(arrived[:, 8], axis=0)
-    sources = arrived.reshape(1152, 128)
+def mode_kernel(place, weight, arrived, g_there, message, g_hat, sent):
+    sources = arrived.reshape(1024, 128)
     table = y_table(lambda source: source & 7)
-    g_real, g_imag = along_y(table, [(sources, 72 * peer) for peer in range(16)])
+    g_real, g_imag = along_y(table, [(sources, 64 * peer) for peer in range(16)])
     g_hat[0] = g_real
     g_hat[1] = g_imag
     store = pltpu.make_async_copy(g_hat, g_there, sent)
@@ -392,10 +390,14 @@
         out_specs=[field, whole(8, 128)],
         out_shape=[shaped(64, 4, 16, 128), shaped(8, 128)],
         scratch_shapes=[pltpu.VMEM((64, 64), F32), pltpu.VMEM((1024, 128), F32)],
-        compiler_params=params(2),
+        compiler_params=params(2, 60),
         cost_estimate=cost(1 << 30, 8 * mega),
         name="local",
     )(both, layer, pre, slope_in)
+
+    for axes, size, bit in (("co", 2, 1), ("zl", 4, 1), ("zl", 4, 2), ("zh", 2, 1)):
+        sums = sums + lax.ppermute(sums, axes, [(i, i ^ bit) for i in range(size)])
+    arrived, sums = lax.optimization_barrier((arrived, sums))
 
     spread = np.kron(np.eye(64, dtype=np.float32), np.ones((1, 32), np.float32))
     column = pl.BlockSpec((128, 512), lambda i: (0, i))
@@ -432,12 +434,12 @@
 
     message = pl.pallas_call(
         x_kernel,
-        grid_spec=placed([one_field(1), whole(8, 128)], whole(16, 9, 8, 128)),
-        out_shape=shaped(16, 9, 8, 128),
+        grid_spec=placed([one_field(1)], whole(16, 8, 8, 128)),
+        out_shape=shaped(16, 8, 8, 128),
         compiler_params=params(1),
         cost_estimate=cost(1 << 29, 2 * mega),
         name="x_modes",
-    )(place, arrived, sums)
+    )(place, arrived)
     keep, give = pl.pallas_call(
         x_side_kernel,
         grid_spec=placed(
@@ -467,14 +469,14 @@
 
     sent = {0: pairs[0]}
     weight, sent, pairs = lax.optimization_barrier((weight, sent, pairs))
-    g_hat, message, sums = pl.pallas_call(
+    g_hat, message = pl.pallas_call(
         mode_kernel,
         grid_spec=placed(
-            [whole(128, 2048), whole(16, 9, 8, 128)],
-            [in_hbm, whole(16, 8, 8, 128), whole(8, 128)],
+            [whole(128, 2048), whole(16, 8, 8, 128)],
+            [in_hbm, whole(16, 8, 8, 128)],
             [pltpu.VMEM((2, 128, 128), F32), pltpu.SemaphoreType.DMA],
         ),
-        out_shape=[shaped(2, 128, 128), shaped(16, 8, 8, 128), shaped(8, 128)],
+        out_shape=[pltpu.HBM((2, 128, 128), F32), shaped(16, 8, 8, 128)],
         compiler_params=params(1),
         cost_estimate=cost(1 << 30, 3 * mega),
         name="modes",

time: 133 us -> 132 us (level); the launches traced: 133 us -> 130 us
  waiting for transfers between devices: 53.7 us -> 41.5 us
  starting transfers between devices: 38.6 us -> 50 us
  local copies, waits for them, and re-layouts: 8.25 us -> 3.37 us
  Pallas kernels: 31 us -> 33.2 us
    all_to_all x4, waiting for transfers between devices: 34.4 us -> 19.8 us  [exchange(): lax.all_to_all(message, axes, split_axis=0, concat_axis=0, tiled=True)]
    ppermute x0 -> x4, starting transfers between devices: none -> 11.8 us  [per_device(): sums = sums + lax.ppermute(sums, axes, [(i, i ^ bit) for i in range(size)])]
    unnamed x42 -> x32, local copies, waits for them, and re-layouts: 8.07 us -> 2.57 us
    ppermute x0 -> x4, waiting for transfers between devices: none -> 4.46 us  [per_device(): sums = sums + lax.ppermute(sums, axes, [(i, i ^ bit) for i in range(size)])]
    pallas_call x1, Pallas kernels: 4.99 us -> 7.2 us  [per_device(): pl.pallas_call(local_kernel, grid=(2, 2), in_specs=[whole(64, 64), field,...]
    ppermute x7, waiting for transfers between devices: 19.2 us -> 17.2 us  [hop(): return lax.ppermute(pairs[step], ('zh', 'zl'), route)]
  transfers between devices with their start and end apart: 12 -> 16, of which waited for: 7 -> 12; matrix products, arithmetic and copies ran while one was open for 0% -> 1% of each run, Pallas kernels for 9% -> 11%
where the time goes in v5:
time: 132 us; the launch traced here: 130 us
  starting transfers between devices  50 us (38%)
  waiting for transfers between devices  41.5 us (31%)
  Pallas kernels  33.2 us (25%)
  local copies, waits for them, and re-layouts  3.37 us (3%)
    all_to_all x4, starting transfers between devices, exchange(): lax.all_to_all(message, axes, split_axis=0, concat_axis=0, tiled=True)  25.7 us
    all_to_all x4, waiting for transfers between devices, exchange(): lax.all_to_all(message, axes, split_axis=0, concat_axis=0, tiled=True)  19.8 us
    ppermute x7, waiting for transfers between devices, hop(): return lax.ppermute(pairs[step], ('zh', 'zl'), route)  17.2 us
    ppermute x7, starting transfers between devices, hop(): return lax.ppermute(pairs[step], ('zh', 'zl'), route)  12.3 us
    ppermute x4, starting transfers between devices, per_device(): sums = sums + lax.ppermute(sums, axes, [(i, i ^ bit) for i in range(size)])  11.8 us
    pallas_call x1, Pallas kernels, per_device(): pl.pallas_call(local_kernel, grid=(2, 2), in_specs=[whole(64, 64), field,...  7.2 us
    pallas_call x1, Pallas kernels, per_device(): pl.pallas_call(front_kernel, grid=(2, 2), in_specs=[field, field, field],...  6.87 us
    pallas_call x1, Pallas kernels, per_device(): pl.pallas_call(mode_kernel, grid_spec=placed([whole(128, 2048), whole(16,...  4.7 us
  transfers between devices with their start and end apart: 16, of which 12 were waited for; matrix products, arithmetic and copies ran while one was open for 1% of the time, Pallas kernels for 11%

profile of v5, /device:TPU:1, one launch (start us, length us, event | category | flops | bytes accessed | tf_op | source)
XLA Modules:
  0.0 129.7 jit_solution(5411696658614874697)
XLA Ops:
  0.6 6.9 %front.1 = f32[16,2,2,64,128]{4,3,2,1,0:T(8,128)} custom-call(f32[64,4,16,128]{3,2,1,0:T(8,128)} %bitcast.17, f32[64,4,16,128]{3,2,1,0:T(8,128)} %bitcast.19, f32[64,4,16,128]{3,2,1,0:T(8,128)} %bitcast.21), custom_call_target="tpu_custom_call" | custom-call | flops 1073741824 | bytes 10485760 | tf_op jit(solution)/shard_map/front/pallas_call | solution.py:371
  7.5 0.0 copy-start.7
  7.5 0.0 copy-start.8
  7.5 7.7 %all-to-all-start = ((f32[16,2,2,64,128]{4,3,2,1,0:T(8,128)}), f32[16,2,2,64,128]{4,3,2,1,0:T(8,128)S(1)}, u32[]{:S(2)}, u32[]{:S(2)}) async-start(f32[16,2,2,64,128]{4,3,2,1,0:T(8,128)} %front.1), calls=%async_computation | async-start | bytes 4194304 | tf_op jit(solution)/shard_map/all_to_all | solution.py:358
  15.2 0.0 copy-done.7
  15.2 0.0 copy-done.8
  15.3 0.7 reshape.46.point
  16.0 7.2 %local.1 = (f32[64,4,16,128]{3,2,1,0:T(8,128)}, f32[8,128]{1,0:T(8,128)}) custom-call(f32[64,64]{1,0:T(8,128)} %reshape.46.point, f32[64,4,16,128]{3,2,1,0:T(8,128)} %bitcast.18, f32[64,4,16,128]{3,2,1,0:T(8,128)} %bitcast.20, f32[64,4,16,128]{3,2,1,0:T(8,128)} %bitcast.22), custom_call_target="tpu_custom_call" | custom-call | flops 1073741824 | bytes 8388608 | tf_op jit(solution)/shard_map/local/pallas_call | solution.py:386
  23.2 1.0 collective-permute-start
  24.2 1.0 collective-permute-done
  25.2 0.7 add.28
  25.9 1.6 %collective-permute-start.1 = (f32[8,128]{1,0:T(8,128)S(1)}, f32[8,128]{1,0:T(8,128)S(1)}, u32[]{:S(2)}, u32[]{:S(2)}) collective-permute-start(f32[8,128]{1,0:T(8,128)S(1)} %add.28), channel_id=1, source_target_pairs={{0,2},{2,0},{4,6},{6,4},{1,3},{3,1},{5,7},{7,5},{8,10},{10,8},{12,... | collective-permute-start | bytes 12296 | tf_op jit(solution)/shard_map/ppermute | solution.py:399
  27.5 1.3 collective-permute-done.1
  28.8 3.0 %collective-permute-start.2 = (f32[8,128]{1,0:T(8,128)S(1)}, f32[8,128]{1,0:T(8,128)S(1)}, u32[]{:S(2)}, u32[]{:S(2)}) collective-permute-start(f32[8,128]{1,0:T(8,128)S(1)} %add.29), channel_id=1, source_target_pairs={{0,4},{2,6},{4,0},{6,2},{1,5},{3,7},{5,1},{7,3},{8,12},{10,14},{12... | collective-permute-start | bytes 12296 | tf_op jit(solution)/shard_map/ppermute | solution.py:399
  31.8 1.2 collective-permute-done.2
  33.0 6.2 %collective-permute-start.3 = (f32[8,128]{1,0:T(8,128)S(1)}, f32[8,128]{1,0:T(8,128)S(1)}, u32[]{:S(2)}, u32[]{:S(2)}) collective-permute-start(f32[8,128]{1,0:T(8,128)S(1)} %add.30), channel_id=1, source_target_pairs={{0,32},{32,0},{1,33},{33,1},{2,34},{34,2},{3,35},{35,3},{4,36},{36... | collective-permute-start | bytes 12296 | tf_op jit(solution)/shard_map/ppermute | solution.py:399
  39.2 0.1 stack.23.place
  39.3 0.9 collective-permute-done.3
  40.2 5.5 %all-to-all-done.arrived = f32[16,2,2,64,128]{4,3,2,1,0:T(8,128)S(1)} async-done(((f32[16,2,2,64,128]{4,3,2,1,0:T(8,128)}), f32[16,2,2,64,128]{4,3,2,1,0:T(8,128)S(1)}, u32[]{:S(2)}, u32[]{:S(2)}) %all-to-all-start) | async-done | bytes 2097184 | tf_op jit(solution)/shard_map/all_to_all | solution.py:358
  45.7 1.9 %x_modes.1 = f32[16,8,8,128]{3,2,1,0:T(8,128)} custom-call(s32[5]{0:T(128)S(1)} %stack.23.place, f32[16,2,2,64,128]{4,3,2,1,0:T(8,128)S(1)} %all-to-all-done.arrived), custom_call_target="tpu_custom_call" | custom-call | flops 536870912 | bytes 2097152 | tf_op jit(solution)/shard_map/x_modes/pallas_call | solution.py:435
  47.6 10.8 %all-to-all-start.1 = ((f32[16,8,8,128]{3,2,1,0:T(8,128)}), f32[16,8,8,128]{3,2,1,0:T(8,128)}, u32[]{:S(2)}, u32[]{:S(2)}) async-start(f32[16,8,8,128]{3,2,1,0:T(8,128)} %x_modes.1), calls=%async_computation.1 | async-start | bytes 1048576 | tf_op jit(solution)/shard_map/all_to_all | solution.py:358
  58.3 1.1 x_side.1
  59.5 0.2 collective-permute-start.4
  59.7 0.0 copy-done.1
  59.7 0.0 copy-done.3
  59.7 0.0 copy-done.4
  59.7 0.0 copy-done.2
  59.7 1.3 %weight.1 = f32[128,2048]{1,0:T(8,128)S(1)} custom-call(bf16[64,2048]{1,0:T(8,128)(2,1)S(1)} %copy-done.3, s32[128,2048]{1,0:T(8,128)S(1)} %bitcast.14, s32[128,64]{1,0:T(8,128)S(1)} %bitcast.16, f32[128,2048]{1,0:T(8,128)S(1)} %bitcast.15), custom_call_target="tpu_custom_call" | custom-call | flops 134217728 | bytes 3145728 | tf_op jit(solution)/shard_map/weight/pallas_call | solution.py:405
  61.0 0.1 collective-permute-done.4.got
  61.1 0.0 copy-start.6
  61.1 0.6 copy-done.6
  61.7 14.0 %all-to-all-done.1.arrived = f32[16,8,8,128]{3,2,1,0:T(8,128)} async-done(((f32[16,8,8,128]{3,2,1,0:T(8,128)}), f32[16,8,8,128]{3,2,1,0:T(8,128)}, u32[]{:S(2)}, u32[]{:S(2)}) %all-to-all-start.1) | async-done | bytes 524320 | tf_op jit(solution)/shard_map/all_to_all | solution.py:358
  75.7 4.7 %modes.1 = (f32[2,128,128]{2,1,0:T(8,128)}, f32[16,8,8,128]{3,2,1,0:T(8,128)}) custom-call(s32[5]{0:T(128)S(1)} %stack.23.place, f32[128,2048]{1,0:T(8,128)S(1)} %weight.1, f32[16,8,8,128]{3,2,1,0:T(8,128)} %all-to-all-done.1.arrived), custom_call_target="tpu_custom_call" | custom-call | flops 1073741824 | bytes 3145728 | tf_op jit(solution)/shard_map/modes/pallas_call | solution.py:472
  80.5 3.5 %all-to-all-start.2 = ((f32[16,8,8,128]{3,2,1,0:T(8,128)}), f32[16,8,8,128]{3,2,1,0:T(8,128)S(1)}, u32[]{:S(2)}, u32[]{:S(2)}) async-start(f32[16,8,8,128]{3,2,1,0:T(8,128)} %get-tuple-element.57), calls=%async_computation.2 | async-start | bytes 1048576 | tf_op jit(solution)/shard_map/all_to_all | solution.py:358
  83.9 0.8 collective-permute-start.5
  84.8 2.1 %collective-permute-start.6 = (f32[2,8,8,128]{3,2,1,0:T(8,128)S(1)}, f32[2,8,8,128]{3,2,1,0:T(8,128)S(1)}, u32[]{:S(2)}, u32[]{:S(2)}) collective-permute-start(f32[2,8,8,128]{3,2,1,0:T(8,128)S(1)} %get-tuple-element.60), channel_id=1, source_target_pairs={{0,4},{2,6},{4,32},{6,34},{32,36},{34,38},{36,0},{38,2},{1,5},{3,7... | collective-permute-start | bytes 196616 | tf_op jit(solution)/shard_map/ppermute | solution.py:468
  86.8 1.5 %collective-permute-start.7 = (f32[2,8,8,128]{3,2,1,0:T(8,128)S(1)}, f32[2,8,8,128]{3,2,1,0:T(8,128)S(1)}, u32[]{:S(2)}, u32[]{:S(2)}) collective-permute-start(f32[2,8,8,128]{3,2,1,0:T(8,128)S(1)} %get-tuple-element.61), channel_id=1, source_target_pairs={{0,36},{2,38},{4,0},{6,2},{32,4},{34,6},{36,32},{38,34},{1,37},{3,... | collective-permute-start | bytes 196616 | tf_op jit(solution)/shard_map/ppermute | solution.py:468
  88.3 0.7 collective-permute-start.8
  89.1 10.1 %collective-permute-done.5.refs_1_ = f32[2,8,8,128]{3,2,1,0:T(8,128)S(1)} collective-permute-done((f32[2,8,8,128]{3,2,1,0:T(8,128)S(1)}, f32[2,8,8,128]{3,2,1,0:T(8,128)S(1)}, u32[]{:S(2)}, u32[]{:S(2)}) %collective-permute-start.5) | collective-permute-done | bytes 65568 | tf_op jit(solution)/shard_map/ppermute | solution.py:468
  99.2 3.2 %collective-permute-done.6.refs_2_ = f32[2,8,8,128]{3,2,1,0:T(8,128)S(1)} collective-permute-done((f32[2,8,8,128]{3,2,1,0:T(8,128)S(1)}, f32[2,8,8,128]{3,2,1,0:T(8,128)S(1)}, u32[]{:S(2)}, u32[]{:S(2)}) %collective-permute-start.6) | collective-permute-done | bytes 65568 | tf_op jit(solution)/shard_map/ppermute | solution.py:468
  102.4 0.0 collective-permute-done.7.refs_6_
  102.4 0.0 collective-permute-done.8.refs_7_
  102.4 0.6 copy-done.11
  103.0 0.6 copy-done.12
  103.7 0.0 all-to-all-done.2.arrived
  103.7 0.0 copy-done.5
  103.7 2.2 %x_cells.1 = f32[16,17,8,128]{3,2,1,0:T(8,128)} custom-call(s32[5]{0:T(128)S(1)} %stack.23.place, f32[16,8,8,128]{3,2,1,0:T(8,128)S(1)} %all-to-all-done.2.arrived, f32[8,128]{1,0:T(8,128)S(1)} %add.31.sums), custom_call_target="tpu_custom_call" | custom-call | flops 536870912 | bytes 2097152 | tf_op jit(solution)/shard_map/x_cells/pallas_call | solution.py:488
  105.9 0.0 copy-done.9
  105.9 0.0 copy-done.10
  105.9 3.7 %all-to-all-start.3 = ((f32[16,17,8,128]{3,2,1,0:T(8,128)}), f32[16,17,8,128]{3,2,1,0:T(8,128)S(1)}, u32[]{:S(2)}, u32[]{:S(2)}) async-start(f32[16,17,8,128]{3,2,1,0:T(8,128)} %x_cells.1), calls=%async_computation.3 | async-start | bytes 2228224 | tf_op jit(solution)/shard_map/all_to_all | solution.py:358
  109.6 0.0 copy-start
  109.6 3.0 %collective-permute-start.9 = (f32[2,8,8,128]{3,2,1,0:T(8,128)S(1)}, f32[2,8,8,128]{3,2,1,0:T(8,128)S(1)}, u32[]{:S(2)}, u32[]{:S(2)}) collective-permute-start(f32[2,8,8,128]{3,2,1,0:T(8,128)S(1)} %get-tuple-element.72), channel_id=1, source_target_pairs={{0,6},{2,32},{4,34},{6,36},{32,38},{34,0},{36,2},{38,4},{1,7},{3,3... | collective-permute-start | bytes 196616 | tf_op jit(solution)/shard_map/ppermute | solution.py:468
  112.6 1.3 %collective-permute-start.10 = (f32[2,8,8,128]{3,2,1,0:T(8,128)S(1)}, f32[2,8,8,128]{3,2,1,0:T(8,128)S(1)}, u32[]{:S(2)}, u32[]{:S(2)}) collective-permute-start(f32[2,8,8,128]{3,2,1,0:T(8,128)S(1)} %get-tuple-element.73), channel_id=1, source_target_pairs={{0,32},{2,34},{4,36},{6,38},{32,0},{34,2},{36,4},{38,6},{1,33},{3,... | collective-permute-start | bytes 196616 | tf_op jit(solution)/shard_map/ppermute | solution.py:468
  113.9 2.9 %collective-permute-start.11 = (f32[2,8,8,128]{3,2,1,0:T(8,128)S(1)}, f32[2,8,8,128]{3,2,1,0:T(8,128)S(1)}, u32[]{:S(2)}, u32[]{:S(2)}) collective-permute-start(f32[2,8,8,128]{3,2,1,0:T(8,128)S(1)} %get-tuple-element.74), channel_id=1, source_target_pairs={{0,34},{2,36},{4,38},{6,0},{32,2},{34,4},{36,6},{38,32},{1,35},{3,... | collective-permute-start | bytes 196616 | tf_op jit(solution)/shard_map/ppermute | solution.py:468
  116.8 0.0 collective-permute-done.9.refs_3_
  116.8 3.2 %collective-permute-done.10.refs_4_ = f32[2,8,8,128]{3,2,1,0:T(8,128)S(1)} collective-permute-done((f32[2,8,8,128]{3,2,1,0:T(8,128)S(1)}, f32[2,8,8,128]{3,2,1,0:T(8,128)S(1)}, u32[]{:S(2)}, u32[]{:S(2)}) %collective-permute-start.10) | collective-permute-done | bytes 65568 | tf_op jit(solution)/shard_map/ppermute | solution.py:468
  120.0 0.7 collective-permute-done.11.refs_5_
  120.7 0.0 copy-done.13
  120.7 0.0 copy-done.14
  120.7 0.6 copy-done.15
  121.3 4.1 %outer.1 = f32[128,2048]{1,0:T(8,128)} custom-call(s32[5]{0:T(128)} %copy-done.5, f32[2,8,8,128]{3,2,1,0:T(8,128)} %copy-done.6, f32[2,8,8,128]{3,2,1,0:T(8,128)} %copy-done.9, f32[2,8,8,128]{3,2,1,0:T(8,128)} %copy-done.10, f32[2,8,8,128]{3,2,1,0:T(8,128)} %copy-done.13, f32[2,8,8,128]{3,2,1,0:T(8,128)} %copy-done.14, f32[2,8,8,128]{3,2,1,0:T(8,128)} %copy-done.15, ...), custom_call_target="tpu_custom_call" | custom-call | flops 1073741824 | bytes 4194304 | tf_op jit(solution)/shard_map/outer/pallas_call | solution.py:500
  125.4 0.4 all-to-all-done.3.arrived.sums
  125.8 0.0 copy-done
  125.8 3.8 %end.1 = (f32[64,4,16,128]{3,2,1,0:T(8,128)}, f32[32,32]{1,0:T(8,128)}, f32[1,32]{1,0:T(1,128)}) custom-call(f32[16,17,8,128]{3,2,1,0:T(8,128)S(1)} %all-to-all-done.3.arrived.sums, f32[16,17,8,128]{3,2,1,0:T(8,128)S(1)} %all-to-all-done.3.arrived.sums, f32[64,4,16,128]{3,2,1,0:T(8,128)S(1)} %copy-done), custom_call_target="tpu_custom_call" | custom-call | flops 536870912 | bytes 5242880 | tf_op jit(solution)/shard_map/end/pallas_call | solution.py:509
  (17 shorter events, 0.1 us)
Async XLA Ops:
  7.5 7.7 %copy-start.7 = (f32[2,32,2,32]{3,2,1,0:T(2,128)S(1)}, f32[2,32,2,32]{3,2,1,0:T(2,128)}, u32[]{:S(2)}) copy-start(f32[2,32,2,32]{3,2,1,0:T(2,128)} %constant.40) | copy-start | bytes 49156
  7.5 7.7 %copy-start.8 = (f32[32,32]{1,0:T(8,128)S(1)}, f32[32,32]{1,0:T(8,128)}, u32[]{:S(2)}) copy-start(f32[32,32]{1,0:T(8,128)} %param.15) | copy-start | bytes 12292
  7.5 38.2 %all-to-all-start = ((f32[16,2,2,64,128]{4,3,2,1,0:T(8,128)}), f32[16,2,2,64,128]{4,3,2,1,0:T(8,128)S(1)}, u32[]{:S(2)}, u32[]{:S(2)}) async-start(f32[16,2,2,64,128]{4,3,2,1,0:T(8,128)} %front.1), calls=%async_computation | async-start | bytes 4194304 | tf_op jit(solution)/shard_map/all_to_all | solution.py:358
  23.2 2.0 %collective-permute-start = (f32[8,128]{1,0:T(8,128)}, f32[8,128]{1,0:T(8,128)S(1)}, u32[]{:S(2)}, u32[]{:S(2)}) collective-permute-start(f32[8,128]{1,0:T(8,128)} %get-tuple-element.42), channel_id=1, source_target_pairs={{0,1},{1,0},{2,3},{3,2},{4,5},{5,4},{6,7},{7,6},{8,9},{9,8},{10,11... | collective-permute-start | bytes 12296 | tf_op jit(solution)/shard_map/ppermute | solution.py:399
  25.9 2.9 %collective-permute-start.1 = (f32[8,128]{1,0:T(8,128)S(1)}, f32[8,128]{1,0:T(8,128)S(1)}, u32[]{:S(2)}, u32[]{:S(2)}) collective-permute-start(f32[8,128]{1,0:T(8,128)S(1)} %add.28), channel_id=1, source_target_pairs={{0,2},{2,0},{4,6},{6,4},{1,3},{3,1},{5,7},{7,5},{8,10},{10,8},{12,... | collective-permute-start | bytes 12296 | tf_op jit(solution)/shard_map/ppermute | solution.py:399
  28.8 4.2 %collective-permute-start.2 = (f32[8,128]{1,0:T(8,128)S(1)}, f32[8,128]{1,0:T(8,128)S(1)}, u32[]{:S(2)}, u32[]{:S(2)}) collective-permute-start(f32[8,128]{1,0:T(8,128)S(1)} %add.29), channel_id=1, source_target_pairs={{0,4},{2,6},{4,0},{6,2},{1,5},{3,7},{5,1},{7,3},{8,12},{10,14},{12... | collective-permute-start | bytes 12296 | tf_op jit(solution)/shard_map/ppermute | solution.py:399
  33.0 7.2 %collective-permute-start.3 = (f32[8,128]{1,0:T(8,128)S(1)}, f32[8,128]{1,0:T(8,128)S(1)}, u32[]{:S(2)}, u32[]{:S(2)}) collective-permute-start(f32[8,128]{1,0:T(8,128)S(1)} %add.30), channel_id=1, source_target_pairs={{0,32},{32,0},{1,33},{33,1},{2,34},{34,2},{3,35},{35,3},{4,36},{36... | collective-permute-start | bytes 12296 | tf_op jit(solution)/shard_map/ppermute | solution.py:399
  39.3 64.4 %copy-start.5 = (s32[5]{0:T(128)}, s32[5]{0:T(128)S(1)}, u32[]{:S(2)}) copy-start(s32[5]{0:T(128)S(1)} %stack.23.place) | copy-start | bytes 64
  47.6 12.1 %copy-start.1 = (s32[1,4,32,2048]{3,2,1,0:T(8,128)S(1)}, s32[1,4,32,2048]{3,2,1,0:T(8,128)}, u32[]{:S(2)}) copy-start(s32[1,4,32,2048]{3,2,1,0:T(8,128)} %param.12) | copy-start | bytes 3145732
  47.6 12.1 %copy-start.3 = (bf16[64,2048]{1,0:T(8,128)(2,1)S(1)}, bf16[64,2048]{1,0:T(8,128)(2,1)}, u32[]{:S(2)}) copy-start(bf16[64,2048]{1,0:T(8,128)(2,1)} %constant.33.clone.spread) | copy-start | bytes 786436
  47.6 12.1 %copy-start.4 = (s32[1,4,32,64]{3,2,1,0:T(8,128)S(1)}, s32[1,4,32,64]{3,2,1,0:T(8,128)}, u32[]{:S(2)}) copy-start(s32[1,4,32,64]{3,2,1,0:T(8,128)} %param.13) | copy-start | bytes 98308
  47.6 28.2 %all-to-all-start.1 = ((f32[16,8,8,128]{3,2,1,0:T(8,128)}), f32[16,8,8,128]{3,2,1,0:T(8,128)}, u32[]{:S(2)}, u32[]{:S(2)}) async-start(f32[16,8,8,128]{3,2,1,0:T(8,128)} %x_modes.1), calls=%async_computation.1 | async-start | bytes 1048576 | tf_op jit(solution)/shard_map/all_to_all | solution.py:358
  58.3 1.4 %copy-start.2 = (f32[1,4,32,2048]{3,2,1,0:T(8,128)S(1)}, f32[1,4,32,2048]{3,2,1,0:T(8,128)}, u32[]{:S(2)}) copy-start(f32[1,4,32,2048]{3,2,1,0:T(8,128)} %param.14) | copy-start | bytes 3145732
  59.5 1.6 %collective-permute-start.4 = (f32[8,8,8,128]{3,2,1,0:T(8,128)S(1)}, f32[8,8,8,128]{3,2,1,0:T(8,128)S(1)}, u32[]{:S(2)}, u32[]{:S(2)}) collective-permute-start(f32[8,8,8,128]{3,2,1,0:T(8,128)S(1)} %get-tuple-element.47), channel_id=1, source_target_pairs={{0,1},{1,0},{2,3},{3,2},{4,5},{5,4},{6,7},{7,6},{8,9},{9,8},{10,11... | collective-permute-start | bytes 786440 | tf_op jit(solution)/shard_map/ppermute | solution.py:454
  61.1 0.6 copy-start.6
  80.5 23.2 %all-to-all-start.2 = ((f32[16,8,8,128]{3,2,1,0:T(8,128)}), f32[16,8,8,128]{3,2,1,0:T(8,128)S(1)}, u32[]{:S(2)}, u32[]{:S(2)}) async-start(f32[16,8,8,128]{3,2,1,0:T(8,128)} %get-tuple-element.57), calls=%async_computation.2 | async-start | bytes 1048576 | tf_op jit(solution)/shard_map/all_to_all | solution.py:358
  83.9 15.3 %collective-permute-start.5 = (f32[2,8,8,128]{3,2,1,0:T(8,128)S(1)}, f32[2,8,8,128]{3,2,1,0:T(8,128)S(1)}, u32[]{:S(2)}, u32[]{:S(2)}) collective-permute-start(f32[2,8,8,128]{3,2,1,0:T(8,128)S(1)} %get-tuple-element.59), channel_id=1, source_target_pairs={{0,2},{2,4},{4,6},{6,32},{32,34},{34,36},{36,38},{38,0},{1,3},{3,5... | collective-permute-start | bytes 196616 | tf_op jit(solution)/shard_map/ppermute | solution.py:468
  84.8 17.6 %collective-permute-start.6 = (f32[2,8,8,128]{3,2,1,0:T(8,128)S(1)}, f32[2,8,8,128]{3,2,1,0:T(8,128)S(1)}, u32[]{:S(2)}, u32[]{:S(2)}) collective-permute-start(f32[2,8,8,128]{3,2,1,0:T(8,128)S(1)} %get-tuple-element.60), channel_id=1, source_target_pairs={{0,4},{2,6},{4,32},{6,34},{32,36},{34,38},{36,0},{38,2},{1,5},{3,7... | collective-permute-start | bytes 196616 | tf_op jit(solution)/shard_map/ppermute | solution.py:468
  86.8 15.5 %collective-permute-start.7 = (f32[2,8,8,128]{3,2,1,0:T(8,128)S(1)}, f32[2,8,8,128]{3,2,1,0:T(8,128)S(1)}, u32[]{:S(2)}, u32[]{:S(2)}) collective-permute-start(f32[2,8,8,128]{3,2,1,0:T(8,128)S(1)} %get-tuple-element.61), channel_id=1, source_target_pairs={{0,36},{2,38},{4,0},{6,2},{32,4},{34,6},{36,32},{38,34},{1,37},{3,... | collective-permute-start | bytes 196616 | tf_op jit(solution)/shard_map/ppermute | solution.py:468
  88.3 14.0 %collective-permute-start.8 = (f32[2,8,8,128]{3,2,1,0:T(8,128)S(1)}, f32[2,8,8,128]{3,2,1,0:T(8,128)S(1)}, u32[]{:S(2)}, u32[]{:S(2)}) collective-permute-start(f32[2,8,8,128]{3,2,1,0:T(8,128)S(1)} %get-tuple-element.62), channel_id=1, source_target_pairs={{0,38},{2,0},{4,2},{6,4},{32,6},{34,32},{36,34},{38,36},{1,39},{3,... | collective-permute-start | bytes 196616 | tf_op jit(solution)/shard_map/ppermute | solution.py:468
  99.2 6.7 %copy-start.9 = (f32[2,8,8,128]{3,2,1,0:T(8,128)}, f32[2,8,8,128]{3,2,1,0:T(8,128)S(1)}, u32[]{:S(2)}) copy-start(f32[2,8,8,128]{3,2,1,0:T(8,128)S(1)} %collective-permute-done.5.refs_1_) | copy-start | bytes 196612
  102.4 3.5 %copy-start.10 = (f32[2,8,8,128]{3,2,1,0:T(8,128)}, f32[2,8,8,128]{3,2,1,0:T(8,128)S(1)}, u32[]{:S(2)}) copy-start(f32[2,8,8,128]{3,2,1,0:T(8,128)S(1)} %collective-permute-done.6.refs_2_) | copy-start | bytes 196612
  102.4 0.7 copy-start.11
  103.0 0.6 copy-start.12
  105.9 19.9 %all-to-all-start.3 = ((f32[16,17,8,128]{3,2,1,0:T(8,128)}), f32[16,17,8,128]{3,2,1,0:T(8,128)S(1)}, u32[]{:S(2)}, u32[]{:S(2)}) async-start(f32[16,17,8,128]{3,2,1,0:T(8,128)} %x_cells.1), calls=%async_computation.3 | async-start | bytes 2228224 | tf_op jit(solution)/shard_map/all_to_all | solution.py:358
  109.6 16.2 %copy-start = (f32[64,4,16,128]{3,2,1,0:T(8,128)S(1)}, f32[64,4,16,128]{3,2,1,0:T(8,128)}, u32[]{:S(2)}) copy-start(f32[64,4,16,128]{3,2,1,0:T(8,128)} %get-tuple-element.64.base) | copy-start | bytes 6291460
  109.6 7.2 %collective-permute-start.9 = (f32[2,8,8,128]{3,2,1,0:T(8,128)S(1)}, f32[2,8,8,128]{3,2,1,0:T(8,128)S(1)}, u32[]{:S(2)}, u32[]{:S(2)}) collective-permute-start(f32[2,8,8,128]{3,2,1,0:T(8,128)S(1)} %get-tuple-element.72), channel_id=1, source_target_pairs={{0,6},{2,32},{4,34},{6,36},{32,38},{34,0},{36,2},{38,4},{1,7},{3,3... | collective-permute-start | bytes 196616 | tf_op jit(solution)/shard_map/ppermute | solution.py:468
  112.6 7.4 %collective-permute-start.10 = (f32[2,8,8,128]{3,2,1,0:T(8,128)S(1)}, f32[2,8,8,128]{3,2,1,0:T(8,128)S(1)}, u32[]{:S(2)}, u32[]{:S(2)}) collective-permute-start(f32[2,8,8,128]{3,2,1,0:T(8,128)S(1)} %get-tuple-element.73), channel_id=1, source_target_pairs={{0,32},{2,34},{4,36},{6,38},{32,0},{34,2},{36,4},{38,6},{1,33},{3,... | collective-permute-start | bytes 196616 | tf_op jit(solution)/shard_map/ppermute | solution.py:468
  113.9 6.8 %collective-permute-start.11 = (f32[2,8,8,128]{3,2,1,0:T(8,128)S(1)}, f32[2,8,8,128]{3,2,1,0:T(8,128)S(1)}, u32[]{:S(2)}, u32[]{:S(2)}) collective-permute-start(f32[2,8,8,128]{3,2,1,0:T(8,128)S(1)} %get-tuple-element.74), channel_id=1, source_target_pairs={{0,34},{2,36},{4,38},{6,0},{32,2},{34,4},{36,6},{38,32},{1,35},{3,... | collective-permute-start | bytes 196616 | tf_op jit(solution)/shard_map/ppermute | solution.py:468
  116.8 3.9 %copy-start.13 = (f32[2,8,8,128]{3,2,1,0:T(8,128)}, f32[2,8,8,128]{3,2,1,0:T(8,128)S(1)}, u32[]{:S(2)}) copy-start(f32[2,8,8,128]{3,2,1,0:T(8,128)S(1)} %collective-permute-done.9.refs_3_) | copy-start | bytes 196612
  120.0 0.7 copy-start.14
  120.7 0.6 copy-start.15

commit v6 on v5

--- a/solution.py
+++ b/solution.py
@@ -457,7 +457,7 @@
         grid=(1,),
         in_specs=[whole(8, 8, 8, 128)] * 2,
         out_specs=[whole(2, 8, 8, 128)] * 8,
-        out_shape=[shaped(2, 8, 8, 128)] * 8,
+        out_shape=[pltpu.HBM((2, 8, 8, 128), F32)] * 8,
         compiler_params=params(1),
         cost_estimate=cost(1 << 20, mega),
         name="pair",

time: 132 us -> 132 us (level)
  local copies, waits for them, and re-layouts: 3.37 us -> 1.51 us
  waiting for transfers between devices: 41.5 us -> 42.9 us
    ppermute x7, waiting for transfers between devices: 17.2 us -> 19.1 us  [hop(): return lax.ppermute(pairs[step], ('zh', 'zl'), route)]
    unnamed x32 -> x44, local copies, waits for them, and re-layouts: 2.57 us -> 0.71 us
  transfers between devices with their start and end apart: 16 -> 16, of which waited for: 12 -> 11; matrix products, arithmetic and copies ran while one was open for 1% -> 1% of each run, Pallas kernels for 11% -> 11%
where the time goes in v6:
time: 132 us; the launch traced here: 131 us
  starting transfers between devices  50.6 us (38%)
  waiting for transfers between devices  42.9 us (32%)
  Pallas kernels  34 us (26%)
  local copies, waits for them, and re-layouts  1.51 us (1%)
    all_to_all x4, starting transfers between devices, exchange(): lax.all_to_all(message, axes, split_axis=0, concat_axis=0, tiled=True)  25.7 us
    all_to_all x4, waiting for transfers between devices, exchange(): lax.all_to_all(message, axes, split_axis=0, concat_axis=0, tiled=True)  19.3 us
    ppermute x7, waiting for transfers between devices, hop(): return lax.ppermute(pairs[step], ('zh', 'zl'), route)  19.1 us
    ppermute x7, starting transfers between devices, hop(): return lax.ppermute(pairs[step], ('zh', 'zl'), route)  12.9 us
    ppermute x4, starting transfers between devices, per_device(): sums = sums + lax.ppermute(sums, axes, [(i, i ^ bit) for i in range(size)])  11.8 us
    pallas_call x1, Pallas kernels, per_device(): pl.pallas_call(local_kernel, grid=(2, 2), in_specs=[whole(64, 64), field,...  7.21 us
    pallas_call x1, Pallas kernels, per_device(): pl.pallas_call(front_kernel, grid=(2, 2), in_specs=[field, field, field],...  6.87 us
    pallas_call x1, Pallas kernels, per_device(): pl.pallas_call(mode_kernel, grid_spec=placed([whole(128, 2048), whole(16,...  4.71 us
  transfers between devices with their start and end apart: 16, of which 11 were waited for; matrix products, arithmetic and copies ran while one was open for 1% of the time, Pallas kernels for 11%

profile of v6, /device:TPU:1, one launch (start us, length us, event | category | flops | bytes accessed | tf_op | source)
XLA Modules:
  0.0 130.8 jit_solution(10626650012274222831)
XLA Ops:
  0.6 6.9 %front.1 = f32[16,2,2,64,128]{4,3,2,1,0:T(8,128)} custom-call(f32[64,4,16,128]{3,2,1,0:T(8,128)} %bitcast.17, f32[64,4,16,128]{3,2,1,0:T(8,128)} %bitcast.19, f32[64,4,16,128]{3,2,1,0:T(8,128)} %bitcast.21), custom_call_target="tpu_custom_call" | custom-call | flops 1073741824 | bytes 10485760 | tf_op jit(solution)/shard_map/front/pallas_call | solution.py:371
  7.5 7.7 %all-to-all-start = ((f32[16,2,2,64,128]{4,3,2,1,0:T(8,128)}), f32[16,2,2,64,128]{4,3,2,1,0:T(8,128)S(1)}, u32[]{:S(2)}, u32[]{:S(2)}) async-start(f32[16,2,2,64,128]{4,3,2,1,0:T(8,128)} %front.1), calls=%async_computation | async-start | bytes 4194304 | tf_op jit(solution)/shard_map/all_to_all | solution.py:358
  15.2 0.0 copy-done.6
  15.2 0.0 copy-done.7
  15.3 0.7 reshape.46.point
  16.0 7.2 %local.1 = (f32[64,4,16,128]{3,2,1,0:T(8,128)}, f32[8,128]{1,0:T(8,128)}) custom-call(f32[64,64]{1,0:T(8,128)} %reshape.46.point, f32[64,4,16,128]{3,2,1,0:T(8,128)} %bitcast.18, f32[64,4,16,128]{3,2,1,0:T(8,128)} %bitcast.20, f32[64,4,16,128]{3,2,1,0:T(8,128)} %bitcast.22), custom_call_target="tpu_custom_call" | custom-call | flops 1073741824 | bytes 8388608 | tf_op jit(solution)/shard_map/local/pallas_call | solution.py:386
  23.2 1.0 collective-permute-start
  24.2 1.0 collective-permute-done
  25.2 0.7 add.28
  25.9 1.6 %collective-permute-start.1 = (f32[8,128]{1,0:T(8,128)S(1)}, f32[8,128]{1,0:T(8,128)S(1)}, u32[]{:S(2)}, u32[]{:S(2)}) collective-permute-start(f32[8,128]{1,0:T(8,128)S(1)} %add.28), channel_id=1, source_target_pairs={{0,2},{2,0},{4,6},{6,4},{1,3},{3,1},{5,7},{7,5},{8,10},{10,8},{12,... | collective-permute-start | bytes 12296 | tf_op jit(solution)/shard_map/ppermute | solution.py:399
  27.5 1.3 collective-permute-done.1
  28.8 3.0 %collective-permute-start.2 = (f32[8,128]{1,0:T(8,128)S(1)}, f32[8,128]{1,0:T(8,128)S(1)}, u32[]{:S(2)}, u32[]{:S(2)}) collective-permute-start(f32[8,128]{1,0:T(8,128)S(1)} %add.29), channel_id=1, source_target_pairs={{0,4},{2,6},{4,0},{6,2},{1,5},{3,7},{5,1},{7,3},{8,12},{10,14},{12... | collective-permute-start | bytes 12296 | tf_op jit(solution)/shard_map/ppermute | solution.py:399
  31.8 1.2 collective-permute-done.2
  33.0 6.2 %collective-permute-start.3 = (f32[8,128]{1,0:T(8,128)S(1)}, f32[8,128]{1,0:T(8,128)S(1)}, u32[]{:S(2)}, u32[]{:S(2)}) collective-permute-start(f32[8,128]{1,0:T(8,128)S(1)} %add.30), channel_id=1, source_target_pairs={{0,32},{32,0},{1,33},{33,1},{2,34},{34,2},{3,35},{35,3},{4,36},{36... | collective-permute-start | bytes 12296 | tf_op jit(solution)/shard_map/ppermute | solution.py:399
  39.2 0.1 stack.23.place
  39.3 0.9 collective-permute-done.3
  40.2 5.5 %all-to-all-done.arrived = f32[16,2,2,64,128]{4,3,2,1,0:T(8,128)S(1)} async-done(((f32[16,2,2,64,128]{4,3,2,1,0:T(8,128)}), f32[16,2,2,64,128]{4,3,2,1,0:T(8,128)S(1)}, u32[]{:S(2)}, u32[]{:S(2)}) %all-to-all-start) | async-done | bytes 2097184 | tf_op jit(solution)/shard_map/all_to_all | solution.py:358
  45.7 1.9 %x_modes.1 = f32[16,8,8,128]{3,2,1,0:T(8,128)} custom-call(s32[5]{0:T(128)S(1)} %stack.23.place, f32[16,2,2,64,128]{4,3,2,1,0:T(8,128)S(1)} %all-to-all-done.arrived), custom_call_target="tpu_custom_call" | custom-call | flops 536870912 | bytes 2097152 | tf_op jit(solution)/shard_map/x_modes/pallas_call | solution.py:435
  47.6 10.8 %all-to-all-start.1 = ((f32[16,8,8,128]{3,2,1,0:T(8,128)}), f32[16,8,8,128]{3,2,1,0:T(8,128)}, u32[]{:S(2)}, u32[]{:S(2)}) async-start(f32[16,8,8,128]{3,2,1,0:T(8,128)} %x_modes.1), calls=%async_computation.1 | async-start | bytes 1048576 | tf_op jit(solution)/shard_map/all_to_all | solution.py:358
  58.3 1.1 x_side.1
  59.5 0.2 collective-permute-start.4
  59.7 0.0 copy-done.1
  59.7 0.0 copy-done.3
  59.7 0.0 copy-done.4
  59.7 0.0 copy-done.2
  59.7 1.3 %weight.1 = f32[128,2048]{1,0:T(8,128)S(1)} custom-call(bf16[64,2048]{1,0:T(8,128)(2,1)S(1)} %copy-done.3, s32[128,2048]{1,0:T(8,128)S(1)} %bitcast.14, s32[128,64]{1,0:T(8,128)S(1)} %bitcast.16, f32[128,2048]{1,0:T(8,128)S(1)} %bitcast.15), custom_call_target="tpu_custom_call" | custom-call | flops 134217728 | bytes 3145728 | tf_op jit(solution)/shard_map/weight/pallas_call | solution.py:405
  61.0 0.1 collective-permute-done.4.got
  61.1 0.8 pair.1
  61.9 0.0 copy-start.15
  61.9 13.8 %all-to-all-done.1.arrived = f32[16,8,8,128]{3,2,1,0:T(8,128)} async-done(((f32[16,8,8,128]{3,2,1,0:T(8,128)}), f32[16,8,8,128]{3,2,1,0:T(8,128)}, u32[]{:S(2)}, u32[]{:S(2)}) %all-to-all-start.1) | async-done | bytes 524320 | tf_op jit(solution)/shard_map/all_to_all | solution.py:358
  75.7 4.7 %modes.1 = (f32[2,128,128]{2,1,0:T(8,128)}, f32[16,8,8,128]{3,2,1,0:T(8,128)}) custom-call(s32[5]{0:T(128)S(1)} %stack.23.place, f32[128,2048]{1,0:T(8,128)S(1)} %weight.1, f32[16,8,8,128]{3,2,1,0:T(8,128)} %all-to-all-done.1.arrived), custom_call_target="tpu_custom_call" | custom-call | flops 1073741824 | bytes 3145728 | tf_op jit(solution)/shard_map/modes/pallas_call | solution.py:472
  80.5 3.5 %all-to-all-start.2 = ((f32[16,8,8,128]{3,2,1,0:T(8,128)}), f32[16,8,8,128]{3,2,1,0:T(8,128)S(1)}, u32[]{:S(2)}, u32[]{:S(2)}) async-start(f32[16,8,8,128]{3,2,1,0:T(8,128)} %get-tuple-element.57), calls=%async_computation.2 | async-start | bytes 1048576 | tf_op jit(solution)/shard_map/all_to_all | solution.py:358
  84.0 0.0 copy-done.18
  84.0 0.0 copy-start.10
  84.0 0.0 copy-start.9
  84.0 0.0 copy-start.8
  84.0 0.9 collective-permute-start.5
  84.9 0.0 copy-done.17
  84.9 2.1 %collective-permute-start.6 = (f32[2,8,8,128]{3,2,1,0:T(8,128)S(1)}, f32[2,8,8,128]{3,2,1,0:T(8,128)S(1)}, u32[]{:S(2)}, u32[]{:S(2)}) collective-permute-start(f32[2,8,8,128]{3,2,1,0:T(8,128)S(1)} %copy-done.17), channel_id=1, source_target_pairs={{0,4},{2,6},{4,32},{6,34},{32,36},{34,38},{36,0},{38,2},{1,5},{3,7... | collective-permute-start | bytes 196616 | tf_op jit(solution)/shard_map/ppermute | solution.py:468
  87.0 0.0 copy-done.16
  87.0 1.5 %collective-permute-start.7 = (f32[2,8,8,128]{3,2,1,0:T(8,128)S(1)}, f32[2,8,8,128]{3,2,1,0:T(8,128)S(1)}, u32[]{:S(2)}, u32[]{:S(2)}) collective-permute-start(f32[2,8,8,128]{3,2,1,0:T(8,128)S(1)} %copy-done.16), channel_id=1, source_target_pairs={{0,36},{2,38},{4,0},{6,2},{32,4},{34,6},{36,32},{38,34},{1,37},{3,... | collective-permute-start | bytes 196616 | tf_op jit(solution)/shard_map/ppermute | solution.py:468
  88.5 0.0 copy-done.15
  88.5 0.7 collective-permute-start.8
  89.1 10.1 %collective-permute-done.5.refs_1_ = f32[2,8,8,128]{3,2,1,0:T(8,128)S(1)} collective-permute-done((f32[2,8,8,128]{3,2,1,0:T(8,128)S(1)}, f32[2,8,8,128]{3,2,1,0:T(8,128)S(1)}, u32[]{:S(2)}, u32[]{:S(2)}) %collective-permute-start.5) | collective-permute-done | bytes 65568 | tf_op jit(solution)/shard_map/ppermute | solution.py:468
  99.2 3.2 %collective-permute-done.6.refs_2_ = f32[2,8,8,128]{3,2,1,0:T(8,128)S(1)} collective-permute-done((f32[2,8,8,128]{3,2,1,0:T(8,128)S(1)}, f32[2,8,8,128]{3,2,1,0:T(8,128)S(1)}, u32[]{:S(2)}, u32[]{:S(2)}) %collective-permute-start.6) | collective-permute-done | bytes 65568 | tf_op jit(solution)/shard_map/ppermute | solution.py:468
  102.4 0.0 collective-permute-done.7.refs_6_
  102.4 0.0 collective-permute-done.8.refs_7_
  102.4 0.0 all-to-all-done.2.arrived
  102.4 2.2 %x_cells.1 = f32[16,17,8,128]{3,2,1,0:T(8,128)} custom-call(s32[5]{0:T(128)S(1)} %stack.23.place, f32[16,8,8,128]{3,2,1,0:T(8,128)S(1)} %all-to-all-done.2.arrived, f32[8,128]{1,0:T(8,128)S(1)} %add.31.sums), custom_call_target="tpu_custom_call" | custom-call | flops 536870912 | bytes 2097152 | tf_op jit(solution)/shard_map/x_cells/pallas_call | solution.py:488
  104.7 0.0 copy-done.11
  104.7 3.7 %all-to-all-start.3 = ((f32[16,17,8,128]{3,2,1,0:T(8,128)}), f32[16,17,8,128]{3,2,1,0:T(8,128)S(1)}, u32[]{:S(2)}, u32[]{:S(2)}) async-start(f32[16,17,8,128]{3,2,1,0:T(8,128)} %x_cells.1), calls=%async_computation.3 | async-start | bytes 2228224 | tf_op jit(solution)/shard_map/all_to_all | solution.py:358
  108.4 0.0 copy-done.10
  108.4 0.0 copy-start
  108.4 3.6 %collective-permute-start.9 = (f32[2,8,8,128]{3,2,1,0:T(8,128)S(1)}, f32[2,8,8,128]{3,2,1,0:T(8,128)S(1)}, u32[]{:S(2)}, u32[]{:S(2)}) collective-permute-start(f32[2,8,8,128]{3,2,1,0:T(8,128)S(1)} %copy-done.10), channel_id=1, source_target_pairs={{0,6},{2,32},{4,34},{6,36},{32,38},{34,0},{36,2},{38,4},{1,7},{3,3... | collective-permute-start | bytes 196616 | tf_op jit(solution)/shard_map/ppermute | solution.py:468
  112.0 0.7 collective-permute-start.10
  112.7 3.5 %collective-permute-start.11 = (f32[2,8,8,128]{3,2,1,0:T(8,128)S(1)}, f32[2,8,8,128]{3,2,1,0:T(8,128)S(1)}, u32[]{:S(2)}, u32[]{:S(2)}) collective-permute-start(f32[2,8,8,128]{3,2,1,0:T(8,128)S(1)} %copy-done.8), channel_id=1, source_target_pairs={{0,34},{2,36},{4,38},{6,0},{32,2},{34,4},{36,6},{38,32},{1,35},{3,... | collective-permute-start | bytes 196616 | tf_op jit(solution)/shard_map/ppermute | solution.py:468
  116.2 0.2 collective-permute-done.9.refs_3_
  116.4 5.6 %collective-permute-done.10.refs_4_ = f32[2,8,8,128]{3,2,1,0:T(8,128)S(1)} collective-permute-done((f32[2,8,8,128]{3,2,1,0:T(8,128)S(1)}, f32[2,8,8,128]{3,2,1,0:T(8,128)S(1)}, u32[]{:S(2)}, u32[]{:S(2)}) %collective-permute-start.10) | collective-permute-done | bytes 65568 | tf_op jit(solution)/shard_map/ppermute | solution.py:468
  122.1 0.0 collective-permute-done.11.refs_5_
  122.1 0.6 copy-done.20
  122.7 0.0 copy-done.21
  122.7 4.1 %outer.1 = f32[128,2048]{1,0:T(8,128)} custom-call(s32[5]{0:T(128)} %copy-done.5, f32[2,8,8,128]{3,2,1,0:T(8,128)} %get-tuple-element.66.refs_0_, f32[2,8,8,128]{3,2,1,0:T(8,128)} %copy-done.11, f32[2,8,8,128]{3,2,1,0:T(8,128)} %copy-done.12, f32[2,8,8,128]{3,2,1,0:T(8,128)} %copy-done.19, f32[2,8,8,128]{3,2,1,0:T(8,128)} %copy-done.20, ...), custom_call_target="tpu_custom_call" | custom-call | flops 1073741824 | bytes 4194304 | tf_op jit(solution)/shard_map/outer/pallas_call | solution.py:500
  126.8 0.0 all-to-all-done.3.arrived.sums
  126.8 3.8 %end.1 = (f32[64,4,16,128]{3,2,1,0:T(8,128)}, f32[32,32]{1,0:T(8,128)}, f32[1,32]{1,0:T(1,128)}) custom-call(f32[16,17,8,128]{3,2,1,0:T(8,128)S(1)} %all-to-all-done.3.arrived.sums, f32[16,17,8,128]{3,2,1,0:T(8,128)S(1)} %all-to-all-done.3.arrived.sums, f32[64,4,16,128]{3,2,1,0:T(8,128)S(1)} %copy-done), custom_call_target="tpu_custom_call" | custom-call | flops 536870912 | bytes 5242880 | tf_op jit(solution)/shard_map/end/pallas_call | solution.py:509
  (29 shorter events, 0.1 us)
Async XLA Ops:
  7.5 7.7 %copy-start.6 = (f32[2,32,2,32]{3,2,1,0:T(2,128)S(1)}, f32[2,32,2,32]{3,2,1,0:T(2,128)}, u32[]{:S(2)}) copy-start(f32[2,32,2,32]{3,2,1,0:T(2,128)} %constant.40) | copy-start | bytes 49156
  7.5 7.7 %copy-start.7 = (f32[32,32]{1,0:T(8,128)S(1)}, f32[32,32]{1,0:T(8,128)}, u32[]{:S(2)}) copy-start(f32[32,32]{1,0:T(8,128)} %param.15) | copy-start | bytes 12292
  7.5 38.2 %all-to-all-start = ((f32[16,2,2,64,128]{4,3,2,1,0:T(8,128)}), f32[16,2,2,64,128]{4,3,2,1,0:T(8,128)S(1)}, u32[]{:S(2)}, u32[]{:S(2)}) async-start(f32[16,2,2,64,128]{4,3,2,1,0:T(8,128)} %front.1), calls=%async_computation | async-start | bytes 4194304 | tf_op jit(solution)/shard_map/all_to_all | solution.py:358
  23.2 2.0 %collective-permute-start = (f32[8,128]{1,0:T(8,128)}, f32[8,128]{1,0:T(8,128)S(1)}, u32[]{:S(2)}, u32[]{:S(2)}) collective-permute-start(f32[8,128]{1,0:T(8,128)} %get-tuple-element.42), channel_id=1, source_target_pairs={{0,1},{1,0},{2,3},{3,2},{4,5},{5,4},{6,7},{7,6},{8,9},{9,8},{10,11... | collective-permute-start | bytes 12296 | tf_op jit(solution)/shard_map/ppermute | solution.py:399
  25.9 2.9 %collective-permute-start.1 = (f32[8,128]{1,0:T(8,128)S(1)}, f32[8,128]{1,0:T(8,128)S(1)}, u32[]{:S(2)}, u32[]{:S(2)}) collective-permute-start(f32[8,128]{1,0:T(8,128)S(1)} %add.28), channel_id=1, source_target_pairs={{0,2},{2,0},{4,6},{6,4},{1,3},{3,1},{5,7},{7,5},{8,10},{10,8},{12,... | collective-permute-start | bytes 12296 | tf_op jit(solution)/shard_map/ppermute | solution.py:399
  28.8 4.2 %collective-permute-start.2 = (f32[8,128]{1,0:T(8,128)S(1)}, f32[8,128]{1,0:T(8,128)S(1)}, u32[]{:S(2)}, u32[]{:S(2)}) collective-permute-start(f32[8,128]{1,0:T(8,128)S(1)} %add.29), channel_id=1, source_target_pairs={{0,4},{2,6},{4,0},{6,2},{1,5},{3,7},{5,1},{7,3},{8,12},{10,14},{12... | collective-permute-start | bytes 12296 | tf_op jit(solution)/shard_map/ppermute | solution.py:399
  33.0 7.2 %collective-permute-start.3 = (f32[8,128]{1,0:T(8,128)S(1)}, f32[8,128]{1,0:T(8,128)S(1)}, u32[]{:S(2)}, u32[]{:S(2)}) collective-permute-start(f32[8,128]{1,0:T(8,128)S(1)} %add.30), channel_id=1, source_target_pairs={{0,32},{32,0},{1,33},{33,1},{2,34},{34,2},{3,35},{35,3},{4,36},{36... | collective-permute-start | bytes 12296 | tf_op jit(solution)/shard_map/ppermute | solution.py:399
  39.3 63.1 %copy-start.5 = (s32[5]{0:T(128)}, s32[5]{0:T(128)S(1)}, u32[]{:S(2)}) copy-start(s32[5]{0:T(128)S(1)} %stack.23.place) | copy-start | bytes 64
  47.6 12.1 %copy-start.1 = (s32[1,4,32,2048]{3,2,1,0:T(8,128)S(1)}, s32[1,4,32,2048]{3,2,1,0:T(8,128)}, u32[]{:S(2)}) copy-start(s32[1,4,32,2048]{3,2,1,0:T(8,128)} %param.12) | copy-start | bytes 3145732
  47.6 12.1 %copy-start.3 = (bf16[64,2048]{1,0:T(8,128)(2,1)S(1)}, bf16[64,2048]{1,0:T(8,128)(2,1)}, u32[]{:S(2)}) copy-start(bf16[64,2048]{1,0:T(8,128)(2,1)} %constant.33.clone.spread) | copy-start | bytes 786436
  47.6 12.1 %copy-start.4 = (s32[1,4,32,64]{3,2,1,0:T(8,128)S(1)}, s32[1,4,32,64]{3,2,1,0:T(8,128)}, u32[]{:S(2)}) copy-start(s32[1,4,32,64]{3,2,1,0:T(8,128)} %param.13) | copy-start | bytes 98308
  47.6 28.2 %all-to-all-start.1 = ((f32[16,8,8,128]{3,2,1,0:T(8,128)}), f32[16,8,8,128]{3,2,1,0:T(8,128)}, u32[]{:S(2)}, u32[]{:S(2)}) async-start(f32[16,8,8,128]{3,2,1,0:T(8,128)} %x_modes.1), calls=%async_computation.1 | async-start | bytes 1048576 | tf_op jit(solution)/shard_map/all_to_all | solution.py:358
  58.3 1.4 %copy-start.2 = (f32[1,4,32,2048]{3,2,1,0:T(8,128)S(1)}, f32[1,4,32,2048]{3,2,1,0:T(8,128)}, u32[]{:S(2)}) copy-start(f32[1,4,32,2048]{3,2,1,0:T(8,128)} %param.14) | copy-start | bytes 3145732
  59.5 1.6 %collective-permute-start.4 = (f32[8,8,8,128]{3,2,1,0:T(8,128)S(1)}, f32[8,8,8,128]{3,2,1,0:T(8,128)S(1)}, u32[]{:S(2)}, u32[]{:S(2)}) collective-permute-start(f32[8,8,8,128]{3,2,1,0:T(8,128)S(1)} %get-tuple-element.47), channel_id=1, source_target_pairs={{0,1},{1,0},{2,3},{3,2},{4,5},{5,4},{6,7},{7,6},{8,9},{9,8},{10,11... | collective-permute-start | bytes 786440 | tf_op jit(solution)/shard_map/ppermute | solution.py:454
  61.9 22.1 %copy-start.18 = (f32[2,8,8,128]{3,2,1,0:T(8,128)S(1)}, f32[2,8,8,128]{3,2,1,0:T(8,128)}, u32[]{:S(2)}) copy-start(f32[2,8,8,128]{3,2,1,0:T(8,128)} %get-tuple-element.59) | copy-start | bytes 196612
  61.9 23.0 %copy-start.17 = (f32[2,8,8,128]{3,2,1,0:T(8,128)S(1)}, f32[2,8,8,128]{3,2,1,0:T(8,128)}, u32[]{:S(2)}) copy-start(f32[2,8,8,128]{3,2,1,0:T(8,128)} %get-tuple-element.60) | copy-start | bytes 196612
  61.9 25.1 %copy-start.16 = (f32[2,8,8,128]{3,2,1,0:T(8,128)S(1)}, f32[2,8,8,128]{3,2,1,0:T(8,128)}, u32[]{:S(2)}) copy-start(f32[2,8,8,128]{3,2,1,0:T(8,128)} %get-tuple-element.61) | copy-start | bytes 196612
  61.9 26.6 %copy-start.15 = (f32[2,8,8,128]{3,2,1,0:T(8,128)S(1)}, f32[2,8,8,128]{3,2,1,0:T(8,128)}, u32[]{:S(2)}) copy-start(f32[2,8,8,128]{3,2,1,0:T(8,128)} %get-tuple-element.62) | copy-start | bytes 196612
  80.5 21.9 %all-to-all-start.2 = ((f32[16,8,8,128]{3,2,1,0:T(8,128)}), f32[16,8,8,128]{3,2,1,0:T(8,128)S(1)}, u32[]{:S(2)}, u32[]{:S(2)}) async-start(f32[16,8,8,128]{3,2,1,0:T(8,128)} %get-tuple-element.57), calls=%async_computation.2 | async-start | bytes 1048576 | tf_op jit(solution)/shard_map/all_to_all | solution.py:358
  84.0 24.4 %copy-start.10 = (f32[2,8,8,128]{3,2,1,0:T(8,128)S(1)}, f32[2,8,8,128]{3,2,1,0:T(8,128)}, u32[]{:S(2)}) copy-start(f32[2,8,8,128]{3,2,1,0:T(8,128)} %get-tuple-element.72) | copy-start | bytes 196612
  84.0 28.0 %copy-start.9 = (f32[2,8,8,128]{3,2,1,0:T(8,128)S(1)}, f32[2,8,8,128]{3,2,1,0:T(8,128)}, u32[]{:S(2)}) copy-start(f32[2,8,8,128]{3,2,1,0:T(8,128)} %get-tuple-element.73) | copy-start | bytes 196612
  84.0 28.7 %copy-start.8 = (f32[2,8,8,128]{3,2,1,0:T(8,128)S(1)}, f32[2,8,8,128]{3,2,1,0:T(8,128)}, u32[]{:S(2)}) copy-start(f32[2,8,8,128]{3,2,1,0:T(8,128)} %get-tuple-element.74) | copy-start | bytes 196612
  84.0 15.2 %collective-permute-start.5 = (f32[2,8,8,128]{3,2,1,0:T(8,128)S(1)}, f32[2,8,8,128]{3,2,1,0:T(8,128)S(1)}, u32[]{:S(2)}, u32[]{:S(2)}) collective-permute-start(f32[2,8,8,128]{3,2,1,0:T(8,128)S(1)} %copy-done.18), channel_id=1, source_target_pairs={{0,2},{2,4},{4,6},{6,32},{32,34},{34,36},{36,38},{38,0},{1,3},{3,5... | collective-permute-start | bytes 196616 | tf_op jit(solution)/shard_map/ppermute | solution.py:468
  84.9 17.5 %collective-permute-start.6 = (f32[2,8,8,128]{3,2,1,0:T(8,128)S(1)}, f32[2,8,8,128]{3,2,1,0:T(8,128)S(1)}, u32[]{:S(2)}, u32[]{:S(2)}) collective-permute-start(f32[2,8,8,128]{3,2,1,0:T(8,128)S(1)} %copy-done.17), channel_id=1, source_target_pairs={{0,4},{2,6},{4,32},{6,34},{32,36},{34,38},{36,0},{38,2},{1,5},{3,7... | collective-permute-start | bytes 196616 | tf_op jit(solution)/shard_map/ppermute | solution.py:468
  87.0 15.4 %collective-permute-start.7 = (f32[2,8,8,128]{3,2,1,0:T(8,128)S(1)}, f32[2,8,8,128]{3,2,1,0:T(8,128)S(1)}, u32[]{:S(2)}, u32[]{:S(2)}) collective-permute-start(f32[2,8,8,128]{3,2,1,0:T(8,128)S(1)} %copy-done.16), channel_id=1, source_target_pairs={{0,36},{2,38},{4,0},{6,2},{32,4},{34,6},{36,32},{38,34},{1,37},{3,... | collective-permute-start | bytes 196616 | tf_op jit(solution)/shard_map/ppermute | solution.py:468
  88.5 13.9 %collective-permute-start.8 = (f32[2,8,8,128]{3,2,1,0:T(8,128)S(1)}, f32[2,8,8,128]{3,2,1,0:T(8,128)S(1)}, u32[]{:S(2)}, u32[]{:S(2)}) collective-permute-start(f32[2,8,8,128]{3,2,1,0:T(8,128)S(1)} %copy-done.15), channel_id=1, source_target_pairs={{0,38},{2,0},{4,2},{6,4},{32,6},{34,32},{36,34},{38,36},{1,39},{3,... | collective-permute-start | bytes 196616 | tf_op jit(solution)/shard_map/ppermute | solution.py:468
  99.2 5.4 %copy-start.11 = (f32[2,8,8,128]{3,2,1,0:T(8,128)}, f32[2,8,8,128]{3,2,1,0:T(8,128)S(1)}, u32[]{:S(2)}) copy-start(f32[2,8,8,128]{3,2,1,0:T(8,128)S(1)} %collective-permute-done.5.refs_1_) | copy-start | bytes 196612
  102.4 2.3 %copy-start.12 = (f32[2,8,8,128]{3,2,1,0:T(8,128)}, f32[2,8,8,128]{3,2,1,0:T(8,128)S(1)}, u32[]{:S(2)}) copy-start(f32[2,8,8,128]{3,2,1,0:T(8,128)S(1)} %collective-permute-done.6.refs_2_) | copy-start | bytes 196612
  102.4 2.3 %copy-start.13 = (f32[2,8,8,128]{3,2,1,0:T(8,128)}, f32[2,8,8,128]{3,2,1,0:T(8,128)S(1)}, u32[]{:S(2)}) copy-start(f32[2,8,8,128]{3,2,1,0:T(8,128)S(1)} %collective-permute-done.7.refs_6_) | copy-start | bytes 196612
  102.4 2.3 %copy-start.14 = (f32[2,8,8,128]{3,2,1,0:T(8,128)}, f32[2,8,8,128]{3,2,1,0:T(8,128)S(1)}, u32[]{:S(2)}) copy-start(f32[2,8,8,128]{3,2,1,0:T(8,128)S(1)} %collective-permute-done.8.refs_7_) | copy-start | bytes 196612
  104.7 22.1 %all-to-all-start.3 = ((f32[16,17,8,128]{3,2,1,0:T(8,128)}), f32[16,17,8,128]{3,2,1,0:T(8,128)S(1)}, u32[]{:S(2)}, u32[]{:S(2)}) async-start(f32[16,17,8,128]{3,2,1,0:T(8,128)} %x_cells.1), calls=%async_computation.3 | async-start | bytes 2228224 | tf_op jit(solution)/shard_map/all_to_all | solution.py:358
  108.4 18.4 %copy-start = (f32[64,4,16,128]{3,2,1,0:T(8,128)S(1)}, f32[64,4,16,128]{3,2,1,0:T(8,128)}, u32[]{:S(2)}) copy-start(f32[64,4,16,128]{3,2,1,0:T(8,128)} %get-tuple-element.64.base) | copy-start | bytes 6291460
  108.4 8.0 %collective-permute-start.9 = (f32[2,8,8,128]{3,2,1,0:T(8,128)S(1)}, f32[2,8,8,128]{3,2,1,0:T(8,128)S(1)}, u32[]{:S(2)}, u32[]{:S(2)}) collective-permute-start(f32[2,8,8,128]{3,2,1,0:T(8,128)S(1)} %copy-done.10), channel_id=1, source_target_pairs={{0,6},{2,32},{4,34},{6,36},{32,38},{34,0},{36,2},{38,4},{1,7},{3,3... | collective-permute-start | bytes 196616 | tf_op jit(solution)/shard_map/ppermute | solution.py:468
  112.0 10.0 %collective-permute-start.10 = (f32[2,8,8,128]{3,2,1,0:T(8,128)S(1)}, f32[2,8,8,128]{3,2,1,0:T(8,128)S(1)}, u32[]{:S(2)}, u32[]{:S(2)}) collective-permute-start(f32[2,8,8,128]{3,2,1,0:T(8,128)S(1)} %copy-done.9), channel_id=1, source_target_pairs={{0,32},{2,34},{4,36},{6,38},{32,0},{34,2},{36,4},{38,6},{1,33},{3,... | collective-permute-start | bytes 196616 | tf_op jit(solution)/shard_map/ppermute | solution.py:468
  112.7 9.3 %collective-permute-start.11 = (f32[2,8,8,128]{3,2,1,0:T(8,128)S(1)}, f32[2,8,8,128]{3,2,1,0:T(8,128)S(1)}, u32[]{:S(2)}, u32[]{:S(2)}) collective-permute-start(f32[2,8,8,128]{3,2,1,0:T(8,128)S(1)} %copy-done.8), channel_id=1, source_target_pairs={{0,34},{2,36},{4,38},{6,0},{32,2},{34,4},{36,6},{38,32},{1,35},{3,... | collective-permute-start | bytes 196616 | tf_op jit(solution)/shard_map/ppermute | solution.py:468
  116.4 5.6 %copy-start.19 = (f32[2,8,8,128]{3,2,1,0:T(8,128)}, f32[2,8,8,128]{3,2,1,0:T(8,128)S(1)}, u32[]{:S(2)}) copy-start(f32[2,8,8,128]{3,2,1,0:T(8,128)S(1)} %collective-permute-done.9.refs_3_) | copy-start | bytes 196612
  122.1 0.6 copy-start.20
  122.1 0.6 copy-start.21
